TPU v7x, 32 devices: a whole 2x2x4 slice. The times are simulated.
32 devices in a mesh: dp: 4 (over x, core), seq: 2 (over y), tensor: 4 (over z).
Axes of the slice: x: 2, y: 2, z: 4, core: 2. Of those that a mesh axis runs over, the one named last changes fastest.
Arguments:
- tokens: bfloat16 [8, 2, 544, 2304], P('dp', 'seq'), may hold values from -6 to 6
- cotangent: bfloat16 [8, 2, 544, 2304], P('dp', 'seq'), may hold values from -6 to 6
- prompt_of: int32 [8, 2], P('dp', 'seq'), may hold values from 0 to 1
- query_weight: bfloat16 [2304, 2048], P(('dp', 'seq'), 'tensor'), may hold values from -0.125 to 0.125
- key_weight: bfloat16 [2304, 1024], P(('dp', 'seq'), 'tensor'), may hold values from -0.125 to 0.125
- value_weight: bfloat16 [2304, 1024], P(('dp', 'seq'), 'tensor'), may hold values from -0.125 to 0.125
- out_weight: bfloat16 [2048, 2304], P('tensor', ('dp', 'seq')), may hold values from -0.125 to 0.125
- gate_weight: bfloat16 [2304, 9216], P(('dp', 'seq'), 'tensor'), may hold values from -0.125 to 0.125
- up_weight: bfloat16 [2304, 9216], P(('dp', 'seq'), 'tensor'), may hold values from -0.125 to 0.125
- down_weight: bfloat16 [9216, 2304], P('tensor', ('dp', 'seq')), may hold values from -0.0625 to 0.0625
- norm_gains: bfloat16 [4, 2304], P(None, ('dp', 'seq')), may hold values from 0.099609375 to 1.8984375
Outputs:
- output: bfloat16 [8, 2, 544, 2304], P('dp', 'seq')
- input_grad: float32 [8, 2, 544, 2304], P('dp', 'seq')
- grad_query: float32 [2304, 2048], P(('dp', 'seq'), 'tensor')
- grad_key: float32 [2304, 1024], P(('dp', 'seq'), 'tensor')
- grad_value: float32 [2304, 1024], P(('dp', 'seq'), 'tensor')
- grad_out: float32 [2048, 2304], P('tensor', ('dp', 'seq'))
- grad_gate: float32 [2304, 9216], P(('dp', 'seq'), 'tensor')
- grad_up: float32 [2304, 9216], P(('dp', 'seq'), 'tensor')
- grad_down: float32 [9216, 2304], P('tensor', ('dp', 'seq'))
- grad_gains: float32 [4, 2304], P(None, ('dp', 'seq'))
Inputs may be any that keep to these rules, and one draw needn't show every extreme that they name: prompt_of[g, s] names one of the 2 groups held by the same index of dp.
All inputs are finite; a program needn't handle non-finite values.
Results may differ from a plain program's by a relative error of at most 0.025.
Values may be sent and summed in bfloat16 or wider, within the bound.
A program may use at most 320 MiB of HBM per device.

v0:
```python
import jax
import jax.numpy as jnp
from jax import lax
from jax.sharding import PartitionSpec as P

HEAD = 256
CONT = 32


EPS = 1e-06
SOFTCAP = 50.0
THETA = 10000.0


def normalize(values):
    return values * lax.rsqrt(jnp.mean(values * values, axis=-1, keepdims=True) + EPS)


def norm_back(values, gain, upstream):
    inverse = lax.rsqrt(jnp.mean(values * values, axis=-1, keepdims=True) + EPS)
    normed = values * inverse
    scaled = upstream * gain
    backed = inverse * (scaled - normed * jnp.mean(scaled * normed, axis=-1, keepdims=True))
    return (backed, jnp.sum(upstream * normed, axis=0))


def rotate(values, places):
    half_width = values.shape[-1] // 2
    spectrum = THETA ** (-2.0 * jnp.arange(half_width, dtype=jnp.float32) / values.shape[-1])
    angles = places.astype(jnp.float32)[..., None] * spectrum
    angles = jnp.concatenate([angles, angles], axis=-1)[..., None, :]
    turned = jnp.concatenate([-values[..., half_width:], values[..., :half_width]], axis=-1)
    return values * jnp.cos(angles) + turned * jnp.sin(angles)


def visibility(micro_count, row_count, prompt_dev, prompt_all, cont_rows, seq_pos, owners):
    local_rows = jnp.arange(row_count)
    prompt_rows = local_rows < prompt_dev
    places_local = jnp.where(
        prompt_rows, seq_pos * prompt_dev + local_rows, prompt_all + local_rows - prompt_dev
    )
    micro_ids = jnp.arange(micro_count)
    row_micro = jnp.repeat(micro_ids, row_count)
    row_prompt = jnp.tile(prompt_rows, micro_count)
    row_place = jnp.tile(places_local, micro_count)
    first_slot = jnp.where(row_prompt, row_micro, jnp.repeat(owners, row_count))
    second_slot = jnp.where(row_prompt, -1, micro_count + row_micro)
    key_slot = jnp.concatenate(
        [jnp.repeat(micro_ids, prompt_all), micro_count + jnp.repeat(micro_ids, cont_rows)]
    )
    key_place = jnp.concatenate(
        [
            jnp.tile(jnp.arange(prompt_all), micro_count),
            prompt_all + jnp.tile(jnp.arange(cont_rows), micro_count),
        ]
    )
    matched = (key_slot[None, :] == first_slot[:, None]) | (
        key_slot[None, :] == second_slot[:, None]
    )
    return (matched & (key_place[None, :] <= row_place[:, None]), row_place)


def scores_for(query, key_rows, visible, score_scale):
    raw_scores = jnp.einsum("rd,kd->rk", query, key_rows, preferred_element_type=jnp.float32)
    curved = jnp.tanh(raw_scores * score_scale / SOFTCAP)
    return (curved, jnp.where(visible, SOFTCAP * curved, -1e30))


def per_device(
    tokens,
    cotangent,
    prompt_of,
    query_weight,
    key_weight,
    value_weight,
    out_weight,
    gate_weight,
    up_weight,
    down_weight,
    norm_gains,
):
    micro_count = tokens.shape[0]
    row_count = tokens.shape[2]
    model_width = tokens.shape[3]
    seq_count = lax.axis_size("seq")
    seq_pos = lax.axis_index("seq")
    prompt_dev = row_count - CONT
    prompt_all = prompt_dev * seq_count
    total_rows = micro_count * row_count
    score_scale = HEAD ** (-0.5)
    visible, places = visibility(
        micro_count, row_count, prompt_dev, prompt_all, CONT, seq_pos, prompt_of[:, 0]
    )
    full_query, full_key, full_value, full_out, full_gate, full_up, full_down, gain_rows = (
        lax.all_gather(query_weight, ("dp", "seq"), axis=0, tiled=True),
        lax.all_gather(key_weight, ("dp", "seq"), axis=0, tiled=True),
        lax.all_gather(value_weight, ("dp", "seq"), axis=0, tiled=True),
        lax.all_gather(out_weight, ("dp", "seq"), axis=1, tiled=True),
        lax.all_gather(gate_weight, ("dp", "seq"), axis=0, tiled=True),
        lax.all_gather(up_weight, ("dp", "seq"), axis=0, tiled=True),
        lax.all_gather(down_weight, ("dp", "seq"), axis=1, tiled=True),
        lax.all_gather(norm_gains, ("dp", "seq"), axis=1, tiled=True),
    )
    gain_float = gain_rows.astype(jnp.float32)
    inputs = tokens.reshape(total_rows, model_width).astype(jnp.float32)
    normed_in = (normalize(inputs) * gain_float[0]).astype(jnp.bfloat16)
    query_heads = jnp.dot(normed_in, full_query, preferred_element_type=jnp.float32).reshape(
        total_rows, -1, HEAD
    )
    key_heads = jnp.dot(normed_in, full_key, preferred_element_type=jnp.float32).reshape(
        total_rows, 1, HEAD
    )
    value_raw = jnp.dot(normed_in, full_value, preferred_element_type=jnp.float32)
    query_rows = rotate(query_heads, places).astype(jnp.bfloat16)
    key_local = rotate(key_heads, places)[:, 0].astype(jnp.bfloat16)
    value_local = value_raw.astype(jnp.bfloat16)
    key_grid = key_local.reshape(micro_count, row_count, HEAD)
    value_grid = value_local.reshape(micro_count, row_count, HEAD)
    prompt_keys, prompt_values = (
        lax.all_gather(key_grid[:, :prompt_dev], "seq", axis=1, tiled=True),
        lax.all_gather(value_grid[:, :prompt_dev], "seq", axis=1, tiled=True),
    )
    key_rows = jnp.concatenate(
        [
            prompt_keys.reshape(micro_count * prompt_all, HEAD),
            key_grid[:, prompt_dev:].reshape(micro_count * CONT, HEAD),
        ],
        axis=0,
    )
    value_rows = jnp.concatenate(
        [
            prompt_values.reshape(micro_count * prompt_all, HEAD),
            value_grid[:, prompt_dev:].reshape(micro_count * CONT, HEAD),
        ],
        axis=0,
    )
    head_count = query_rows.shape[1]
    contexts = []
    log_sums = []
    for head_pos in range(head_count):
        curved, masked = scores_for(query_rows[:, head_pos], key_rows, visible, score_scale)
        row_peak = jnp.max(masked, axis=-1, keepdims=True)
        weights = jnp.exp(masked - row_peak)
        summed = jnp.sum(weights, axis=-1, keepdims=True)
        probs = (weights / summed).astype(jnp.bfloat16)
        contexts.append(jnp.dot(probs, value_rows, preferred_element_type=jnp.float32))
        log_sums.append(row_peak + jnp.log(summed))
    context = jnp.stack(contexts, axis=1).reshape(total_rows, -1).astype(jnp.bfloat16)
    attn = lax.psum(
        jnp.dot(context, full_out, preferred_element_type=jnp.float32).astype(jnp.bfloat16),
        "tensor",
    ).astype(jnp.float32)
    middle = inputs + normalize(attn) * gain_float[1]
    ffn_in = (normalize(middle) * gain_float[2]).astype(jnp.bfloat16)
    gate = jnp.dot(ffn_in, full_gate, preferred_element_type=jnp.float32)
    up_val = jnp.dot(ffn_in, full_up, preferred_element_type=jnp.float32)
    hidden_act, glu_pull = jax.vjp(
        lambda gate_in, up_in: jax.nn.gelu(gate_in, approximate=True) * up_in, gate, up_val
    )
    hidden = hidden_act.astype(jnp.bfloat16)
    ffn = lax.psum(
        jnp.dot(hidden, full_down, preferred_element_type=jnp.float32).astype(jnp.bfloat16),
        "tensor",
    ).astype(jnp.float32)
    result = middle + normalize(ffn) * gain_float[3]
    full_query, full_key, full_value, full_out, full_gate, full_up, full_down, gain_rows = (
        lax.all_gather(query_weight, ("dp", "seq"), axis=0, tiled=True),
        lax.all_gather(key_weight, ("dp", "seq"), axis=0, tiled=True),
        lax.all_gather(value_weight, ("dp", "seq"), axis=0, tiled=True),
        lax.all_gather(out_weight, ("dp", "seq"), axis=1, tiled=True),
        lax.all_gather(gate_weight, ("dp", "seq"), axis=0, tiled=True),
        lax.all_gather(up_weight, ("dp", "seq"), axis=0, tiled=True),
        lax.all_gather(down_weight, ("dp", "seq"), axis=1, tiled=True),
        lax.all_gather(norm_gains, ("dp", "seq"), axis=1, tiled=True),
    )
    gain_float = gain_rows.astype(jnp.float32)
    upstream = cotangent.reshape(total_rows, model_width).astype(jnp.float32)
    d_ffn, gain_fourth = norm_back(ffn, gain_float[3], upstream)
    d_ffn = d_ffn.astype(jnp.bfloat16)
    grad_down = jnp.einsum("rf,rd->fd", hidden, d_ffn, preferred_element_type=jnp.float32)
    d_hidden = jnp.einsum("rd,fd->rf", d_ffn, full_down, preferred_element_type=jnp.float32)
    d_gate, d_up = glu_pull(d_hidden)
    d_gate = d_gate.astype(jnp.bfloat16)
    d_up = d_up.astype(jnp.bfloat16)
    grad_gate = jnp.einsum("rd,rf->df", ffn_in, d_gate, preferred_element_type=jnp.float32)
    grad_up = jnp.einsum("rd,rf->df", ffn_in, d_up, preferred_element_type=jnp.float32)
    ffn_part = jnp.einsum(
        "rf,df->rd", d_gate, full_gate, preferred_element_type=jnp.float32
    ) + jnp.einsum("rf,df->rd", d_up, full_up, preferred_element_type=jnp.float32)
    d_ffn_in = lax.psum(ffn_part.astype(jnp.bfloat16), "tensor").astype(jnp.float32)
    d_mid_norm, gain_third = norm_back(middle, gain_float[2], d_ffn_in)
    d_middle = upstream + d_mid_norm
    d_attn, gain_second = norm_back(attn, gain_float[1], d_middle)
    d_attn = d_attn.astype(jnp.bfloat16)
    grad_out = jnp.einsum("rc,rd->cd", context, d_attn, preferred_element_type=jnp.float32)
    d_context = (
        jnp.einsum("rd,cd->rc", d_attn, full_out, preferred_element_type=jnp.float32)
        .astype(jnp.bfloat16)
        .reshape(total_rows, head_count, HEAD)
    )
    key_grad = jnp.zeros((key_rows.shape[0], HEAD), jnp.float32)
    value_grad = jnp.zeros((key_rows.shape[0], HEAD), jnp.float32)
    query_grads = []
    for head_pos in range(head_count):
        curved, masked = scores_for(query_rows[:, head_pos], key_rows, visible, score_scale)
        probs = jnp.where(visible, jnp.exp(masked - log_sums[head_pos]), 0.0)
        probs_low = probs.astype(jnp.bfloat16)
        d_probs = jnp.einsum(
            "rd,kd->rk", d_context[:, head_pos], value_rows, preferred_element_type=jnp.float32
        )
        inner_sum = jnp.sum(probs * d_probs, axis=-1, keepdims=True)
        d_scores = (probs * (d_probs - inner_sum) * score_scale * (1.0 - curved * curved)).astype(
            jnp.bfloat16
        )
        query_grads.append(jnp.dot(d_scores, key_rows, preferred_element_type=jnp.float32))
        key_grad = key_grad + jnp.einsum(
            "rk,rd->kd", d_scores, query_rows[:, head_pos], preferred_element_type=jnp.float32
        )
        value_grad = value_grad + jnp.einsum(
            "rk,rd->kd", probs_low, d_context[:, head_pos], preferred_element_type=jnp.float32
        )
    split_at = micro_count * prompt_all
    prompt_key_grad, prompt_value_grad = (
        lax.psum_scatter(
            key_grad[:split_at].reshape(micro_count, prompt_all, HEAD).astype(jnp.bfloat16),
            "seq",
            scatter_dimension=1,
            tiled=True,
        ).astype(jnp.float32),
        lax.psum_scatter(
            value_grad[:split_at].reshape(micro_count, prompt_all, HEAD).astype(jnp.bfloat16),
            "seq",
            scatter_dimension=1,
            tiled=True,
        ).astype(jnp.float32),
    )
    own_keys = jnp.concatenate(
        [prompt_key_grad, key_grad[split_at:].reshape(micro_count, CONT, HEAD)], axis=1
    ).reshape(total_rows, HEAD)
    own_values = jnp.concatenate(
        [prompt_value_grad, value_grad[split_at:].reshape(micro_count, CONT, HEAD)], axis=1
    ).reshape(total_rows, HEAD)
    unused_query, unturn_query = jax.vjp(lambda turned_in: rotate(turned_in, places), query_heads)
    d_query = (
        unturn_query(jnp.stack(query_grads, axis=1))[0].reshape(total_rows, -1).astype(jnp.bfloat16)
    )
    unused_key, unturn_key = jax.vjp(lambda turned_in: rotate(turned_in, places), key_heads)
    d_key = unturn_key(own_keys[:, None, :])[0].reshape(total_rows, HEAD).astype(jnp.bfloat16)
    d_value = own_values.astype(jnp.bfloat16)
    grad_query = jnp.einsum("rd,rc->dc", normed_in, d_query, preferred_element_type=jnp.float32)
    grad_key = jnp.einsum("rd,rc->dc", normed_in, d_key, preferred_element_type=jnp.float32)
    grad_value = jnp.einsum("rd,rc->dc", normed_in, d_value, preferred_element_type=jnp.float32)
    attn_part = jnp.einsum("rc,dc->rd", d_query, full_query, preferred_element_type=jnp.float32)
    attn_part = attn_part + jnp.einsum(
        "rc,dc->rd", d_key, full_key, preferred_element_type=jnp.float32
    )
    attn_part = attn_part + jnp.einsum(
        "rc,dc->rd", d_value, full_value, preferred_element_type=jnp.float32
    )
    d_normed = lax.psum(attn_part.astype(jnp.bfloat16), "tensor").astype(jnp.float32)
    d_in_norm, gain_first = norm_back(inputs, gain_float[0], d_normed)
    input_grad = d_middle + d_in_norm
    grad_gains = jnp.stack([gain_first, gain_second, gain_third, gain_fourth], axis=0)
    shares = (
        lax.psum_scatter(
            grad_query.astype(jnp.bfloat16), ("dp", "seq"), scatter_dimension=0, tiled=True
        ).astype(jnp.float32),
        lax.psum_scatter(
            grad_key.astype(jnp.bfloat16), ("dp", "seq"), scatter_dimension=0, tiled=True
        ).astype(jnp.float32),
        lax.psum_scatter(
            grad_value.astype(jnp.bfloat16), ("dp", "seq"), scatter_dimension=0, tiled=True
        ).astype(jnp.float32),
        lax.psum_scatter(
            grad_out.astype(jnp.bfloat16), ("dp", "seq"), scatter_dimension=1, tiled=True
        ).astype(jnp.float32),
        lax.psum_scatter(
            grad_gate.astype(jnp.bfloat16), ("dp", "seq"), scatter_dimension=0, tiled=True
        ).astype(jnp.float32),
        lax.psum_scatter(
            grad_up.astype(jnp.bfloat16), ("dp", "seq"), scatter_dimension=0, tiled=True
        ).astype(jnp.float32),
        lax.psum_scatter(
            grad_down.astype(jnp.bfloat16), ("dp", "seq"), scatter_dimension=1, tiled=True
        ).astype(jnp.float32),
        lax.psum_scatter(
            grad_gains.astype(jnp.bfloat16), ("dp", "seq"), scatter_dimension=1, tiled=True
        ).astype(jnp.float32),
    )
    return (
        result.reshape(tokens.shape).astype(jnp.bfloat16),
        input_grad.reshape(tokens.shape),
        shares[0],
        shares[1],
        shares[2],
        shares[3],
        shares[4],
        shares[5],
        shares[6],
        shares[7],
    )


def solution(mesh):
    placed = (
        P("dp", "seq", None, None),
        P("dp", "seq", None, None),
        P("dp", "seq"),
        P(("dp", "seq"), "tensor"),
        P(("dp", "seq"), "tensor"),
        P(("dp", "seq"), "tensor"),
        P("tensor", ("dp", "seq")),
        P(("dp", "seq"), "tensor"),
        P(("dp", "seq"), "tensor"),
        P("tensor", ("dp", "seq")),
        P(None, ("dp", "seq")),
    )
    return jax.shard_map(
        per_device,
        mesh=mesh,
        in_specs=placed,
        out_specs=(
            P("dp", "seq", None, None),
            P("dp", "seq", None, None),
            P(("dp", "seq"), "tensor"),
            P(("dp", "seq"), "tensor"),
            P(("dp", "seq"), "tensor"),
            P("tensor", ("dp", "seq")),
            P(("dp", "seq"), "tensor"),
            P(("dp", "seq"), "tensor"),
            P("tensor", ("dp", "seq")),
            P(None, ("dp", "seq")),
        ),
        check_vma=False,
    )
```

profile of v0, /device:TPU:0, one launch (start us, length us, event | category | flops | bytes accessed | tf_op | source)
XLA Modules:
  0.0 1822.1 jit_solution(5972916923408912814)
XLA Ops:
  13.0 14.7 all-gather
  29.6 5.9 multiply_convert_fusion.3
  36.7 4.2 fusion.97
  41.1 4.1 fusion.67
  46.2 16.4 all-gather.17.cloned.1.call-done
  62.7 4.2 convolution_convert_fusion.10
  68.5 5.9 multiply_convert_fusion.4
  75.0 18.6 %all-gather.11.cloned.1.call-done = bf16[2304,512]{1,0:T(8,128)(2,1)} async-done(((bf16[288,512]{1,0:T(8,128)(2,1)}), bf16[2304,512]{1,0:T(8,128)(2,1)}) %all-gather.11.cloned.1.call-update) | async-done | bytes 2359312 | tf_op jit(solution)/shard_map/all_gather | solution.py:95
  93.6 4.5 copy.41
  98.1 5.4 fusion.96
  104.2 12.7 all-gather.15.cloned.1.call-done
  116.9 5.0 fusion.55
  122.0 5.6 fusion.44
  131.1 4.8 fusion.45
  135.9 4.3 all-gather.19.cloned.1.call-done
  140.2 6.6 fusion.60
  151.3 19.7 %all-gather.21.cloned.1.call-done = bf16[512,2304]{0,1:T(8,128)(2,1)} async-done(((bf16[512,288]{0,1:T(8,128)(2,1)}), bf16[512,2304]{0,1:T(8,128)(2,1)}) %all-gather.21.cloned.1.call-update) | async-done | bytes 2359312 | tf_op jit(solution)/shard_map/all_gather | solution.py:98
  171.0 7.0 convolution_convert_fusion.4
  180.4 179.4 %all-reduce.9.cloned.1.call-done = bf16[1088,2304]{1,0:T(8,128)(2,1)} async-done(((bf16[1088,2304]{1,0:T(8,128)(2,1)}), bf16[1088,2304]{1,0:T(8,128)(2,1)}) %all-reduce.9.cloned.1.call-update) | async-done | bytes 5013520 | tf_op jit(solution)/shard_map/psum | solution.py:149
  363.7 4.6 fusion.23
  375.5 48.9 %all-gather.23.cloned.1.call-done = bf16[2304,2304]{1,0:T(8,128)(2,1)} async-done(((bf16[288,2304]{1,0:T(8,128)(2,1)}), bf16[2304,2304]{1,0:T(8,128)(2,1)}) %all-gather.23.cloned.1.call-update) | async-done | bytes 10616848 | tf_op jit(solution)/shard_map/all_gather | solution.py:99
  424.4 17.5 fusion.98
  441.9 48.2 %all-gather.25.cloned.1.call-done = bf16[2304,2304]{1,0:T(8,128)(2,1)} async-done(((bf16[288,2304]{1,0:T(8,128)(2,1)}), bf16[2304,2304]{1,0:T(8,128)(2,1)}) %all-gather.25.cloned.1.call-update) | async-done | bytes 10616848 | tf_op jit(solution)/shard_map/all_gather | solution.py:100
  490.2 22.1 %multiply_convert_fusion.1 = (bf16[1088,2304]{1,0:T(8,128)(2,1)}, f32[1088,2304]{1,0:T(8,128)}) fusion(f32[1088,2304]{1,0:T(8,128)} %fusion.98, bf16[1088,2304]{1,0:T(8,128)(2,1)} %multiply_convert_fusion.2, bf16[2304,2304]{1,0:T(8,128)(2,1)} %all-gather.25.cloned.1.call-done), kind=kOutput, calls=%fused_computation.68 | convolution fusion | flops 11576180736 | bytes 40697856 | tf_op jit(solution)/shard_map/dot_general | solution.py:156
  512.3 43.4 %all-gather.27.cloned.1.call-done = bf16[2304,2304]{0,1:T(8,128)(2,1)} async-done(((bf16[2304,288]{0,1:T(8,128)(2,1)}), bf16[2304,2304]{0,1:T(8,128)(2,1)}) %all-gather.27.cloned.1.call-update) | async-done | bytes 10616848 | tf_op jit(solution)/shard_map/all_gather | solution.py:101
  555.8 17.0 convolution_convert_fusion.3
  573.1 181.4 %all-reduce.11.cloned.1.call-done = bf16[1088,2304]{1,0:T(8,128)(2,1)} async-done(((bf16[1088,2304]{1,0:T(8,128)(2,1)}), bf16[1088,2304]{1,0:T(8,128)(2,1)}) %all-reduce.11.cloned.1.call-update) | async-done | bytes 5013520 | tf_op jit(solution)/shard_map/psum | solution.py:161
  758.4 7.9 fusion.43
  766.3 4.5 fusion.17
  770.7 25.7 %multiply_convert_fusion = (bf16[1088,2304]{1,0:T(8,128)(2,1)}, bf16[1088,2304]{1,0:T(8,128)(2,1)S(1)}) fusion(f32[1088,2304]{1,0:T(8,128)} %fusion.98, f32[1088,2304]{1,0:T(8,128)} %get-tuple-element.93, bf16[1088,2304]{1,0:T(8,128)(2,1)} %fusion.17, bf16[2304,2304]{0,1:T(8,128)(2,1)} %all-gather.27.cloned.1.call-done), kind=kOutput, calls=%fused_computation.67 | convolution fusion | flops 11611275264 | bytes 45711360 | tf_op jit(solution)/shard_map/rd,fd->rf/dot_general | solution.py:181
  796.5 14.3 fusion.99
  810.8 20.1 %fusion.14 = bf16[1088,2304]{1,0:T(8,128)(2,1)} fusion(f32[1088,2304]{1,0:T(8,128)} %fusion.99, bf16[1088,2304]{1,0:T(8,128)(2,1)} %get-tuple-element.66, bf16[2304,2304]{1,0:T(8,128)(2,1)} %all-gather.25.cloned.1.call-done), kind=kOutput, calls=%fused_computation.35 | convolution fusion | flops 11556126720 | bytes 30670848 | tf_op jit(solution)/shard_map/rf,df->rd/dot_general | solution.py:189
  831.7 180.0 %all-reduce.13.cloned.1.call-done = bf16[1088,2304]{1,0:T(8,128)(2,1)} async-done(((bf16[1088,2304]{1,0:T(8,128)(2,1)}), bf16[1088,2304]{1,0:T(8,128)(2,1)}) %all-reduce.13.cloned.1.call-update) | async-done | bytes 5013520 | tf_op jit(solution)/shard_map/psum | solution.py:190
  1011.6 8.8 fusion.34
  1020.4 12.6 convert_add_fusion
  1033.0 8.5 fusion.28
  1041.6 4.7 fusion.27
  1053.3 9.0 fusion.46
  1062.3 8.2 fusion.52
  1073.3 12.4 multiply_reduce_fusion.3
  1085.7 14.7 multiply_convert_fusion.6
  1100.5 5.5 convolution_bitcast_fusion.1
  1110.9 3.9 convolution_bitcast_fusion
  1117.8 8.7 fusion.100
  1126.5 3.8 reduce-scatter.13.cloned.1.call-done
  1139.0 13.8 reduce-scatter.15.cloned.1.call-done
  1153.9 5.4 convolution_add_fusion.1
  1164.4 8.0 convolution_convert_fusion.5
  1172.6 7.0 convolution_convert_fusion.6
  1179.7 5.3 convolution_convert_fusion.7
  1185.1 5.3 convolution_convert_fusion.8
  1190.5 154.3 %all-reduce.15.cloned.1.call-done = bf16[1088,2304]{1,0:T(8,128)(2,1)} async-done(((bf16[1088,2304]{1,0:T(8,128)(2,1)}), bf16[1088,2304]{1,0:T(8,128)(2,1)}) %all-reduce.15.cloned.1.call-update) | async-done | bytes 5013520 | tf_op jit(solution)/shard_map/psum | solution.py:260
  1344.8 7.7 fusion.35
  1354.0 20.2 %convolution_convert_fusion = bf16[2304,2304]{0,1:T(8,128)(2,1)} fusion(bf16[1088,2304]{1,0:T(8,128)(2,1)} %get-tuple-element.92, bf16[1088,2304]{1,0:T(8,128)(2,1)} %fusion.17), kind=kOutput, calls=%fused_computation | convolution fusion | flops 11556421632 | bytes 20643840 | tf_op jit(solution)/shard_map/rf,rd->fd/dot_general | solution.py:180
  1374.5 19.9 %convolution_convert_fusion.2 = bf16[2304,2304]{1,0:T(8,128)(2,1)} fusion(bf16[1088,2304]{1,0:T(8,128)(2,1)} %multiply_convert_fusion.2, bf16[1088,2304]{1,0:T(8,128)(2,1)} %copy-done.65), kind=kOutput, calls=%fused_computation.2 | convolution fusion | flops 11556421632 | bytes 20643840 | tf_op jit(solution)/shard_map/rd,rf->df/dot_general | solution.py:185
  1394.8 19.8 %convolution_convert_fusion.1 = bf16[2304,2304]{1,0:T(8,128)(2,1)} fusion(bf16[1088,2304]{1,0:T(8,128)(2,1)} %multiply_convert_fusion.2, bf16[1088,2304]{1,0:T(8,128)(2,1)} %get-tuple-element.66), kind=kOutput, calls=%fused_computation.1 | convolution fusion | flops 11556421632 | bytes 20643840 | tf_op jit(solution)/shard_map/rd,rf->df/dot_general | solution.py:186
  1416.5 20.2 %reduce-scatter.17.cloned.1.call-done = bf16[288,512]{1,0:T(8,128)(2,1)} async-done(((bf16[2304,512]{1,0:T(8,128)(2,1)}), bf16[288,512]{1,0:T(8,128)(2,1)}) %reduce-scatter.17.cloned.1.call-update) | async-done | bytes 294928 | tf_op jit(solution)/shard_map/reduce_scatter | solution.py:265
  1438.6 38.0 %reduce-scatter.21.cloned.1.call-done = bf16[288,256]{1,0:T(8,128)(2,1)} async-done(((bf16[2304,256]{1,0:T(8,128)(2,1)}), bf16[288,256]{1,0:T(8,128)(2,1)}) %reduce-scatter.21.cloned.1.call-update) | async-done | bytes 147472 | tf_op jit(solution)/shard_map/reduce_scatter | solution.py:271
  1478.3 39.3 %reduce-scatter.19.cloned.1.call-done = bf16[288,256]{1,0:T(8,128)(2,1)} async-done(((bf16[2304,256]{1,0:T(8,128)(2,1)}), bf16[288,256]{1,0:T(8,128)(2,1)}) %reduce-scatter.19.cloned.1.call-update) | async-done | bytes 147472 | tf_op jit(solution)/shard_map/reduce_scatter | solution.py:268
  1519.2 13.4 fusion.20
  1532.6 22.3 %reduce-scatter.31.cloned.1.call-done = bf16[288,4]{1,0:T(8,128)(2,1)} async-done(((bf16[2304,4]{1,0:T(8,128)(2,1)}), bf16[288,4]{1,0:T(8,128)(2,1)}) %reduce-scatter.31.cloned.1.call-update) | async-done | bytes 2320
  1556.5 84.2 %reduce-scatter.29.cloned.1.call-done = bf16[2304,288]{0,1:T(8,128)(2,1)} async-done(((bf16[2304,2304]{0,1:T(8,128)(2,1)}), bf16[2304,288]{0,1:T(8,128)(2,1)}) %reduce-scatter.29.cloned.1.call-update) | async-done | bytes 1327120 | tf_op jit(solution)/shard_map/reduce_scatter | solution.py:283
  1643.6 82.7 %reduce-scatter.25.cloned.1.call-done = bf16[288,2304]{1,0:T(8,128)(2,1)} async-done(((bf16[2304,2304]{1,0:T(8,128)(2,1)}), bf16[288,2304]{1,0:T(8,128)(2,1)}) %reduce-scatter.25.cloned.1.call-update) | async-done | bytes 1327120 | tf_op jit(solution)/shard_map/reduce_scatter | solution.py:277
  1729.4 82.7 %reduce-scatter.27.cloned.1.call-done = bf16[288,2304]{1,0:T(8,128)(2,1)} async-done(((bf16[2304,2304]{1,0:T(8,128)(2,1)}), bf16[288,2304]{1,0:T(8,128)(2,1)}) %reduce-scatter.27.cloned.1.call-update) | async-done | bytes 1327120 | tf_op jit(solution)/shard_map/reduce_scatter | solution.py:280
  (300 shorter events, 91.1 us)
Async XLA Ops:
  7.2 29.5 %all-gather.13.cloned.1.call-start = ((), (), s32[]{:S(2)}) async-start(), calls=%async_computation.11 | async-start | bytes 1327104 | tf_op jit(solution)/shard_map/all_gather | solution.py:96
  7.9 54.8 %all-gather.17.cloned.1.call-start = ((), (), s32[]{:S(2)}) async-start(), calls=%async_computation.13 | async-start | bytes 1327104 | tf_op jit(solution)/shard_map/all_gather | solution.py:97
  8.7 84.9 %all-gather.11.cloned.1.call-start = ((), (), s32[]{:S(2)}) async-start(), calls=%async_computation.10 | async-start | bytes 2654208 | tf_op jit(solution)/shard_map/all_gather | solution.py:95
  9.4 107.5 %all-gather.15.cloned.1.call-start = ((), (), s32[]{:S(2)}) async-start(), calls=%async_computation.12 | async-start | bytes 1572864 | tf_op jit(solution)/shard_map/all_gather | solution.py:120
  28.4 40.1 %copy-start.22 = (f32[2304]{0:T(1024)}, f32[2304]{0:T(1024)S(1)}, u32[]{:S(2)}) copy-start(f32[2304]{0:T(1024)S(1)} %get-tuple-element.65) | copy-start | bytes 27652
  28.4 335.0 %copy-start.24 = (f32[2304]{0:T(1024)}, f32[2304]{0:T(1024)S(1)}, u32[]{:S(2)}) copy-start(f32[2304]{0:T(1024)S(1)} %get-tuple-element.64) | copy-start | bytes 27652
  28.4 340.6 %copy-start.27 = (f32[2304]{0:T(1024)}, f32[2304]{0:T(1024)S(1)}, u32[]{:S(2)}) copy-start(f32[2304]{0:T(1024)S(1)} %get-tuple-element.63) | copy-start | bytes 27652
  28.5 118.3 %copy-start.33 = (s32[1088]{0:T(1024)}, s32[1088]{0:T(1024)S(1)}, u32[]{:S(2)}) copy-start(s32[1088]{0:T(1024)S(1)} %le.16) | copy-start | bytes 13060
  45.2 58.4 %copy-start.5 = (f32[1088,256]{1,0:T(8,128)}, f32[1088,256]{1,0:T(8,128)S(1)}, u32[]{:S(2)}) copy-start(f32[1088,256]{1,0:T(8,128)S(1)} %get-tuple-element.82) | copy-start | bytes 3342340
  45.2 58.4 %copy-start.7 = (f32[1088,256]{1,0:T(8,128)}, f32[1088,256]{1,0:T(8,128)S(1)}, u32[]{:S(2)}) copy-start(f32[1088,256]{1,0:T(8,128)S(1)} %get-tuple-element.81) | copy-start | bytes 3342340
  46.2 94.0 %all-gather.19.cloned.1.call-start = ((), (), s32[]{:S(2)}) async-start(), calls=%async_computation.14 | async-start | bytes 1572864 | tf_op jit(solution)/shard_map/all_gather | solution.py:121
  67.8 103.2 %all-gather.21.cloned.1.call-start = ((), (), s32[]{:S(2)}) async-start(), calls=%async_computation.15 | async-start | bytes 2654208 | tf_op jit(solution)/shard_map/all_gather | solution.py:98
  68.3 291.4 %all-reduce.9.cloned.1.call-start = ((), (), s32[]{:S(2)}) async-start(), calls=%async_computation.16 | async-start | bytes 10027008 | tf_op jit(solution)/shard_map/psum | solution.py:149
  74.9 72.0 %copy-start.43 = (s32[1088]{0:T(1024)}, s32[1088]{0:T(1024)S(1)}, u32[]{:S(2)}) copy-start(s32[1088]{0:T(1024)S(1)} %get-tuple-element.85) | copy-start | bytes 13060
  74.9 72.0 %copy-start.45 = (s32[1088]{0:T(1024)}, s32[1088]{0:T(1024)S(1)}, u32[]{:S(2)}) copy-start(s32[1088]{0:T(1024)S(1)} %get-tuple-element.86) | copy-start | bytes 13060
  74.9 72.0 %copy-start.39 = (s32[2112]{0:T(1024)}, s32[2112]{0:T(1024)S(1)}, u32[]{:S(2)}) copy-start(s32[2112]{0:T(1024)S(1)} %get-tuple-element.95) | copy-start | bytes 25348
  74.9 72.0 %copy-start.41 = (s32[2112]{0:T(1024)}, s32[2112]{0:T(1024)S(1)}, u32[]{:S(2)}) copy-start(s32[2112]{0:T(1024)S(1)} %get-tuple-element.96) | copy-start | bytes 25348
  74.9 71.9 %copy-start.31 = (bf16[2,32,256]{2,1,0:T(8,128)(2,1)}, bf16[2,32,256]{2,1,0:T(8,128)(2,1)S(1)}, u32[]{:S(2)}) copy-start(bf16[2,32,256]{2,1,0:T(8,128)(2,1)S(1)} %slice.101) | copy-start | bytes 98308
  75.0 47.0 %copy-start.51 = (bf16[2,32,256]{2,1,0:T(8,128)(2,1)}, bf16[2,32,256]{2,1,0:T(8,128)(2,1)S(1)}, u32[]{:S(2)}) copy-start(bf16[2,32,256]{2,1,0:T(8,128)(2,1)S(1)} %slice.99) | copy-start | bytes 98308
  104.2 17.7 copy-start.17
  121.9 25.0 %copy-start.55 = (f32[1088]{0:T(1024)}, f32[1088]{0:T(1024)S(1)}, u32[]{:S(2)}) copy-start(f32[1088]{0:T(1024)S(1)} %get-tuple-element.89) | copy-start | bytes 13060
  127.6 19.2 %copy-start.47 = (f32[1088]{0:T(1024)}, f32[1088]{0:T(1024)S(1)}, u32[]{:S(2)}) copy-start(f32[1088]{0:T(1024)S(1)} %get-tuple-element.61) | copy-start | bytes 13060
  127.6 19.3 %copy-start.57 = (f32[1088]{0:T(1024)}, f32[1088]{0:T(1024)S(1)}, u32[]{:S(2)}) copy-start(f32[1088]{0:T(1024)S(1)} %get-tuple-element.60) | copy-start | bytes 13060
  131.1 15.8 slice-start.5
  135.9 10.9 copy-start.49
  151.3 26.7 %copy-start.15 = (bf16[1088,2,256]{0,2,1:T(8,128)(2,1)}, bf16[1088,2,256]{0,2,1:T(8,128)(2,1)S(1)}, u32[]{:S(2)}) copy-start(bf16[1088,2,256]{0,2,1:T(8,128)(2,1)S(1)} %copy.42) | copy-start | bytes 3342340
  178.1 246.4 %all-gather.23.cloned.1.call-start = ((), (), s32[]{:S(2)}) async-start(), calls=%async_computation.17 | async-start | bytes 11943936 | tf_op jit(solution)/shard_map/all_gather | solution.py:99
  178.8 311.3 %all-gather.25.cloned.1.call-start = ((), (), s32[]{:S(2)}) async-start(), calls=%async_computation.18 | async-start | bytes 11943936 | tf_op jit(solution)/shard_map/all_gather | solution.py:100
  179.6 376.2 %all-gather.27.cloned.1.call-start = ((), (), s32[]{:S(2)}) async-start(), calls=%async_computation.19 | async-start | bytes 11943936 | tf_op jit(solution)/shard_map/all_gather | solution.py:101
  180.2 574.3 %all-reduce.11.cloned.1.call-start = ((), (), s32[]{:S(2)}) async-start(), calls=%async_computation.20 | async-start | bytes 10027008 | tf_op jit(solution)/shard_map/psum | solution.py:161
  572.8 185.3 %copy-start.26 = (f32[2304]{0:T(1024)S(1)}, f32[2304]{0:T(1024)}, u32[]{:S(2)}) copy-start(f32[2304]{0:T(1024)} %get-tuple-element.62) | copy-start | bytes 27652
  572.8 438.8 %all-reduce.13.cloned.1.call-start = ((), (), s32[]{:S(2)}) async-start(), calls=%async_computation.21 | async-start | bytes 10027008 | tf_op jit(solution)/shard_map/psum | solution.py:190
  754.5 11.8 slice-start
  766.2 30.2 %slice-start.11 = ((s8[10616832]{0:T(1024)(128)(4,1)}), s8[4194304]{0:T(1024)(128)(4,1)S(1)}, s32[]{:S(2)}) async-start(s8[10616832]{0:T(1024)(128)(4,1)} %bitcast.195), calls=%async_computation.44 | async-start | bytes 8388608
  770.7 25.7 %slice-start.12 = ((s8[10616832]{0:T(1024)(128)(4,1)}), s8[4194304]{0:T(1024)(128)(4,1)S(1)}, s32[]{:S(2)}) async-start(s8[10616832]{0:T(1024)(128)(4,1)} %bitcast.195), calls=%async_computation.45 | async-start | bytes 8388608
  770.7 25.7 %slice-start.13 = ((s8[10616832]{0:T(1024)(128)(4,1)}), s8[2228224]{0:T(1024)(128)(4,1)S(1)}, s32[]{:S(2)}) async-start(s8[10616832]{0:T(1024)(128)(4,1)} %bitcast.195), calls=%async_computation.46 | async-start | bytes 4456448
  796.4 14.4 copy-start.65
  830.9 180.7 %copy-start.28 = (f32[2304]{0:T(1024)S(1)}, f32[2304]{0:T(1024)}, u32[]{:S(2)}) copy-start(f32[2304]{0:T(1024)} %copy-done.27) | copy-start | bytes 27652
  830.9 180.7 %copy-start.36 = (f32[1088]{0:T(1024)S(1)}, f32[1088]{0:T(1024)}, u32[]{:S(2)}) copy-start(f32[1088]{0:T(1024)} %copy-done.35) | copy-start | bytes 13060
  831.0 299.3 %reduce-scatter.13.cloned.1.call-start = ((), (), s32[]{:S(2)}) async-start(), calls=%async_computation.22 | async-start | bytes 1572864 | tf_op jit(solution)/shard_map/reduce_scatter | solution.py:224
  1020.4 12.6 copy-start.25
  1020.4 12.6 copy-start.30
  1053.3 20.0 %slice-start.2 = ((s8[9469952]{0:T(1024)(128)(4,1)}), s8[4194304]{0:T(1024)(128)(4,1)S(1)}, s32[]{:S(2)}) async-start(s8[9469952]{0:T(1024)(128)(4,1)} %bitcast.147), calls=%async_computation.35 | async-start | bytes 8388608
  1053.3 20.0 %slice-start.3 = ((s8[9469952]{0:T(1024)(128)(4,1)}), s8[4194304]{0:T(1024)(128)(4,1)S(1)}, s32[]{:S(2)}) async-start(s8[9469952]{0:T(1024)(128)(4,1)} %bitcast.147), calls=%async_computation.36 | async-start | bytes 8388608
  1062.3 9.4 copy-start.21
  1062.3 9.4 copy-start.32
  1062.3 10.9 slice-start.4
  1085.7 14.7 copy-start.52
  1085.7 14.8 copy-start.63
  1110.9 42.0 %reduce-scatter.15.cloned.1.call-start = ((), (), s32[]{:S(2)}) async-start(), calls=%async_computation.23 | async-start | bytes 1572864 | tf_op jit(solution)/shard_map/reduce_scatter | solution.py:230
  1117.3 227.5 %all-reduce.15.cloned.1.call-start = ((), (), s32[]{:S(2)}) async-start(), calls=%async_computation.24 | async-start | bytes 10027008 | tf_op jit(solution)/shard_map/psum | solution.py:260
  1117.8 13.7 copy-start.10
  1131.4 21.4 %slice-start.10 = ((bf16[2112,256]{1,0:T(8,128)(2,1)}), bf16[64,256]{1,0:T(8,128)(2,1)S(1)}, s32[]{:S(2)}) async-start(bf16[2112,256]{1,0:T(8,128)(2,1)} %copy-done.19), calls=%async_computation.43 | async-start | bytes 65536 | tf_op jit(solution)/shard_map/slice | solution.py:241
  1131.5 22.4 %copy-start.13 = (bf16[2304,256]{1,0:T(8,128)(2,1)S(1)}, bf16[2304,256]{1,0:T(8,128)(2,1)}, u32[]{:S(2)}) copy-start(bf16[2304,256]{1,0:T(8,128)(2,1)} %all-gather.13.cloned.1.call-done) | copy-start | bytes 3538948
  1163.1 251.5 %reduce-scatter.23.cloned.1.call-start = ((), (), s32[]{:S(2)}) async-start(), calls=%async_computation.28 | async-start | bytes 2654208 | tf_op jit(solution)/shard_map/reduce_scatter | solution.py:274
  1172.4 264.4 %reduce-scatter.17.cloned.1.call-start = ((), (), s32[]{:S(2)}) async-start(), calls=%async_computation.25 | async-start | bytes 2654208 | tf_op jit(solution)/shard_map/reduce_scatter | solution.py:265
  1179.6 297.0 %reduce-scatter.21.cloned.1.call-start = ((), (), s32[]{:S(2)}) async-start(), calls=%async_computation.27 | async-start | bytes 1327104 | tf_op jit(solution)/shard_map/reduce_scatter | solution.py:271
  1185.0 159.8 %copy-start.23 = (f32[2304]{0:T(1024)S(1)}, f32[2304]{0:T(1024)}, u32[]{:S(2)}) copy-start(f32[2304]{0:T(1024)} %copy-done.22) | copy-start | bytes 27652
  1185.0 159.8 %copy-start.38 = (f32[1088]{0:T(1024)S(1)}, f32[1088]{0:T(1024)}, u32[]{:S(2)}) copy-start(f32[1088]{0:T(1024)} %copy-done.37) | copy-start | bytes 13060
  1185.0 332.5 %reduce-scatter.19.cloned.1.call-start = ((), (), s32[]{:S(2)}) async-start(), calls=%async_computation.26 | async-start | bytes 1327104 | tf_op jit(solution)/shard_map/reduce_scatter | solution.py:268
  1190.4 364.5 %reduce-scatter.31.cloned.1.call-start = ((), (), s32[]{:S(2)}) async-start(), calls=%async_computation.32 | async-start | bytes 663552
  1353.7 286.9 %reduce-scatter.29.cloned.1.call-start = ((), (), s32[]{:S(2)}) async-start(), calls=%async_computation.31 | async-start | bytes 11943936 | tf_op jit(solution)/shard_map/reduce_scatter | solution.py:283
  1374.2 352.1 %reduce-scatter.25.cloned.1.call-start = ((), (), s32[]{:S(2)}) async-start(), calls=%async_computation.29 | async-start | bytes 11943936 | tf_op jit(solution)/shard_map/reduce_scatter | solution.py:277
  1394.5 417.7 %reduce-scatter.27.cloned.1.call-start = ((), (), s32[]{:S(2)}) async-start(), calls=%async_computation.30 | async-start | bytes 11943936 | tf_op jit(solution)/shard_map/reduce_scatter | solution.py:280
  (39 other events, 164.5 us)
Sparse Core Ops, SparseCore 0:
  9.9 26.7 all-gather.12
  38.6 24.0 all-gather.16
  64.6 28.9 all-gather.10
  95.6 21.2 all-gather.14
  118.9 21.2 all-gather.18
  142.0 28.9 all-gather.20
  178.2 181.4 all-reduce.8
  361.6 62.7 all-gather.22
  426.3 63.7 all-gather.24
  491.9 63.8 all-gather.26
  572.9 181.4 all-reduce.10
  831.1 180.4 all-reduce.12
  1111.0 19.2 reduce-scatter.12
  1132.5 20.3 reduce-scatter.14
  1163.3 181.4 all-reduce.14
  1348.6 41.4 reduce-scatter.22
  1394.2 42.4 reduce-scatter.16
  1439.8 36.7 reduce-scatter.20
  1480.8 36.7 reduce-scatter.18
  1520.5 34.3 reduce-scatter.30
  1558.4 82.1 reduce-scatter.28
  1644.2 82.1 reduce-scatter.24
  1729.9 82.1 reduce-scatter.26
where the time goes:
time: 1830 us; the launch traced here: 1820 us
  waiting for transfers between devices  1300 us (71%)
  matrix products  308 us (17%)
  other arithmetic  152 us (8%)
  local copies, waits for them, and re-layouts  28.1 us (2%)
    psum x1, waiting for transfers between devices, per_device(): lax.psum(jnp.dot(hidden, full_down, preferred_element_type=jnp.float32).a...  181 us
    psum x1, waiting for transfers between devices, per_device(): lax.psum(ffn_part.astype(jnp.bfloat16), 'tensor').astype(jnp.float32)  180 us
    psum x1, waiting for transfers between devices, per_device(): lax.psum(jnp.dot(context, full_out, preferred_element_type=jnp.float32).a...  179 us
    psum x1, waiting for transfers between devices, per_device(): lax.psum(attn_part.astype(jnp.bfloat16), 'tensor').astype(jnp.float32)  154 us
    reduce_scatter x1, waiting for transfers between devices, per_device(): lax.psum_scatter(grad_down.astype(jnp.bfloat16), ('dp', 'seq'), scatter_d...  84.2 us
    reduce_scatter x1, waiting for transfers between devices, per_device(): lax.psum_scatter(grad_up.astype(jnp.bfloat16), ('dp', 'seq'), scatter_dim...  82.7 us
    reduce_scatter x1, waiting for transfers between devices, per_device(): lax.psum_scatter(grad_gate.astype(jnp.bfloat16), ('dp', 'seq'), scatter_d...  82.7 us
    all_gather x1, waiting for transfers between devices, per_device(): lax.all_gather(gate_weight, ('dp', 'seq'), axis=0, tiled=True)  48.9 us
  transfers between devices with their start and end apart: 23, of which 22 were waited for; matrix products, arithmetic and copies ran while one was open for 15% of the time, Pallas kernels for 0%

commit v1 on v0

--- a/solution.py
+++ b/solution.py
@@ -1,7 +1,13 @@
+import functools
+
 import jax
 import jax.numpy as jnp
 from jax import lax
+from jax.experimental import pallas as pl
+from jax.experimental.pallas import tpu as pltpu
 from jax.sharding import PartitionSpec as P
+
+MESH = pl.DeviceIdType.MESH
 
 HEAD = 256
 CONT = 32
@@ -10,6 +16,123 @@
 EPS = 1e-06
 SOFTCAP = 50.0
 THETA = 10000.0
+
+
+def chain_kernel(size, width, x_ref, o_ref, low_buf, high_buf, *sems):
+    low_in, low_out, low_last_in, low_last_out, high_in, high_out, high_last_in, high_last_out = sems
+    place = lax.axis_index("tensor")
+    dp, seq = lax.axis_index("dp"), lax.axis_index("seq")
+    down = (dp, seq, jnp.maximum(place - 1, 0))
+    up = (dp, seq, jnp.minimum(place + 1, size - 1))
+    first, last = place == 0, place == size - 1
+    chunks = x_ref.shape[1] // width
+    half = x_ref.shape[0] // 2
+    rows = (pl.ds(0, half), pl.ds(half, half))
+    barrier = pltpu.get_barrier_semaphore()
+
+    @pl.when(jnp.logical_not(first))
+    def _():
+        pl.semaphore_signal(barrier, inc=1, device_id=down, device_id_type=MESH)
+
+    @pl.when(jnp.logical_not(last))
+    def _():
+        pl.semaphore_signal(barrier, inc=1, device_id=up, device_id_type=MESH)
+    pl.semaphore_wait(barrier, 2 - first.astype(jnp.int32) - last.astype(jnp.int32))
+
+    def columns(c):
+        return pl.ds(pl.multiple_of(c * width, 128), width)
+
+    def side(which):
+        buf = (low_buf, high_buf)[which]
+        sin, sout, lin, lout = (sems[4 * which: 4 * which + 4])
+        toward = (down, up)[which]
+        back = (up, down)[which]
+        start = (last, first)[which]
+        end = (first, last)[which]
+        rank = (size - 1 - place, place)[which]
+        rs = rows[which]
+
+        def passing(c, src):
+            return pltpu.make_async_remote_copy(src, buf.at[c], sout.at[c], sin.at[c], device_id=toward, device_id_type=MESH)
+
+        def sharing(c, ):
+            view = o_ref.at[rs, columns(c)]
+            return pltpu.make_async_remote_copy(view, view, lout.at[c], lin.at[c], device_id=back, device_id_type=MESH)
+
+        def reduce_step(s):
+            c = s - rank
+            ok = (c >= 0) & (c < chunks)
+
+            @pl.when(ok & start)
+            def _():
+                passing(c, x_ref.at[rs, columns(c)]).start()
+
+            @pl.when(ok & jnp.logical_not(start))
+            def _():
+                passing(c, buf.at[c]).wait_recv()
+                total = buf[c].astype(jnp.float32) + x_ref[rs, columns(c)].astype(jnp.float32)
+
+                @pl.when(end)
+                def _():
+                    o_ref[rs, columns(c)] = total.astype(jnp.bfloat16)
+                    sharing(c).start()
+
+                @pl.when(jnp.logical_not(end))
+                def _():
+                    buf[c] = total.astype(jnp.bfloat16)
+                    passing(c, buf.at[c]).start()
+
+        def share_step(s):
+            c = s - (size - 1) - (size - 1 - rank)
+            ok = (c >= 0) & (c < chunks)
+
+            @pl.when(ok & jnp.logical_not(end))
+            def _():
+                sharing(c).wait_recv()
+
+                @pl.when(jnp.logical_not(start))
+                def _():
+                    sharing(c).start()
+
+        def finish(c):
+            @pl.when(jnp.logical_not(end))
+            def _():
+                passing(c, buf.at[c]).wait_send()
+
+            @pl.when(jnp.logical_not(start))
+            def _():
+                sharing(c).wait_send()
+        return reduce_step, share_step, finish
+
+    sides = [side(0), side(1)]
+
+    @pl.loop(0, chunks + 2 * (size - 1))
+    def _(s):
+        for one in sides:
+            one[0](s)
+        for one in sides:
+            one[1](s)
+
+    @pl.loop(0, chunks)
+    def _(c):
+        for one in sides:
+            one[2](c)
+
+
+def chain_sum(x, cid, width=256):
+    size = lax.axis_size("tensor")
+    rows, cols = x.shape
+    chunks = cols // width
+    return pl.pallas_call(
+        functools.partial(chain_kernel, size, width),
+        out_shape=jax.ShapeDtypeStruct(x.shape, jnp.bfloat16),
+        in_specs=[pl.BlockSpec(memory_space=pltpu.VMEM)],
+        out_specs=pl.BlockSpec(memory_space=pltpu.VMEM),
+        scratch_shapes=[pltpu.VMEM((chunks, rows // 2, width), jnp.bfloat16)] * 2
+        + [pltpu.SemaphoreType.DMA((chunks,))] * 8,
+        compiler_params=pltpu.CompilerParams(collective_id=cid, has_side_effects=True, vmem_limit_bytes=48 * 2**20),
+        cost_estimate=pl.CostEstimate(flops=rows*cols, bytes_accessed=200*2**20, transcendentals=0),
+    )(x)
 
 
 def normalize(values):
@@ -91,16 +214,26 @@
     visible, places = visibility(
         micro_count, row_count, prompt_dev, prompt_all, CONT, seq_pos, prompt_of[:, 0]
     )
-    full_query, full_key, full_value, full_out, full_gate, full_up, full_down, gain_rows = (
-        lax.all_gather(query_weight, ("dp", "seq"), axis=0, tiled=True),
-        lax.all_gather(key_weight, ("dp", "seq"), axis=0, tiled=True),
-        lax.all_gather(value_weight, ("dp", "seq"), axis=0, tiled=True),
-        lax.all_gather(out_weight, ("dp", "seq"), axis=1, tiled=True),
-        lax.all_gather(gate_weight, ("dp", "seq"), axis=0, tiled=True),
-        lax.all_gather(up_weight, ("dp", "seq"), axis=0, tiled=True),
-        lax.all_gather(down_weight, ("dp", "seq"), axis=1, tiled=True),
-        lax.all_gather(norm_gains, ("dp", "seq"), axis=1, tiled=True),
-    )
+    axes = ("dp", "seq")
+    query_width = query_weight.shape[1]
+    side_weights = jnp.concatenate(
+        [
+            query_weight,
+            key_weight,
+            value_weight,
+            jnp.pad(norm_gains.T, ((0, 0), (0, 128 - norm_gains.shape[0]))),
+        ],
+        axis=1,
+    )
+    full_side = lax.all_gather(side_weights, axes, axis=0, tiled=True)
+    full_query = full_side[:, :query_width]
+    full_key = full_side[:, query_width : query_width + HEAD]
+    full_value = full_side[:, query_width + HEAD : query_width + 2 * HEAD]
+    gain_rows = full_side[:, query_width + 2 * HEAD : query_width + 2 * HEAD + 4].T
+    full_out = lax.all_gather(out_weight, axes, axis=1, tiled=True)
+    full_gate = lax.all_gather(gate_weight, axes, axis=0, tiled=True)
+    full_up = lax.all_gather(up_weight, axes, axis=0, tiled=True)
+    full_down = lax.all_gather(down_weight, axes, axis=1, tiled=True)
     gain_float = gain_rows.astype(jnp.float32)
     inputs = tokens.reshape(total_rows, model_width).astype(jnp.float32)
     normed_in = (normalize(inputs) * gain_float[0]).astype(jnp.bfloat16)
@@ -116,10 +249,16 @@
     value_local = value_raw.astype(jnp.bfloat16)
     key_grid = key_local.reshape(micro_count, row_count, HEAD)
     value_grid = value_local.reshape(micro_count, row_count, HEAD)
-    prompt_keys, prompt_values = (
-        lax.all_gather(key_grid[:, :prompt_dev], "seq", axis=1, tiled=True),
-        lax.all_gather(value_grid[:, :prompt_dev], "seq", axis=1, tiled=True),
-    )
+    own_pair = jnp.concatenate([key_grid[:, :prompt_dev], value_grid[:, :prompt_dev]], axis=2)
+    if seq_count == 2:
+        other_pair = lax.ppermute(own_pair, "seq", [(0, 1), (1, 0)])
+        early = seq_pos == 0
+        prompt_pair = jnp.concatenate(
+            [jnp.where(early, own_pair, other_pair), jnp.where(early, other_pair, own_pair)], axis=1
+        )
+    else:
+        prompt_pair = lax.all_gather(own_pair, "seq", axis=1, tiled=True)
+    prompt_keys, prompt_values = prompt_pair[..., :HEAD], prompt_pair[..., HEAD:]
     key_rows = jnp.concatenate(
         [
             prompt_keys.reshape(micro_count * prompt_all, HEAD),
@@ -146,9 +285,9 @@
         contexts.append(jnp.dot(probs, value_rows, preferred_element_type=jnp.float32))
         log_sums.append(row_peak + jnp.log(summed))
     context = jnp.stack(contexts, axis=1).reshape(total_rows, -1).astype(jnp.bfloat16)
-    attn = lax.psum(
+    attn = chain_sum(
         jnp.dot(context, full_out, preferred_element_type=jnp.float32).astype(jnp.bfloat16),
-        "tensor",
+        0,
     ).astype(jnp.float32)
     middle = inputs + normalize(attn) * gain_float[1]
     ffn_in = (normalize(middle) * gain_float[2]).astype(jnp.bfloat16)
@@ -158,22 +297,11 @@
         lambda gate_in, up_in: jax.nn.gelu(gate_in, approximate=True) * up_in, gate, up_val
     )
     hidden = hidden_act.astype(jnp.bfloat16)
-    ffn = lax.psum(
+    ffn = chain_sum(
         jnp.dot(hidden, full_down, preferred_element_type=jnp.float32).astype(jnp.bfloat16),
-        "tensor",
+        1,
     ).astype(jnp.float32)
     result = middle + normalize(ffn) * gain_float[3]
-    full_query, full_key, full_value, full_out, full_gate, full_up, full_down, gain_rows = (
-        lax.all_gather(query_weight, ("dp", "seq"), axis=0, tiled=True),
-        lax.all_gather(key_weight, ("dp", "seq"), axis=0, tiled=True),
-        lax.all_gather(value_weight, ("dp", "seq"), axis=0, tiled=True),
-        lax.all_gather(out_weight, ("dp", "seq"), axis=1, tiled=True),
-        lax.all_gather(gate_weight, ("dp", "seq"), axis=0, tiled=True),
-        lax.all_gather(up_weight, ("dp", "seq"), axis=0, tiled=True),
-        lax.all_gather(down_weight, ("dp", "seq"), axis=1, tiled=True),
-        lax.all_gather(norm_gains, ("dp", "seq"), axis=1, tiled=True),
-    )
-    gain_float = gain_rows.astype(jnp.float32)
     upstream = cotangent.reshape(total_rows, model_width).astype(jnp.float32)
     d_ffn, gain_fourth = norm_back(ffn, gain_float[3], upstream)
     d_ffn = d_ffn.astype(jnp.bfloat16)
@@ -187,7 +315,7 @@
     ffn_part = jnp.einsum(
         "rf,df->rd", d_gate, full_gate, preferred_element_type=jnp.float32
     ) + jnp.einsum("rf,df->rd", d_up, full_up, preferred_element_type=jnp.float32)
-    d_ffn_in = lax.psum(ffn_part.astype(jnp.bfloat16), "tensor").astype(jnp.float32)
+    d_ffn_in = chain_sum(ffn_part.astype(jnp.bfloat16), 2).astype(jnp.float32)
     d_mid_norm, gain_third = norm_back(middle, gain_float[2], d_ffn_in)
     d_middle = upstream + d_mid_norm
     d_attn, gain_second = norm_back(attn, gain_float[1], d_middle)
@@ -220,20 +348,24 @@
             "rk,rd->kd", probs_low, d_context[:, head_pos], preferred_element_type=jnp.float32
         )
     split_at = micro_count * prompt_all
-    prompt_key_grad, prompt_value_grad = (
-        lax.psum_scatter(
-            key_grad[:split_at].reshape(micro_count, prompt_all, HEAD).astype(jnp.bfloat16),
-            "seq",
-            scatter_dimension=1,
-            tiled=True,
-        ).astype(jnp.float32),
-        lax.psum_scatter(
-            value_grad[:split_at].reshape(micro_count, prompt_all, HEAD).astype(jnp.bfloat16),
-            "seq",
-            scatter_dimension=1,
-            tiled=True,
-        ).astype(jnp.float32),
-    )
+    pair_grad = jnp.concatenate(
+        [
+            key_grad[:split_at].reshape(micro_count, prompt_all, HEAD),
+            value_grad[:split_at].reshape(micro_count, prompt_all, HEAD),
+        ],
+        axis=2,
+    )
+    if seq_count == 2:
+        low_part, high_part = pair_grad[:, :prompt_dev], pair_grad[:, prompt_dev:]
+        early = seq_pos == 0
+        sent = jnp.where(early, high_part, low_part).astype(jnp.bfloat16)
+        kept = jnp.where(early, low_part, high_part)
+        pair_grad = kept + lax.ppermute(sent, "seq", [(0, 1), (1, 0)]).astype(jnp.float32)
+    else:
+        pair_grad = lax.psum_scatter(
+            pair_grad.astype(jnp.bfloat16), "seq", scatter_dimension=1, tiled=True
+        ).astype(jnp.float32)
+    prompt_key_grad, prompt_value_grad = pair_grad[..., :HEAD], pair_grad[..., HEAD:]
     own_keys = jnp.concatenate(
         [prompt_key_grad, key_grad[split_at:].reshape(micro_count, CONT, HEAD)], axis=1
     ).reshape(total_rows, HEAD)
@@ -257,35 +389,36 @@
     attn_part = attn_part + jnp.einsum(
         "rc,dc->rd", d_value, full_value, preferred_element_type=jnp.float32
     )
-    d_normed = lax.psum(attn_part.astype(jnp.bfloat16), "tensor").astype(jnp.float32)
+    d_normed = chain_sum(attn_part.astype(jnp.bfloat16), 3).astype(jnp.float32)
     d_in_norm, gain_first = norm_back(inputs, gain_float[0], d_normed)
     input_grad = d_middle + d_in_norm
     grad_gains = jnp.stack([gain_first, gain_second, gain_third, gain_fourth], axis=0)
+    def scatter(grad, axis):
+        return lax.psum_scatter(
+            grad.astype(jnp.bfloat16), axes, scatter_dimension=axis, tiled=True
+        ).astype(jnp.float32)
+
+    side_grad = scatter(
+        jnp.concatenate(
+            [
+                grad_query,
+                grad_key,
+                grad_value,
+                jnp.pad(grad_gains.T, ((0, 0), (0, 128 - grad_gains.shape[0]))),
+            ],
+            axis=1,
+        ),
+        0,
+    )
     shares = (
-        lax.psum_scatter(
-            grad_query.astype(jnp.bfloat16), ("dp", "seq"), scatter_dimension=0, tiled=True
-        ).astype(jnp.float32),
-        lax.psum_scatter(
-            grad_key.astype(jnp.bfloat16), ("dp", "seq"), scatter_dimension=0, tiled=True
-        ).astype(jnp.float32),
-        lax.psum_scatter(
-            grad_value.astype(jnp.bfloat16), ("dp", "seq"), scatter_dimension=0, tiled=True
-        ).astype(jnp.float32),
-        lax.psum_scatter(
-            grad_out.astype(jnp.bfloat16), ("dp", "seq"), scatter_dimension=1, tiled=True
-        ).astype(jnp.float32),
-        lax.psum_scatter(
-            grad_gate.astype(jnp.bfloat16), ("dp", "seq"), scatter_dimension=0, tiled=True
-        ).astype(jnp.float32),
-        lax.psum_scatter(
-            grad_up.astype(jnp.bfloat16), ("dp", "seq"), scatter_dimension=0, tiled=True
-        ).astype(jnp.float32),
-        lax.psum_scatter(
-            grad_down.astype(jnp.bfloat16), ("dp", "seq"), scatter_dimension=1, tiled=True
-        ).astype(jnp.float32),
-        lax.psum_scatter(
-            grad_gains.astype(jnp.bfloat16), ("dp", "seq"), scatter_dimension=1, tiled=True
-        ).astype(jnp.float32),
+        side_grad[:, :query_width],
+        side_grad[:, query_width : query_width + HEAD],
+        side_grad[:, query_width + HEAD : query_width + 2 * HEAD],
+        scatter(grad_out, 1),
+        scatter(grad_gate, 0),
+        scatter(grad_up, 0),
+        scatter(grad_down, 1),
+        side_grad[:, query_width + 2 * HEAD : query_width + 2 * HEAD + 4].T,
     )
     return (
         result.reshape(tokens.shape).astype(jnp.bfloat16),

time: 1830 us -> 1320 us (0.72)
  waiting for transfers between devices: 1300 us -> 291 us
  Pallas kernels: 0 us -> 521 us
    psum x4 -> x0, waiting for transfers between devices: 695 us -> none  [the longest x1 181 us: per_device(): lax.psum(jnp.dot(hidden, full_down, preferred_element_type=jnp.float32).a...]
    pallas_call x0 -> x4, Pallas kernels: none -> 521 us  [chain_sum(): pl.pallas_call(functools.partial(chain_kernel, size, width), out_shape=ja...]
    all_gather x9 -> x5, waiting for transfers between devices: 214 us -> 36.5 us  [the longest x1 36.5 us: per_device(): full_side = lax.all_gather(side_weights, axes, axis=0, tiled=True)]
    reduce_scatter x9 -> x4, waiting for transfers between devices: 365 us -> 227 us  [scatter(): lax.psum_scatter(grad.astype(jnp.bfloat16), axes, scatter_dimension=axis,...]
    ppermute x0 -> x2, waiting for transfers between devices: none -> 25.3 us  [the longest x1 25.3 us: per_device(): other_pair = lax.ppermute(own_pair, 'seq', [(0, 1), (1, 0)])]
    unnamed x24 -> x11, waiting for transfers between devices: 27 us -> 2.53 us
  transfers between devices with their start and end apart: 23 -> 12, of which waited for: 22 -> 5; matrix products, arithmetic and copies ran while one was open for 15% -> 20% of each run, Pallas kernels for 0% -> 20%
where the time goes in v1:
time: 1320 us; the launch traced here: 1310 us
  Pallas kernels  521 us (39%)
  matrix products  293 us (22%)
  waiting for transfers between devices  291 us (22%)
  other arithmetic  149 us (11%)
  local copies, waits for them, and re-layouts  37.6 us (3%)
  between operations  15.9 us (1%)
    pallas_call x4, Pallas kernels, chain_sum(): pl.pallas_call(functools.partial(chain_kernel, size, width), out_shape=ja...  521 us
    reduce_scatter x4, waiting for transfers between devices, scatter(): lax.psum_scatter(grad.astype(jnp.bfloat16), axes, scatter_dimension=axis,...  227 us
    all_gather x1, waiting for transfers between devices, per_device(): full_side = lax.all_gather(side_weights, axes, axis=0, tiled=True)  36.5 us
    reduce_sum x4, other arithmetic, norm_back(): return (backed, jnp.sum(upstream * normed, axis=0))  27.9 us
  transfers between devices with their start and end apart: 12, of which 5 were waited for; matrix products, arithmetic and copies ran while one was open for 20% of the time, Pallas kernels for 20%

profile of v1, /device:TPU:0, one launch (start us, length us, event | category | flops | bytes accessed | tf_op | source)
XLA Modules:
  0.0 1309.3 jit_solution(16971690011616808534)
XLA Ops:
  8.1 2.0 fusion.87
  13.4 3.5 multiply_reduce_fusion.1
  18.1 36.5 %all-gather.6.cloned.1.call-done = bf16[2304,1152]{1,0:T(8,128)(2,1)} async-done(((bf16[288,1152]{1,0:T(8,128)(2,1)}), bf16[2304,1152]{1,0:T(8,128)(2,1)}) %all-gather.6.cloned.1.call-update) | async-done | bytes 5308432 | tf_op jit(solution)/shard_map/all_gather | solution.py:228
  55.8 2.5 slice_reduce_fusion
  58.3 6.0 multiply_convert_fusion.4
  68.7 4.1 fusion.73
  74.7 4.4 copy.40
  80.4 5.7 fusion.110
  86.8 25.3 %collective-permute-done = bf16[2,512,512]{2,1,0:T(8,128)(2,1)S(1)} collective-permute-done((bf16[2,512,512]{2,1,0:T(8,128)(2,1)S(1)}, bf16[2,512,512]{2,1,0:T(8,128)(2,1)S(1)}, u32[]{:S(2)}, u32[]{:S(2)}) %collective-permute-start) | collective-permute-done | bytes 1048608 | tf_op jit(solution)/shard_map/ppermute | solution.py:254
  112.8 3.7 fusion.57
  116.5 5.6 fusion.45
  122.2 4.7 fusion.46
  126.9 3.6 fusion.62
  130.6 3.6 fusion.61
  136.0 7.1 convolution_convert_fusion.4.x_ref
  143.2 136.7 %shard_map.186 = bf16[1088,2304]{1,0:T(8,128)(2,1)S(1)} custom-call(bf16[1088,2304]{1,0:T(8,128)(2,1)} %convolution_convert_fusion.4.x_ref), custom_call_target="tpu_custom_call" | custom-call | flops 2506752 | bytes 209715200 | tf_op jit(solution)/shard_map/pallas_call | solution.py:126
  281.0 5.2 fusion.24
  290.2 3.3 multiply_convert_fusion.2
  293.5 17.5 %fusion.111 = f32[1088,2304]{1,0:T(8,128)} fusion(bf16[1088,2304]{1,0:T(8,128)(2,1)} %multiply_convert_fusion.2, bf16[2304,2304]{1,0:T(8,128)(2,1)} %all-gather.10.cloned.1.call-done), kind=kOutput, calls=%fused_computation.226 | convolution fusion | flops 11551113216 | bytes 25657344 | tf_op jit(solution)/shard_map/dot_general | solution.py:294
  311.0 22.5 %multiply_convert_fusion.1 = (bf16[1088,2304]{1,0:T(8,128)(2,1)}, f32[1088,2304]{1,0:T(8,128)}) fusion(f32[1088,2304]{1,0:T(8,128)} %fusion.111, bf16[1088,2304]{1,0:T(8,128)(2,1)} %multiply_convert_fusion.2, bf16[2304,2304]{1,0:T(8,128)(2,1)} %all-gather.12.cloned.1.call-done), kind=kOutput, calls=%fused_computation.70 | convolution fusion | flops 11576180736 | bytes 40697856 | tf_op jit(solution)/shard_map/dot_general | solution.py:295
  333.5 17.0 %convolution_convert_fusion.3.x_ref = bf16[1088,2304]{1,0:T(8,128)(2,1)} fusion(bf16[1088,2304]{1,0:T(8,128)(2,1)} %get-tuple-element.88, bf16[2304,2304]{0,1:T(8,128)(2,1)} %all-gather.14.cloned.1.call-done), kind=kOutput, calls=%fused_computation.37 | convolution fusion | flops 11553619968 | bytes 20643840 | tf_op jit(solution)/shard_map/dot_general | solution.py:301
  350.5 131.1 %shard_map.187 = bf16[1088,2304]{1,0:T(8,128)(2,1)S(1)} custom-call(bf16[1088,2304]{1,0:T(8,128)(2,1)} %convolution_convert_fusion.3.x_ref), custom_call_target="tpu_custom_call" | custom-call | flops 2506752 | bytes 209715200 | tf_op jit(solution)/shard_map/pallas_call | solution.py:126
  482.7 9.4 fusion.44
  492.2 4.3 fusion.18
  496.5 25.8 %multiply_convert_fusion = (bf16[1088,2304]{1,0:T(8,128)(2,1)}, bf16[1088,2304]{1,0:T(8,128)(2,1)S(1)}) fusion(f32[1088,2304]{1,0:T(8,128)} %fusion.111, f32[1088,2304]{1,0:T(8,128)} %get-tuple-element.89, bf16[1088,2304]{1,0:T(8,128)(2,1)} %fusion.18, bf16[2304,2304]{0,1:T(8,128)(2,1)} %all-gather.14.cloned.1.call-done), kind=kOutput, calls=%fused_computation.69 | convolution fusion | flops 11611275264 | bytes 45711360 | tf_op jit(solution)/shard_map/rd,fd->rf/dot_general | solution.py:309
  522.3 14.8 %fusion.112 = f32[1088,2304]{1,0:T(8,128)} fusion(bf16[1088,2304]{1,0:T(8,128)(2,1)S(1)} %get-tuple-element.57, bf16[2304,2304]{1,0:T(8,128)(2,1)S(1)} %bitcast.204), kind=kOutput, calls=%fused_computation.227 | convolution fusion | flops 11551113216 | bytes 25657344 | tf_op jit(solution)/shard_map/rf,df->rd/dot_general | solution.py:315
  537.1 19.7 %fusion.14.x_ref = bf16[1088,2304]{1,0:T(8,128)(2,1)} fusion(f32[1088,2304]{1,0:T(8,128)} %fusion.112, bf16[1088,2304]{1,0:T(8,128)(2,1)} %get-tuple-element.56, bf16[2304,2304]{1,0:T(8,128)(2,1)} %all-gather.12.cloned.1.call-done), kind=kOutput, calls=%fused_computation.35 | convolution fusion | flops 11556126720 | bytes 30670848 | tf_op jit(solution)/shard_map/rf,df->rd/dot_general | solution.py:317
  556.8 126.7 %shard_map.188 = bf16[1088,2304]{1,0:T(8,128)(2,1)S(1)} custom-call(bf16[1088,2304]{1,0:T(8,128)(2,1)} %fusion.14.x_ref), custom_call_target="tpu_custom_call" | custom-call | flops 2506752 | bytes 209715200 | tf_op jit(solution)/shard_map/pallas_call | solution.py:126
  683.5 2.3 copy-done.3
  685.8 8.3 fusion.35
  694.2 14.8 %convert_add_fusion = (f32[1088,2304]{1,0:T(8,128)}, bf16[1088,2304]{1,0:T(8,128)(2,1)}) fusion(bf16[1088,2304]{1,0:T(8,128)(2,1)} %copy-done.3, f32[1088,2304]{1,0:T(8,128)} %copy-done.4, f32[1088]{0:T(1024)S(1)} %broadcast_multiply_fusion.3, f32[2304]{0:T(1024)S(1)} %copy-done.33, f32[1088]{0:T(1024)S(1)} %copy-done.41, ...), kind=kLoop, calls=%fused_computation.4 | loop fusion | flops 32587776 | bytes 40139520 | tf_op jit(solution)/shard_map/add | solution.py:320
  709.0 6.3 fusion.29
  715.4 5.8 fusion.28
  721.2 2.2 copy-done.13
  723.4 4.5 convolution_convert_fusion.6
  727.9 5.9 convolution_convert_fusion.9
  736.1 9.1 fusion.48
  745.2 8.3 fusion.54
  755.3 12.4 multiply_reduce_fusion.3
  767.7 15.1 %multiply_convert_fusion.6 = (bf16[1088,2112]{1,0:T(8,128)(2,1)}, bf16[1088,2112]{1,0:T(8,128)(2,1)S(1)}) fusion(f32[1088,2112]{1,0:T(8,128)} %copy-done.11, f32[1088,2112]{1,0:T(8,128)} %get-tuple-element.90, f32[1088]{0:T(1024)S(1)} %get-tuple-element.52, f32[1088]{0:T(1024)S(1)} %copy-done.52, s32[1088]{0:T(1024)S(1)} %copy-done.39, ...), kind=kLoop, calls=%fused_computation.79 | loop fusion | flops 62042112 | bytes 46004480 | tf_op jit(solution)/shard_map/convert_element_type | solution.py:340
  782.9 5.0 convolution_bitcast_fusion.1
  789.6 2.5 convolution_bitcast_fusion
  795.4 2.9 select_convert_fusion
  801.5 9.2 fusion.66
  810.7 7.0 convolution_convert_fusion.5
  819.7 3.7 fusion.80
  823.5 3.7 fusion.79
  827.2 5.8 convolution_add_fusion.1
  833.0 5.0 fusion.15.x_ref
  838.0 126.1 %shard_map.189 = bf16[1088,2304]{1,0:T(8,128)(2,1)S(1)} custom-call(bf16[1088,2304]{1,0:T(8,128)(2,1)} %fusion.15.x_ref), custom_call_target="tpu_custom_call" | custom-call | flops 2506752 | bytes 209715200 | tf_op jit(solution)/shard_map/pallas_call | solution.py:126
  964.1 3.9 fusion.36
  971.6 2.9 fusion.47
  974.5 8.6 copy.50
  983.2 20.0 %convolution_convert_fusion = bf16[2304,2304]{0,1:T(8,128)(2,1)} fusion(bf16[1088,2304]{1,0:T(8,128)(2,1)} %get-tuple-element.88, bf16[1088,2304]{1,0:T(8,128)(2,1)} %fusion.18), kind=kOutput, calls=%fused_computation | convolution fusion | flops 11556421632 | bytes 20643840 | tf_op jit(solution)/shard_map/rf,rd->fd/dot_general | solution.py:308
  1003.2 20.2 %convolution_convert_fusion.2 = bf16[2304,2304]{1,0:T(8,128)(2,1)} fusion(bf16[1088,2304]{1,0:T(8,128)(2,1)} %multiply_convert_fusion.2, bf16[1088,2304]{1,0:T(8,128)(2,1)} %copy-done.58), kind=kOutput, calls=%fused_computation.2 | convolution fusion | flops 11556421632 | bytes 20643840 | tf_op jit(solution)/shard_map/rd,rf->df/dot_general | solution.py:313
  1023.6 20.0 %convolution_convert_fusion.1 = bf16[2304,2304]{1,0:T(8,128)(2,1)} fusion(bf16[1088,2304]{1,0:T(8,128)(2,1)} %multiply_convert_fusion.2, bf16[1088,2304]{1,0:T(8,128)(2,1)} %get-tuple-element.56), kind=kOutput, calls=%fused_computation.1 | convolution fusion | flops 11556421632 | bytes 20643840 | tf_op jit(solution)/shard_map/rd,rf->df/dot_general | solution.py:314
  1043.6 15.6 %fusion.21 = f32[1088,2304]{1,0:T(8,128)} fusion(f32[1088,2304]{1,0:T(8,128)} %get-tuple-element.58, bf16[1088,2304]{1,0:T(8,128)(2,1)} %copy-done.2, f32[1088]{0:T(1024)S(1)} %broadcast_multiply_fusion.1, f32[2304]{0:T(1024)S(1)} %copy-done.28, f32[1088]{0:T(1024)S(1)} %copy-done.43, bf16[2,1,544,2304]{3,2,1,0:T(8,128)(2,1)} %param.11), kind=kLoop, calls=%fused_computation.45 | loop fusion | flops 20054016 | bytes 30098944 | tf_op jit(solution)/shard_map/add | solution.py:394
  1059.2 2.0 convert_element_type.254
  1066.4 61.5 %reduce-scatter.14.cloned.1.call-done = bf16[2304,288]{0,1:T(8,128)(2,1)} async-done(((bf16[2304,2304]{0,1:T(8,128)(2,1)}), bf16[2304,288]{0,1:T(8,128)(2,1)}) %reduce-scatter.14.cloned.1.call-update) | async-done | bytes 1327120 | tf_op jit(solution)/shard_map/reduce_scatter | solution.py:397
  1128.0 3.0 convert_element_type.260
  1131.0 82.7 %reduce-scatter.10.cloned.1.call-done = bf16[288,2304]{1,0:T(8,128)(2,1)} async-done(((bf16[2304,2304]{1,0:T(8,128)(2,1)}), bf16[288,2304]{1,0:T(8,128)(2,1)}) %reduce-scatter.10.cloned.1.call-update) | async-done | bytes 1327120 | tf_op jit(solution)/shard_map/reduce_scatter | solution.py:397
  1213.7 3.0 convert_element_type.256
  1216.7 82.6 %reduce-scatter.12.cloned.1.call-done = bf16[288,2304]{1,0:T(8,128)(2,1)} async-done(((bf16[2304,2304]{1,0:T(8,128)(2,1)}), bf16[288,2304]{1,0:T(8,128)(2,1)}) %reduce-scatter.12.cloned.1.call-update) | async-done | bytes 1327120 | tf_op jit(solution)/shard_map/reduce_scatter | solution.py:397
  1299.3 3.0 convert_element_type.258
  (288 shorter events, 46.1 us)
Async XLA Ops:
  7.2 6.1 copy-start.57
  7.2 47.4 %all-gather.6.cloned.1.call-start = ((), (), s32[]{:S(2)}) async-start(), calls=%async_computation.5 | async-start | bytes 5971968 | tf_op jit(solution)/shard_map/all_gather | solution.py:228
  10.1 125.0 %all-gather.8.cloned.1.call-start = ((), (), s32[]{:S(2)}) async-start(), calls=%async_computation.6 | async-start | bytes 2654208 | tf_op jit(solution)/shard_map/all_gather | solution.py:233
  10.8 282.6 %all-gather.10.cloned.1.call-start = ((), (), s32[]{:S(2)}) async-start(), calls=%async_computation.7 | async-start | bytes 11943936 | tf_op jit(solution)/shard_map/all_gather | solution.py:234
  11.6 299.4 %all-gather.12.cloned.1.call-start = ((), (), s32[]{:S(2)}) async-start(), calls=%async_computation.8 | async-start | bytes 11943936 | tf_op jit(solution)/shard_map/all_gather | solution.py:235
  12.2 321.3 %all-gather.14.cloned.1.call-start = ((), (), s32[]{:S(2)}) async-start(), calls=%async_computation.9 | async-start | bytes 11943936 | tf_op jit(solution)/shard_map/all_gather | solution.py:236
  12.7 1046.5 %reduce-scatter.8.cloned.1.call-start = ((), (), s32[]{:S(2)}) async-start(), calls=%async_computation.10 | async-start | bytes 2654208 | tf_op jit(solution)/shard_map/reduce_scatter | solution.py:397
  13.2 117.3 %copy-start.38 = (s32[1088]{0:T(1024)}, s32[1088]{0:T(1024)S(1)}, u32[]{:S(2)}) copy-start(s32[1088]{0:T(1024)S(1)} %le.16) | copy-start | bytes 13060
  17.1 47.2 %copy-start.42 = (f32[1088]{0:T(1024)}, f32[1088]{0:T(1024)S(1)}, u32[]{:S(2)}) copy-start(f32[1088]{0:T(1024)S(1)} %rsqrt.41) | copy-start | bytes 13060
  18.1 112.4 %copy-start.48 = (s32[1088]{0:T(1024)}, s32[1088]{0:T(1024)S(1)}, u32[]{:S(2)}) copy-start(s32[1088]{0:T(1024)S(1)} %get-tuple-element.81) | copy-start | bytes 13060
  18.1 112.4 %copy-start.50 = (s32[1088]{0:T(1024)}, s32[1088]{0:T(1024)S(1)}, u32[]{:S(2)}) copy-start(s32[1088]{0:T(1024)S(1)} %get-tuple-element.82) | copy-start | bytes 13060
  18.1 112.4 %copy-start.44 = (s32[2112]{0:T(1024)}, s32[2112]{0:T(1024)S(1)}, u32[]{:S(2)}) copy-start(s32[2112]{0:T(1024)S(1)} %get-tuple-element.91) | copy-start | bytes 25348
  18.1 112.4 %copy-start.46 = (s32[2112]{0:T(1024)}, s32[2112]{0:T(1024)S(1)}, u32[]{:S(2)}) copy-start(s32[2112]{0:T(1024)S(1)} %get-tuple-element.92) | copy-start | bytes 25348
  55.7 8.6 slice-start.4
  58.3 222.7 %copy-start.29 = (f32[2304]{0:T(1024)}, f32[2304]{0:T(1024)S(1)}, u32[]{:S(2)}) copy-start(f32[2304]{0:T(1024)S(1)} %get-tuple-element.50) | copy-start | bytes 27652
  58.3 231.0 %copy-start.32 = (f32[2304]{0:T(1024)}, f32[2304]{0:T(1024)S(1)}, u32[]{:S(2)}) copy-start(f32[2304]{0:T(1024)S(1)} %get-tuple-element.49) | copy-start | bytes 27652
  58.3 7.3 slice-start.13
  67.1 63.5 %copy-start.36 = (bf16[2,32,256]{2,1,0:T(8,128)(2,1)}, bf16[2,32,256]{2,1,0:T(8,128)(2,1)S(1)}, u32[]{:S(2)}) copy-start(bf16[2,32,256]{2,1,0:T(8,128)(2,1)S(1)} %slice.161) | copy-start | bytes 98308
  72.8 13.4 %copy-start.7 = (f32[1088,256]{1,0:T(8,128)}, f32[1088,256]{1,0:T(8,128)S(1)}, u32[]{:S(2)}) copy-start(f32[1088,256]{1,0:T(8,128)S(1)} %get-tuple-element.78) | copy-start | bytes 3342340
  72.8 13.4 %copy-start.9 = (f32[1088,256]{1,0:T(8,128)}, f32[1088,256]{1,0:T(8,128)S(1)}, u32[]{:S(2)}) copy-start(f32[1088,256]{1,0:T(8,128)S(1)} %get-tuple-element.77) | copy-start | bytes 3342340
  72.8 43.7 %copy-start.54 = (bf16[2,32,256]{2,1,0:T(8,128)(2,1)}, bf16[2,32,256]{2,1,0:T(8,128)(2,1)S(1)}, u32[]{:S(2)}) copy-start(bf16[2,32,256]{2,1,0:T(8,128)(2,1)S(1)} %slice.160) | copy-start | bytes 98308
  79.1 33.0 %collective-permute-start = (bf16[2,512,512]{2,1,0:T(8,128)(2,1)S(1)}, bf16[2,512,512]{2,1,0:T(8,128)(2,1)S(1)}, u32[]{:S(2)}, u32[]{:S(2)}) collective-permute-start(bf16[2,512,512]{2,1,0:T(8,128)(2,1)S(1)} %pad_maximum_fusion.9), channel_id=1, source_target_pairs={{0,4},{4,0},{1,5},{5,1},{2,6},{6,2},{3,7},{7,3},{8,12},{12,8},{9,1... | collective-permute-start | bytes 3145736 | tf_op jit(solution)/shard_map/ppermute | solution.py:254
  86.8 29.7 %copy-start.23 = (bf16[1088,2,256]{2,0,1:T(8,128)(2,1)}, bf16[1088,2,256]{2,0,1:T(8,128)(2,1)S(1)}, u32[]{:S(2)}) copy-start(bf16[1088,2,256]{2,0,1:T(8,128)(2,1)S(1)} %fusion.64) | copy-start | bytes 3342340
  112.7 17.8 %copy-start.16 = (bf16[2,1024,256]{2,1,0:T(8,128)(2,1)}, bf16[2,1024,256]{2,1,0:T(8,128)(2,1)S(1)}, u32[]{:S(2)}) copy-start(bf16[2,1024,256]{2,1,0:T(8,128)(2,1)S(1)} %get-tuple-element.64) | copy-start | bytes 3145732
  116.5 14.1 %copy-start.11 = (f32[1088,2112]{1,0:T(8,128)}, f32[1088,2112]{1,0:T(8,128)S(1)}, u32[]{:S(2)}) copy-start(f32[1088,2112]{1,0:T(8,128)S(1)} %get-tuple-element.86) | copy-start | bytes 27574276
  122.2 8.3 copy-start.5
  279.9 6.3 copy-start
  481.6 10.5 copy-start.1
  481.6 10.5 slice-start.8
  482.7 9.4 slice-start.9
  492.2 30.1 %slice-start.19 = ((s8[10616832]{0:T(1024)(128)(4,1)}), s8[4194304]{0:T(1024)(128)(4,1)S(1)}, s32[]{:S(2)}) async-start(s8[10616832]{0:T(1024)(128)(4,1)} %bitcast.203), calls=%async_computation.34 | async-start | bytes 8388608
  496.5 25.8 %slice-start.20 = ((s8[10616832]{0:T(1024)(128)(4,1)}), s8[4194304]{0:T(1024)(128)(4,1)S(1)}, s32[]{:S(2)}) async-start(s8[10616832]{0:T(1024)(128)(4,1)} %bitcast.203), calls=%async_computation.35 | async-start | bytes 8388608
  496.5 25.8 %slice-start.21 = ((s8[10616832]{0:T(1024)(128)(4,1)}), s8[2228224]{0:T(1024)(128)(4,1)S(1)}, s32[]{:S(2)}) async-start(s8[10616832]{0:T(1024)(128)(4,1)} %bitcast.203), calls=%async_computation.36 | async-start | bytes 4456448
  522.2 14.8 %copy-start.58 = (bf16[1088,2304]{1,0:T(8,128)(2,1)}, bf16[1088,2304]{1,0:T(8,128)(2,1)S(1)}, u32[]{:S(2)}) copy-start(bf16[1088,2304]{1,0:T(8,128)(2,1)S(1)} %get-tuple-element.57) | copy-start | bytes 15040516
  556.8 129.0 %copy-start.33 = (f32[2304]{0:T(1024)S(1)}, f32[2304]{0:T(1024)}, u32[]{:S(2)}) copy-start(f32[2304]{0:T(1024)} %copy-done.32) | copy-start | bytes 27652
  556.8 129.0 %copy-start.41 = (f32[1088]{0:T(1024)S(1)}, f32[1088]{0:T(1024)}, u32[]{:S(2)}) copy-start(f32[1088]{0:T(1024)} %copy-done.40) | copy-start | bytes 13060
  556.8 137.3 %slice-start.2 = ((s8[5013504]{0:T(1024)(128)(4,1)}), s8[4194304]{0:T(1024)(128)(4,1)S(1)}, s32[]{:S(2)}) async-start(s8[5013504]{0:T(1024)(128)(4,1)} %bitcast.141), calls=%async_computation.17 | async-start | bytes 8388608
  685.8 8.4 slice-start.3
  685.8 23.2 %slice-start = ((s8[5013504]{0:T(1024)(128)(4,1)}), s8[4194304]{0:T(1024)(128)(4,1)S(1)}, s32[]{:S(2)}) async-start(s8[5013504]{0:T(1024)(128)(4,1)} %bitcast.139), calls=%async_computation.15 | async-start | bytes 8388608
  694.2 14.8 %slice-start.1 = ((s8[5013504]{0:T(1024)(128)(4,1)}), s8[819200]{0:T(1024)(128)(4,1)S(1)}, s32[]{:S(2)}) async-start(s8[5013504]{0:T(1024)(128)(4,1)} %bitcast.139), calls=%async_computation.16 | async-start | bytes 1638400
  694.2 14.8 %copy-start.30 = (f32[2304]{0:T(1024)S(1)}, f32[2304]{0:T(1024)}, u32[]{:S(2)}) copy-start(f32[2304]{0:T(1024)} %copy-done.29) | copy-start | bytes 27652
  694.2 14.8 %copy-start.35 = (f32[1088]{0:T(1024)S(1)}, f32[1088]{0:T(1024)}, u32[]{:S(2)}) copy-start(f32[1088]{0:T(1024)} %copy-done.34) | copy-start | bytes 13060
  715.4 8.0 copy-start.20
  736.0 9.2 copy-start.22
  736.1 9.1 copy-start.52
  736.1 19.2 %slice-start.10 = ((s8[9469952]{0:T(1024)(128)(4,1)}), s8[4194304]{0:T(1024)(128)(4,1)S(1)}, s32[]{:S(2)}) async-start(s8[9469952]{0:T(1024)(128)(4,1)} %bitcast.151), calls=%async_computation.25 | async-start | bytes 8388608
  736.1 19.2 %slice-start.11 = ((s8[9469952]{0:T(1024)(128)(4,1)}), s8[4194304]{0:T(1024)(128)(4,1)S(1)}, s32[]{:S(2)}) async-start(s8[9469952]{0:T(1024)(128)(4,1)} %bitcast.151), calls=%async_computation.26 | async-start | bytes 8388608
  745.2 8.5 copy-start.17
  745.2 8.5 copy-start.37
  745.2 10.1 slice-start.12
  767.7 15.2 %copy-start.26 = (bf16[2,1024,256]{2,1,0:T(8,128)(2,1)S(1)}, bf16[2,1024,256]{2,1,0:T(8,128)(2,1)}, u32[]{:S(2)}) copy-start(bf16[2,1024,256]{2,1,0:T(8,128)(2,1)} %copy-done.25) | copy-start | bytes 3145732
  767.7 15.2 %copy-start.55 = (bf16[2,32,256]{2,1,0:T(8,128)(2,1)S(1)}, bf16[2,32,256]{2,1,0:T(8,128)(2,1)}, u32[]{:S(2)}) copy-start(bf16[2,32,256]{2,1,0:T(8,128)(2,1)} %copy-done.54) | copy-start | bytes 98308
  795.4 265.8 %reduce-scatter.16.cloned.1.call-start = ((), (), s32[]{:S(2)}) async-start(), calls=%async_computation.14 | async-start | bytes 5971968
  798.3 19.4 %collective-permute-start.1 = (bf16[2,512,512]{2,1,0:T(8,128)(2,1)}, bf16[2,512,512]{2,1,0:T(8,128)(2,1)}, u32[]{:S(2)}, u32[]{:S(2)}) collective-permute-start(bf16[2,512,512]{2,1,0:T(8,128)(2,1)} %select_convert_fusion), channel_id=1, source_target_pairs={{0,4},{4,0},{1,5},{5,1},{2,6},{6,2},{3,7},{7,3},{8,12},{12,8},{9,1... | collective-permute-start | bytes 3145736 | tf_op jit(solution)/shard_map/ppermute | solution.py:363
  801.5 9.2 copy-start.21
  810.7 7.0 copy-start.6
  823.4 140.7 %slice-start.6 = ((s8[5013504]{0:T(1024)(128)(4,1)}), s8[4194304]{0:T(1024)(128)(4,1)S(1)}, s32[]{:S(2)}) async-start(s8[5013504]{0:T(1024)(128)(4,1)} %bitcast.145), calls=%async_computation.21 | async-start | bytes 8388608
  827.2 136.9 %slice-start.7 = ((s8[5013504]{0:T(1024)(128)(4,1)}), s8[819200]{0:T(1024)(128)(4,1)S(1)}, s32[]{:S(2)}) async-start(s8[5013504]{0:T(1024)(128)(4,1)} %bitcast.145), calls=%async_computation.22 | async-start | bytes 1638400
  838.0 126.1 %copy-start.28 = (f32[2304]{0:T(1024)S(1)}, f32[2304]{0:T(1024)}, u32[]{:S(2)}) copy-start(f32[2304]{0:T(1024)} %copy-done.27) | copy-start | bytes 27652
  838.0 126.1 %copy-start.43 = (f32[1088]{0:T(1024)S(1)}, f32[1088]{0:T(1024)}, u32[]{:S(2)}) copy-start(f32[1088]{0:T(1024)} %copy-done.42) | copy-start | bytes 13060
  838.0 130.1 %slice-start.15 = ((s8[5013504]{0:T(1024)(128)(4,1)}), s8[4194304]{0:T(1024)(128)(4,1)S(1)}, s32[]{:S(2)}) async-start(s8[5013504]{0:T(1024)(128)(4,1)} %bitcast.163), calls=%async_computation.30 | async-start | bytes 8388608
  983.1 144.9 %reduce-scatter.14.cloned.1.call-start = ((), (), s32[]{:S(2)}) async-start(), calls=%async_computation.13 | async-start | bytes 11943936 | tf_op jit(solution)/shard_map/reduce_scatter | solution.py:397
  1003.2 210.5 %reduce-scatter.10.cloned.1.call-start = ((), (), s32[]{:S(2)}) async-start(), calls=%async_computation.11 | async-start | bytes 11943936 | tf_op jit(solution)/shard_map/reduce_scatter | solution.py:397
  1023.5 275.8 %reduce-scatter.12.cloned.1.call-start = ((), (), s32[]{:S(2)}) async-start(), calls=%async_computation.12 | async-start | bytes 11943936 | tf_op jit(solution)/shard_map/reduce_scatter | solution.py:397
  (29 other events, 91.0 us)
Sparse Core Ops, SparseCore 0:
  10.5 44.0 all-gather.5
  56.5 30.9 all-gather.7
  89.3 69.4 all-gather.9
  160.6 63.7 all-gather.11
  226.1 63.7 all-gather.13
  795.5 43.3 reduce-scatter.7
  983.2 58.9 reduce-scatter.15
  1045.7 82.1 reduce-scatter.13
  1131.5 82.1 reduce-scatter.9
  1217.0 82.2 reduce-scatter.11

commit v2 on v1

--- a/solution.py
+++ b/solution.py
@@ -315,7 +315,15 @@
     ffn_part = jnp.einsum(
         "rf,df->rd", d_gate, full_gate, preferred_element_type=jnp.float32
     ) + jnp.einsum("rf,df->rd", d_up, full_up, preferred_element_type=jnp.float32)
-    d_ffn_in = chain_sum(ffn_part.astype(jnp.bfloat16), 2).astype(jnp.float32)
+    ffn_part, grad_down, grad_gate, grad_up = lax.optimization_barrier(
+        (
+            ffn_part.astype(jnp.bfloat16),
+            grad_down.astype(jnp.bfloat16),
+            grad_gate.astype(jnp.bfloat16),
+            grad_up.astype(jnp.bfloat16),
+        )
+    )
+    d_ffn_in = chain_sum(ffn_part, 2).astype(jnp.float32)
     d_mid_norm, gain_third = norm_back(middle, gain_float[2], d_ffn_in)
     d_middle = upstream + d_mid_norm
     d_attn, gain_second = norm_back(attn, gain_float[1], d_middle)
@@ -389,7 +397,15 @@
     attn_part = attn_part + jnp.einsum(
         "rc,dc->rd", d_value, full_value, preferred_element_type=jnp.float32
     )
-    d_normed = chain_sum(attn_part.astype(jnp.bfloat16), 3).astype(jnp.float32)
+    attn_part, grad_query, grad_key, grad_value = lax.optimization_barrier(
+        (
+            attn_part.astype(jnp.bfloat16),
+            grad_query.astype(jnp.bfloat16),
+            grad_key.astype(jnp.bfloat16),
+            grad_value.astype(jnp.bfloat16),
+        )
+    )
+    d_normed = chain_sum(attn_part, 3).astype(jnp.float32)
     d_in_norm, gain_first = norm_back(inputs, gain_float[0], d_normed)
     input_grad = d_middle + d_in_norm
     grad_gains = jnp.stack([gain_first, gain_second, gain_third, gain_fourth], axis=0)

time: 1320 us -> 1360 us (1.030)
  waiting for transfers between devices: 291 us -> 331 us
    unnamed x11, waiting for transfers between devices: 2.53 us -> 83.6 us
    reduce_scatter x4, waiting for transfers between devices: 227 us -> 186 us  [scatter(): lax.psum_scatter(grad.astype(jnp.bfloat16), axes, scatter_dimension=axis,...]
    unnamed x172 -> x181, local copies, waits for them, and re-layouts: 21.2 us -> 30.2 us
  transfers between devices with their start and end apart: 12 -> 12, of which waited for: 5 -> 6; matrix products, arithmetic and copies ran while one was open for 20% -> 16% of each run, Pallas kernels for 20% -> 19%
where the time goes in v2:
time: 1360 us; the launch traced here: 1350 us
  Pallas kernels  518 us (38%)
  waiting for transfers between devices  331 us (24%)
  matrix products  288 us (21%)
  other arithmetic  148 us (11%)
  local copies, waits for them, and re-layouts  49.9 us (4%)
  between operations  16 us (1%)
    pallas_call x4, Pallas kernels, chain_sum(): pl.pallas_call(functools.partial(chain_kernel, size, width), out_shape=ja...  518 us
    reduce_scatter x4, waiting for transfers between devices, scatter(): lax.psum_scatter(grad.astype(jnp.bfloat16), axes, scatter_dimension=axis,...  186 us
    unnamed x11, waiting for transfers between devices  83.6 us
    all_gather x1, waiting for transfers between devices, per_device(): full_side = lax.all_gather(side_weights, axes, axis=0, tiled=True)  36.5 us
    unnamed x181, local copies, waits for them, and re-layouts  30.2 us
    reduce_sum x4, other arithmetic, norm_back(): return (backed, jnp.sum(upstream * normed, axis=0))  27.9 us
  transfers between devices with their start and end apart: 12, of which 6 were waited for; matrix products, arithmetic and copies ran while one was open for 16% of the time, Pallas kernels for 19%

profile of v2, /device:TPU:0, one launch (start us, length us, event | category | flops | bytes accessed | tf_op | source)
XLA Modules:
  0.0 1353.8 jit_solution(3481713990137492865)
XLA Ops:
  13.4 3.5 multiply_reduce_fusion.1
  18.1 36.5 %all-gather.6.cloned.1.call-done = bf16[2304,1152]{1,0:T(8,128)(2,1)} async-done(((bf16[288,1152]{1,0:T(8,128)(2,1)}), bf16[2304,1152]{1,0:T(8,128)(2,1)}) %all-gather.6.cloned.1.call-update) | async-done | bytes 5308432 | tf_op jit(solution)/shard_map/all_gather | solution.py:228
  55.8 2.5 slice_reduce_fusion
  58.3 6.0 multiply_convert_fusion.4
  68.7 4.1 fusion.73
  74.7 4.5 copy.42
  80.4 5.6 fusion.110
  86.8 25.3 %collective-permute-done = bf16[2,512,512]{2,1,0:T(8,128)(2,1)S(1)} collective-permute-done((bf16[2,512,512]{2,1,0:T(8,128)(2,1)S(1)}, bf16[2,512,512]{2,1,0:T(8,128)(2,1)S(1)}, u32[]{:S(2)}, u32[]{:S(2)}) %collective-permute-start) | collective-permute-done | bytes 1048608 | tf_op jit(solution)/shard_map/ppermute | solution.py:254
  112.8 3.7 fusion.57
  116.5 5.6 fusion.45
  122.2 4.5 fusion.46
  126.7 3.6 fusion.62
  130.4 3.6 fusion.61
  135.9 7.2 convolution_convert_fusion.4.x_ref
  143.1 136.9 %shard_map.186 = bf16[1088,2304]{1,0:T(8,128)(2,1)S(1)} custom-call(bf16[1088,2304]{1,0:T(8,128)(2,1)} %convolution_convert_fusion.4.x_ref), custom_call_target="tpu_custom_call" | custom-call | flops 2506752 | bytes 209715200 | tf_op jit(solution)/shard_map/pallas_call | solution.py:126
  281.1 5.2 fusion.24
  290.3 3.2 multiply_convert_fusion.2
  293.5 17.5 %fusion.111 = f32[1088,2304]{1,0:T(8,128)} fusion(bf16[1088,2304]{1,0:T(8,128)(2,1)} %multiply_convert_fusion.2, bf16[2304,2304]{1,0:T(8,128)(2,1)} %all-gather.10.cloned.1.call-done), kind=kOutput, calls=%fused_computation.226 | convolution fusion | flops 11551113216 | bytes 25657344 | tf_op jit(solution)/shard_map/dot_general | solution.py:294
  311.0 22.4 %multiply_convert_fusion.1 = (bf16[1088,2304]{1,0:T(8,128)(2,1)}, f32[1088,2304]{1,0:T(8,128)}) fusion(f32[1088,2304]{1,0:T(8,128)} %fusion.111, bf16[1088,2304]{1,0:T(8,128)(2,1)} %multiply_convert_fusion.2, bf16[2304,2304]{1,0:T(8,128)(2,1)} %all-gather.12.cloned.1.call-done), kind=kOutput, calls=%fused_computation.70 | convolution fusion | flops 11576180736 | bytes 40697856 | tf_op jit(solution)/shard_map/dot_general | solution.py:295
  333.4 17.1 %convolution_convert_fusion.3.x_ref = bf16[1088,2304]{1,0:T(8,128)(2,1)} fusion(bf16[1088,2304]{1,0:T(8,128)(2,1)} %get-tuple-element.104, bf16[2304,2304]{0,1:T(8,128)(2,1)} %all-gather.14.cloned.1.call-done), kind=kOutput, calls=%fused_computation.37 | convolution fusion | flops 11553619968 | bytes 20643840 | tf_op jit(solution)/shard_map/dot_general | solution.py:301
  350.5 130.1 %shard_map.187 = bf16[1088,2304]{1,0:T(8,128)(2,1)S(1)} custom-call(bf16[1088,2304]{1,0:T(8,128)(2,1)} %convolution_convert_fusion.3.x_ref), custom_call_target="tpu_custom_call" | custom-call | flops 2506752 | bytes 209715200 | tf_op jit(solution)/shard_map/pallas_call | solution.py:126
  481.8 9.4 fusion.44
  491.2 4.3 fusion.18
  495.6 20.5 %convolution_convert_fusion.2 = bf16[2304,2304]{1,0:T(8,128)(2,1)} fusion(bf16[1088,2304]{1,0:T(8,128)(2,1)} %get-tuple-element.104, bf16[1088,2304]{1,0:T(8,128)(2,1)} %fusion.18), kind=kOutput, calls=%fused_computation.2 | convolution fusion | flops 11556421632 | bytes 20643840 | tf_op jit(solution)/shard_map/rf,rd->fd/dot_general | solution.py:308
  516.1 24.4 %multiply_convert_fusion = (bf16[1088,2304]{1,0:T(8,128)(2,1)S(1)}, bf16[1088,2304]{1,0:T(8,128)(2,1)}) fusion(f32[1088,2304]{1,0:T(8,128)} %fusion.111, f32[1088,2304]{1,0:T(8,128)} %get-tuple-element.105, bf16[1088,2304]{1,0:T(8,128)(2,1)S(1)} %copy-done.13, bf16[2304,2304]{0,1:T(8,128)(2,1)} %all-gather.14.cloned.1.call-done), kind=kOutput, calls=%fused_computation.69 | convolution fusion | flops 11611275264 | bytes 45711360 | tf_op jit(solution)/shard_map/rd,fd->rf/dot_general | solution.py:309
  542.7 17.3 %convolution_convert_fusion = bf16[2304,2304]{1,0:T(8,128)(2,1)} fusion(bf16[1088,2304]{1,0:T(8,128)(2,1)S(1)} %bitcast.163, bf16[1088,2304]{1,0:T(8,128)(2,1)S(1)} %get-tuple-element.72), kind=kOutput, calls=%fused_computation | convolution fusion | flops 11556421632 | bytes 20643840 | tf_op jit(solution)/shard_map/rd,rf->df/dot_general | solution.py:314
  560.0 19.8 %convolution_convert_fusion.1 = bf16[2304,2304]{1,0:T(8,128)(2,1)} fusion(bf16[1088,2304]{1,0:T(8,128)(2,1)} %multiply_convert_fusion.2, bf16[1088,2304]{1,0:T(8,128)(2,1)} %get-tuple-element.73), kind=kOutput, calls=%fused_computation.1 | convolution fusion | flops 11556421632 | bytes 20643840 | tf_op jit(solution)/shard_map/rd,rf->df/dot_general | solution.py:313
  579.8 17.7 %fusion.112 = f32[1088,2304]{1,0:T(8,128)} fusion(bf16[1088,2304]{1,0:T(8,128)(2,1)} %get-tuple-element.73, bf16[2304,2304]{1,0:T(8,128)(2,1)} %all-gather.10.cloned.1.call-done), kind=kOutput, calls=%fused_computation.227 | convolution fusion | flops 11551113216 | bytes 25657344 | tf_op jit(solution)/shard_map/rf,df->rd/dot_general | solution.py:315
  597.5 19.7 %fusion.14.x_ref = bf16[1088,2304]{1,0:T(8,128)(2,1)} fusion(f32[1088,2304]{1,0:T(8,128)} %fusion.112, bf16[1088,2304]{1,0:T(8,128)(2,1)} %copy-done.62, bf16[2304,2304]{1,0:T(8,128)(2,1)} %all-gather.12.cloned.1.call-done), kind=kOutput, calls=%fused_computation.35 | convolution fusion | flops 11556126720 | bytes 30670848 | tf_op jit(solution)/shard_map/rf,df->rd/dot_general | solution.py:317
  617.2 126.5 %shard_map.188 = bf16[1088,2304]{1,0:T(8,128)(2,1)S(1)} custom-call(bf16[1088,2304]{1,0:T(8,128)(2,1)} %fusion.14.x_ref), custom_call_target="tpu_custom_call" | custom-call | flops 2506752 | bytes 209715200 | tf_op jit(solution)/shard_map/pallas_call | solution.py:126
  743.7 2.3 copy-done.3
  746.0 8.3 fusion.35
  754.5 14.8 %convert_add_fusion = (f32[1088,2304]{1,0:T(8,128)}, bf16[1088,2304]{1,0:T(8,128)(2,1)}) fusion(bf16[1088,2304]{1,0:T(8,128)(2,1)} %copy-done.3, f32[1088,2304]{1,0:T(8,128)} %copy-done.4, f32[1088]{0:T(1024)S(1)} %broadcast_multiply_fusion.3, f32[2304]{0:T(1024)S(1)} %copy-done.35, f32[1088]{0:T(1024)S(1)} %copy-done.43, ...), kind=kLoop, calls=%fused_computation.4 | loop fusion | flops 32587776 | bytes 40139520 | tf_op jit(solution)/shard_map/add | solution.py:328
  769.3 6.3 fusion.29
  775.7 5.8 fusion.28
  781.4 2.3 copy-done.14
  783.7 4.5 convolution_convert_fusion.5
  788.2 5.9 convolution_convert_fusion.9
  796.5 9.1 fusion.48
  805.6 8.3 fusion.54
  815.7 12.4 multiply_reduce_fusion.3
  828.1 15.1 %multiply_convert_fusion.6 = (bf16[1088,2112]{1,0:T(8,128)(2,1)}, bf16[1088,2112]{1,0:T(8,128)(2,1)S(1)}) fusion(f32[1088,2112]{1,0:T(8,128)} %copy-done.11, f32[1088,2112]{1,0:T(8,128)} %get-tuple-element.106, f32[1088]{0:T(1024)S(1)} %get-tuple-element.68, f32[1088]{0:T(1024)S(1)} %copy-done.56, s32[1088]{0:T(1024)S(1)} %copy-done.41, ...), kind=kLoop, calls=%fused_computation.79 | loop fusion | flops 62042112 | bytes 46004480 | tf_op jit(solution)/shard_map/convert_element_type | solution.py:348
  843.3 5.0 convolution_bitcast_fusion.1
  850.0 2.5 convolution_bitcast_fusion
  855.8 2.9 select_convert_fusion
  862.2 5.4 fusion.66
  867.6 7.1 convolution_convert_fusion.6
  877.1 3.7 fusion.80
  880.9 3.9 fusion.79
  884.8 2.9 convolution_convert_fusion.8
  887.7 2.8 convolution_add_fusion.1
  890.6 5.2 fusion.15.x_ref
  895.8 2.8 convolution_convert_fusion.7
  898.6 124.9 %shard_map.189 = bf16[1088,2304]{1,0:T(8,128)(2,1)S(1)} custom-call(bf16[1088,2304]{1,0:T(8,128)(2,1)} %fusion.15.x_ref), custom_call_target="tpu_custom_call" | custom-call | flops 2506752 | bytes 209715200 | tf_op jit(solution)/shard_map/pallas_call | solution.py:126
  1023.6 3.9 fusion.36
  1027.9 4.3 fusion.47
  1032.3 15.7 %copy.52 = bf16[2304,2304]{0,1:T(8,128)(2,1)} copy(bf16[2304,2304]{1,0:T(8,128)(2,1)} %convolution_convert_fusion.2) | data formatting | bytes 21233664
  1049.3 14.3 %fusion.21 = f32[1088,2304]{1,0:T(8,128)} fusion(f32[1088,2304]{1,0:T(8,128)} %get-tuple-element.74, bf16[1088,2304]{1,0:T(8,128)(2,1)} %copy-done.2, f32[1088]{0:T(1024)S(1)} %broadcast_multiply_fusion.1, f32[2304]{0:T(1024)S(1)} %copy-done.29, f32[1088]{0:T(1024)S(1)} %copy-done.45, bf16[2,1,544,2304]{3,2,1,0:T(8,128)(2,1)} %param.11), kind=kLoop, calls=%fused_computation.45 | loop fusion | flops 20054016 | bytes 30098944 | tf_op jit(solution)/shard_map/add | solution.py:410
  1065.5 21.1 %reduce-scatter.8.cloned.1.call-done = bf16[288,1152]{1,0:T(8,128)(2,1)} async-done(((bf16[2304,1152]{1,0:T(8,128)(2,1)}), bf16[288,1152]{1,0:T(8,128)(2,1)}) %reduce-scatter.8.cloned.1.call-update) | async-done | bytes 663568 | tf_op jit(solution)/shard_map/reduce_scatter | solution.py:413
  1092.2 80.2 %reduce-scatter.16.cloned.1.call-done = bf16[288,2304]{1,0:T(8,128)(2,1)} async-done(((bf16[2304,2304]{1,0:T(8,128)(2,1)}), bf16[288,2304]{1,0:T(8,128)(2,1)}) %reduce-scatter.16.cloned.1.call-update) | async-done | bytes 1327120
  1176.2 81.9 %reduce-scatter.14.cloned.1.call-done = bf16[288,2304]{1,0:T(8,128)(2,1)} async-done(((bf16[2304,2304]{1,0:T(8,128)(2,1)}), bf16[288,2304]{1,0:T(8,128)(2,1)}) %reduce-scatter.14.cloned.1.call-update) | async-done | bytes 1327120 | tf_op jit(solution)/shard_map/reduce_scatter | solution.py:413
  1258.1 3.0 convert_element_type.274
  1261.1 82.6 %reduce-scatter.12.cloned.1.call-done = bf16[288,2304]{1,0:T(8,128)(2,1)} async-done(((bf16[2304,2304]{1,0:T(8,128)(2,1)}), bf16[288,2304]{1,0:T(8,128)(2,1)}) %reduce-scatter.12.cloned.1.call-update) | async-done | bytes 1327120 | tf_op jit(solution)/shard_map/reduce_scatter | solution.py:413
  1343.7 3.0 convert_element_type.273
  (298 shorter events, 54.9 us)
Async XLA Ops:
  7.2 47.4 %all-gather.6.cloned.1.call-start = ((), (), s32[]{:S(2)}) async-start(), calls=%async_computation.5 | async-start | bytes 5971968 | tf_op jit(solution)/shard_map/all_gather | solution.py:228
  10.1 124.8 %all-gather.8.cloned.1.call-start = ((), (), s32[]{:S(2)}) async-start(), calls=%async_computation.6 | async-start | bytes 2654208 | tf_op jit(solution)/shard_map/all_gather | solution.py:233
  10.8 282.6 %all-gather.10.cloned.1.call-start = ((), (), s32[]{:S(2)}) async-start(), calls=%async_computation.7 | async-start | bytes 11943936 | tf_op jit(solution)/shard_map/all_gather | solution.py:234
  11.6 299.4 %all-gather.12.cloned.1.call-start = ((), (), s32[]{:S(2)}) async-start(), calls=%async_computation.8 | async-start | bytes 11943936 | tf_op jit(solution)/shard_map/all_gather | solution.py:235
  12.2 321.2 %all-gather.14.cloned.1.call-start = ((), (), s32[]{:S(2)}) async-start(), calls=%async_computation.9 | async-start | bytes 11943936 | tf_op jit(solution)/shard_map/all_gather | solution.py:236
  12.7 1050.9 %reduce-scatter.10.cloned.1.call-start = ((), (), s32[]{:S(2)}) async-start(), calls=%async_computation.11 | async-start | bytes 2654208 | tf_op jit(solution)/shard_map/reduce_scatter | solution.py:413
  13.2 117.1 %copy-start.40 = (s32[1088]{0:T(1024)}, s32[1088]{0:T(1024)S(1)}, u32[]{:S(2)}) copy-start(s32[1088]{0:T(1024)S(1)} %le.16) | copy-start | bytes 13060
  17.1 47.3 %copy-start.44 = (f32[1088]{0:T(1024)}, f32[1088]{0:T(1024)S(1)}, u32[]{:S(2)}) copy-start(f32[1088]{0:T(1024)S(1)} %rsqrt.41) | copy-start | bytes 13060
  18.1 112.2 %copy-start.52 = (s32[1088]{0:T(1024)}, s32[1088]{0:T(1024)S(1)}, u32[]{:S(2)}) copy-start(s32[1088]{0:T(1024)S(1)} %get-tuple-element.97) | copy-start | bytes 13060
  18.1 112.3 %copy-start.54 = (s32[1088]{0:T(1024)}, s32[1088]{0:T(1024)S(1)}, u32[]{:S(2)}) copy-start(s32[1088]{0:T(1024)S(1)} %get-tuple-element.98) | copy-start | bytes 13060
  18.1 112.2 %copy-start.48 = (s32[2112]{0:T(1024)}, s32[2112]{0:T(1024)S(1)}, u32[]{:S(2)}) copy-start(s32[2112]{0:T(1024)S(1)} %get-tuple-element.107) | copy-start | bytes 25348
  18.1 112.2 %copy-start.50 = (s32[2112]{0:T(1024)}, s32[2112]{0:T(1024)S(1)}, u32[]{:S(2)}) copy-start(s32[2112]{0:T(1024)S(1)} %get-tuple-element.108) | copy-start | bytes 25348
  55.7 8.6 slice-start.4
  58.3 222.8 %copy-start.30 = (f32[2304]{0:T(1024)}, f32[2304]{0:T(1024)S(1)}, u32[]{:S(2)}) copy-start(f32[2304]{0:T(1024)S(1)} %get-tuple-element.66) | copy-start | bytes 27652
  58.3 231.1 %copy-start.34 = (f32[2304]{0:T(1024)}, f32[2304]{0:T(1024)S(1)}, u32[]{:S(2)}) copy-start(f32[2304]{0:T(1024)S(1)} %get-tuple-element.65) | copy-start | bytes 27652
  67.1 63.3 %copy-start.38 = (bf16[2,32,256]{2,1,0:T(8,128)(2,1)}, bf16[2,32,256]{2,1,0:T(8,128)(2,1)S(1)}, u32[]{:S(2)}) copy-start(bf16[2,32,256]{2,1,0:T(8,128)(2,1)S(1)} %slice.161) | copy-start | bytes 98308
  72.9 13.4 copy-start.7
  72.9 13.4 copy-start.9
  72.9 43.6 %copy-start.58 = (bf16[2,32,256]{2,1,0:T(8,128)(2,1)}, bf16[2,32,256]{2,1,0:T(8,128)(2,1)S(1)}, u32[]{:S(2)}) copy-start(bf16[2,32,256]{2,1,0:T(8,128)(2,1)S(1)} %slice.160) | copy-start | bytes 98308
  79.3 32.8 %collective-permute-start = (bf16[2,512,512]{2,1,0:T(8,128)(2,1)S(1)}, bf16[2,512,512]{2,1,0:T(8,128)(2,1)S(1)}, u32[]{:S(2)}, u32[]{:S(2)}) collective-permute-start(bf16[2,512,512]{2,1,0:T(8,128)(2,1)S(1)} %pad_maximum_fusion.9), channel_id=1, source_target_pairs={{0,4},{4,0},{1,5},{5,1},{2,6},{6,2},{3,7},{7,3},{8,12},{12,8},{9,1... | collective-permute-start | bytes 3145736 | tf_op jit(solution)/shard_map/ppermute | solution.py:254
  86.8 29.7 %copy-start.24 = (bf16[1088,2,256]{2,0,1:T(8,128)(2,1)}, bf16[1088,2,256]{2,0,1:T(8,128)(2,1)S(1)}, u32[]{:S(2)}) copy-start(bf16[1088,2,256]{2,0,1:T(8,128)(2,1)S(1)} %fusion.64) | copy-start | bytes 3342340
  112.7 17.6 %copy-start.17 = (bf16[2,1024,256]{2,1,0:T(8,128)(2,1)}, bf16[2,1024,256]{2,1,0:T(8,128)(2,1)S(1)}, u32[]{:S(2)}) copy-start(bf16[2,1024,256]{2,1,0:T(8,128)(2,1)S(1)} %get-tuple-element.80) | copy-start | bytes 3145732
  116.5 13.9 %copy-start.11 = (f32[1088,2112]{1,0:T(8,128)}, f32[1088,2112]{1,0:T(8,128)S(1)}, u32[]{:S(2)}) copy-start(f32[1088,2112]{1,0:T(8,128)S(1)} %get-tuple-element.102) | copy-start | bytes 27574276
  122.2 8.2 copy-start.5
  480.6 10.6 copy-start.1
  480.7 10.5 slice-start.8
  481.8 9.5 copy-start.46
  481.8 9.4 slice-start.9
  495.6 20.5 %copy-start.13 = (bf16[1088,2304]{1,0:T(8,128)(2,1)S(1)}, bf16[1088,2304]{1,0:T(8,128)(2,1)}, u32[]{:S(2)}) copy-start(bf16[1088,2304]{1,0:T(8,128)(2,1)} %fusion.18) | copy-start | bytes 15040516
  495.6 47.1 %slice-start.15 = ((s8[5013504]{0:T(1024)(128)(4,1)}), s8[4194304]{0:T(1024)(128)(4,1)S(1)}, s32[]{:S(2)}) async-start(s8[5013504]{0:T(1024)(128)(4,1)} %bitcast.162), calls=%async_computation.30 | async-start | bytes 8388608
  516.1 26.6 %slice-start.16 = ((s8[5013504]{0:T(1024)(128)(4,1)}), s8[819200]{0:T(1024)(128)(4,1)S(1)}, s32[]{:S(2)}) async-start(s8[5013504]{0:T(1024)(128)(4,1)} %bitcast.162), calls=%async_computation.31 | async-start | bytes 1638400
  617.2 128.8 %copy-start.35 = (f32[2304]{0:T(1024)S(1)}, f32[2304]{0:T(1024)}, u32[]{:S(2)}) copy-start(f32[2304]{0:T(1024)} %copy-done.34) | copy-start | bytes 27652
  617.2 128.8 %copy-start.43 = (f32[1088]{0:T(1024)S(1)}, f32[1088]{0:T(1024)}, u32[]{:S(2)}) copy-start(f32[1088]{0:T(1024)} %copy-done.42) | copy-start | bytes 13060
  617.2 137.2 %slice-start.2 = ((s8[5013504]{0:T(1024)(128)(4,1)}), s8[4194304]{0:T(1024)(128)(4,1)S(1)}, s32[]{:S(2)}) async-start(s8[5013504]{0:T(1024)(128)(4,1)} %bitcast.141), calls=%async_computation.17 | async-start | bytes 8388608
  746.0 8.4 slice-start.3
  746.0 8.4 copy-start.33
  746.0 8.4 copy-start.47
  746.0 23.2 %slice-start = ((s8[5013504]{0:T(1024)(128)(4,1)}), s8[4194304]{0:T(1024)(128)(4,1)S(1)}, s32[]{:S(2)}) async-start(s8[5013504]{0:T(1024)(128)(4,1)} %bitcast.139), calls=%async_computation.15 | async-start | bytes 8388608
  754.4 14.8 %slice-start.1 = ((s8[5013504]{0:T(1024)(128)(4,1)}), s8[819200]{0:T(1024)(128)(4,1)S(1)}, s32[]{:S(2)}) async-start(s8[5013504]{0:T(1024)(128)(4,1)} %bitcast.139), calls=%async_computation.16 | async-start | bytes 1638400
  754.4 14.8 %copy-start.31 = (f32[2304]{0:T(1024)S(1)}, f32[2304]{0:T(1024)}, u32[]{:S(2)}) copy-start(f32[2304]{0:T(1024)} %copy-done.30) | copy-start | bytes 27652
  754.5 14.8 %copy-start.37 = (f32[1088]{0:T(1024)S(1)}, f32[1088]{0:T(1024)}, u32[]{:S(2)}) copy-start(f32[1088]{0:T(1024)} %copy-done.36) | copy-start | bytes 13060
  775.7 8.1 copy-start.21
  796.4 9.2 copy-start.23
  796.4 9.1 copy-start.56
  796.4 19.2 %slice-start.10 = ((s8[9469952]{0:T(1024)(128)(4,1)}), s8[4194304]{0:T(1024)(128)(4,1)S(1)}, s32[]{:S(2)}) async-start(s8[9469952]{0:T(1024)(128)(4,1)} %bitcast.152), calls=%async_computation.25 | async-start | bytes 8388608
  796.5 19.2 %slice-start.11 = ((s8[9469952]{0:T(1024)(128)(4,1)}), s8[4194304]{0:T(1024)(128)(4,1)S(1)}, s32[]{:S(2)}) async-start(s8[9469952]{0:T(1024)(128)(4,1)} %bitcast.152), calls=%async_computation.26 | async-start | bytes 8388608
  805.6 8.5 copy-start.18
  805.6 8.5 copy-start.39
  805.6 10.1 slice-start.12
  828.1 15.2 %copy-start.27 = (bf16[2,1024,256]{2,1,0:T(8,128)(2,1)S(1)}, bf16[2,1024,256]{2,1,0:T(8,128)(2,1)}, u32[]{:S(2)}) copy-start(bf16[2,1024,256]{2,1,0:T(8,128)(2,1)} %copy-done.26) | copy-start | bytes 3145732
  828.1 15.2 %copy-start.59 = (bf16[2,32,256]{2,1,0:T(8,128)(2,1)S(1)}, bf16[2,32,256]{2,1,0:T(8,128)(2,1)}, u32[]{:S(2)}) copy-start(bf16[2,32,256]{2,1,0:T(8,128)(2,1)} %copy-done.58) | copy-start | bytes 98308
  855.7 230.9 %reduce-scatter.8.cloned.1.call-start = ((), (), s32[]{:S(2)}) async-start(), calls=%async_computation.10 | async-start | bytes 5971968 | tf_op jit(solution)/shard_map/reduce_scatter | solution.py:413
  858.7 16.1 %collective-permute-start.1 = (bf16[2,512,512]{2,1,0:T(8,128)(2,1)}, bf16[2,512,512]{2,1,0:T(8,128)(2,1)}, u32[]{:S(2)}, u32[]{:S(2)}) collective-permute-start(bf16[2,512,512]{2,1,0:T(8,128)(2,1)} %select_convert_fusion), channel_id=1, source_target_pairs={{0,4},{4,0},{1,5},{5,1},{2,6},{6,2},{3,7},{7,3},{8,12},{12,8},{9,1... | collective-permute-start | bytes 3145736 | tf_op jit(solution)/shard_map/ppermute | solution.py:371
  876.9 7.9 slice-start.17
  877.1 7.7 slice-start.18
  884.8 11.0 slice-start.19
  887.7 8.1 slice-start.20
  890.6 132.9 %slice-start.6 = ((s8[5013504]{0:T(1024)(128)(4,1)}), s8[4194304]{0:T(1024)(128)(4,1)S(1)}, s32[]{:S(2)}) async-start(s8[5013504]{0:T(1024)(128)(4,1)} %bitcast.145), calls=%async_computation.21 | async-start | bytes 8388608
  895.8 127.7 %slice-start.7 = ((s8[5013504]{0:T(1024)(128)(4,1)}), s8[819200]{0:T(1024)(128)(4,1)S(1)}, s32[]{:S(2)}) async-start(s8[5013504]{0:T(1024)(128)(4,1)} %bitcast.145), calls=%async_computation.22 | async-start | bytes 1638400
  898.6 124.9 %copy-start.29 = (f32[2304]{0:T(1024)S(1)}, f32[2304]{0:T(1024)}, u32[]{:S(2)}) copy-start(f32[2304]{0:T(1024)} %copy-done.28) | copy-start | bytes 27652
  898.6 124.9 %copy-start.45 = (f32[1088]{0:T(1024)S(1)}, f32[1088]{0:T(1024)}, u32[]{:S(2)}) copy-start(f32[1088]{0:T(1024)} %copy-done.44) | copy-start | bytes 13060
  1032.2 140.1 %reduce-scatter.16.cloned.1.call-start = ((), (), s32[]{:S(2)}) async-start(), calls=%async_computation.14 | async-start | bytes 11943936
  1048.0 210.1 %reduce-scatter.14.cloned.1.call-start = ((), (), s32[]{:S(2)}) async-start(), calls=%async_computation.13 | async-start | bytes 11943936 | tf_op jit(solution)/shard_map/reduce_scatter | solution.py:413
  1048.7 294.9 %reduce-scatter.12.cloned.1.call-start = ((), (), s32[]{:S(2)}) async-start(), calls=%async_computation.12 | async-start | bytes 11943936 | tf_op jit(solution)/shard_map/reduce_scatter | solution.py:413
  (34 other events, 128.0 us)
Sparse Core Ops, SparseCore 0:
  10.5 44.0 all-gather.5
  56.5 30.7 all-gather.7
  89.2 69.5 all-gather.9
  160.6 63.7 all-gather.11
  226.1 63.7 all-gather.13
  855.8 40.9 reduce-scatter.9
  1032.3 54.2 reduce-scatter.7
  1090.1 82.2 reduce-scatter.15
  1175.8 82.2 reduce-scatter.13
  1261.5 82.1 reduce-scatter.11

commit v3 on v2

--- a/solution.py
+++ b/solution.py
@@ -323,7 +323,16 @@
             grad_up.astype(jnp.bfloat16),
         )
     )
-    d_ffn_in = chain_sum(ffn_part, 2).astype(jnp.float32)
+    def scatter(grad, axis):
+        return lax.psum_scatter(
+            grad.astype(jnp.bfloat16), axes, scatter_dimension=axis, tiled=True
+        ).astype(jnp.float32)
+
+    d_ffn_in = chain_sum(ffn_part, 2)
+    share_down = scatter(grad_down, 1)
+    d_ffn_in, share_down = lax.optimization_barrier((d_ffn_in, share_down))
+    d_ffn_in = d_ffn_in.astype(jnp.float32)
+    share_gate = scatter(grad_gate, 0)
     d_mid_norm, gain_third = norm_back(middle, gain_float[2], d_ffn_in)
     d_middle = upstream + d_mid_norm
     d_attn, gain_second = norm_back(attn, gain_float[1], d_middle)
@@ -397,23 +406,23 @@
     attn_part = attn_part + jnp.einsum(
         "rc,dc->rd", d_value, full_value, preferred_element_type=jnp.float32
     )
-    attn_part, grad_query, grad_key, grad_value = lax.optimization_barrier(
+    share_up = scatter(grad_up, 0)
+    share_out = scatter(grad_out, 1)
+    attn_part, share_gate, grad_query, grad_key, grad_value = lax.optimization_barrier(
         (
             attn_part.astype(jnp.bfloat16),
+            share_gate,
             grad_query.astype(jnp.bfloat16),
             grad_key.astype(jnp.bfloat16),
             grad_value.astype(jnp.bfloat16),
         )
     )
-    d_normed = chain_sum(attn_part, 3).astype(jnp.float32)
+    d_normed = chain_sum(attn_part, 3)
+    d_normed, share_up = lax.optimization_barrier((d_normed, share_up))
+    d_normed = d_normed.astype(jnp.float32)
     d_in_norm, gain_first = norm_back(inputs, gain_float[0], d_normed)
     input_grad = d_middle + d_in_norm
     grad_gains = jnp.stack([gain_first, gain_second, gain_third, gain_fourth], axis=0)
-    def scatter(grad, axis):
-        return lax.psum_scatter(
-            grad.astype(jnp.bfloat16), axes, scatter_dimension=axis, tiled=True
-        ).astype(jnp.float32)
-
     side_grad = scatter(
         jnp.concatenate(
             [
@@ -430,10 +439,10 @@
         side_grad[:, :query_width],
         side_grad[:, query_width : query_width + HEAD],
         side_grad[:, query_width + HEAD : query_width + 2 * HEAD],
-        scatter(grad_out, 1),
-        scatter(grad_gate, 0),
-        scatter(grad_up, 0),
-        scatter(grad_down, 1),
+        share_out,
+        share_gate,
+        share_up,
+        share_down,
         side_grad[:, query_width + 2 * HEAD : query_width + 2 * HEAD + 4].T,
     )
     return (

time: 1360 us -> 1160 us (0.85)
  waiting for transfers between devices: 331 us -> 107 us
  Pallas kernels: 518 us -> 532 us
    reduce_scatter x4, waiting for transfers between devices: 186 us -> 41.8 us  [scatter(): lax.psum_scatter(grad.astype(jnp.bfloat16), axes, scatter_dimension=axis,...]
    unnamed x11, waiting for transfers between devices: 83.6 us -> 3.23 us
    unnamed x181 -> x197, local copies, waits for them, and re-layouts: 30.2 us -> 34.5 us
  transfers between devices with their start and end apart: 12 -> 12, of which waited for: 6 -> 4; matrix products, arithmetic and copies ran while one was open for 16% -> 26% of each run, Pallas kernels for 19% -> 35%
where the time goes in v3:
time: 1160 us; the launch traced here: 1150 us
  Pallas kernels  532 us (46%)
  matrix products  288 us (25%)
  other arithmetic  149 us (13%)
  waiting for transfers between devices  107 us (9%)
  local copies, waits for them, and re-layouts  53.2 us (5%)
  between operations  16.4 us (1%)
    pallas_call x4, Pallas kernels, chain_sum(): pl.pallas_call(functools.partial(chain_kernel, size, width), out_shape=ja...  532 us
    reduce_scatter x4, waiting for transfers between devices, scatter(): lax.psum_scatter(grad.astype(jnp.bfloat16), axes, scatter_dimension=axis,...  41.8 us
    all_gather x1, waiting for transfers between devices, per_device(): full_side = lax.all_gather(side_weights, axes, axis=0, tiled=True)  36.5 us
    unnamed x197, local copies, waits for them, and re-layouts  34.5 us
    reduce_sum x4, other arithmetic, norm_back(): return (backed, jnp.sum(upstream * normed, axis=0))  29.1 us
    ppermute x1, waiting for transfers between devices, per_device(): other_pair = lax.ppermute(own_pair, 'seq', [(0, 1), (1, 0)])  25.3 us
    dot_general x1, matrix products, per_device(): jnp.einsum('rd,fd->rf', d_ffn, full_down, preferred_element_type=jnp.floa...  24.4 us
  transfers between devices with their start and end apart: 12, of which 4 were waited for; matrix products, arithmetic and copies ran while one was open for 26% of the time, Pallas kernels for 35%

profile of v3, /device:TPU:0, one launch (start us, length us, event | category | flops | bytes accessed | tf_op | source)
XLA Modules:
  0.0 1147.5 jit_solution(17059014134728941766)
XLA Ops:
  13.4 3.5 multiply_reduce_fusion.1
  18.1 36.5 %all-gather.6.cloned.1.call-done = bf16[2304,1152]{1,0:T(8,128)(2,1)} async-done(((bf16[288,1152]{1,0:T(8,128)(2,1)}), bf16[2304,1152]{1,0:T(8,128)(2,1)}) %all-gather.6.cloned.1.call-update) | async-done | bytes 5308432 | tf_op jit(solution)/shard_map/all_gather | solution.py:228
  55.8 2.5 slice_reduce_fusion
  58.3 6.0 multiply_convert_fusion.4
  68.7 4.1 fusion.73
  74.7 4.5 copy.42
  80.4 5.6 fusion.110
  86.8 25.3 %collective-permute-done = bf16[2,512,512]{2,1,0:T(8,128)(2,1)S(1)} collective-permute-done((bf16[2,512,512]{2,1,0:T(8,128)(2,1)S(1)}, bf16[2,512,512]{2,1,0:T(8,128)(2,1)S(1)}, u32[]{:S(2)}, u32[]{:S(2)}) %collective-permute-start) | collective-permute-done | bytes 1048608 | tf_op jit(solution)/shard_map/ppermute | solution.py:254
  112.8 3.7 fusion.57
  116.6 5.6 fusion.45
  122.2 4.5 fusion.46
  126.8 3.6 fusion.62
  130.5 3.6 fusion.61
  135.0 7.6 convolution_convert_fusion.4.x_ref
  142.6 138.2 %shard_map.186 = bf16[1088,2304]{1,0:T(8,128)(2,1)S(1)} custom-call(bf16[1088,2304]{1,0:T(8,128)(2,1)} %convolution_convert_fusion.4.x_ref), custom_call_target="tpu_custom_call" | custom-call | flops 2506752 | bytes 209715200 | tf_op jit(solution)/shard_map/pallas_call | solution.py:126
  281.9 5.4 fusion.24
  288.1 3.0 copy-done.4
  291.1 3.2 multiply_convert_fusion.2
  294.3 17.5 %fusion.111 = f32[1088,2304]{1,0:T(8,128)} fusion(bf16[1088,2304]{1,0:T(8,128)(2,1)} %multiply_convert_fusion.2, bf16[2304,2304]{1,0:T(8,128)(2,1)} %all-gather.10.cloned.1.call-done), kind=kOutput, calls=%fused_computation.226 | convolution fusion | flops 11551113216 | bytes 25657344 | tf_op jit(solution)/shard_map/dot_general | solution.py:294
  311.8 22.4 %multiply_convert_fusion.1 = (bf16[1088,2304]{1,0:T(8,128)(2,1)}, f32[1088,2304]{1,0:T(8,128)}) fusion(f32[1088,2304]{1,0:T(8,128)} %fusion.111, bf16[1088,2304]{1,0:T(8,128)(2,1)} %multiply_convert_fusion.2, bf16[2304,2304]{1,0:T(8,128)(2,1)} %all-gather.12.cloned.1.call-done), kind=kOutput, calls=%fused_computation.70 | convolution fusion | flops 11576180736 | bytes 40697856 | tf_op jit(solution)/shard_map/dot_general | solution.py:295
  334.2 17.1 %convolution_convert_fusion.3.x_ref = bf16[1088,2304]{1,0:T(8,128)(2,1)} fusion(bf16[1088,2304]{1,0:T(8,128)(2,1)} %get-tuple-element.114, bf16[2304,2304]{0,1:T(8,128)(2,1)} %all-gather.14.cloned.1.call-done), kind=kOutput, calls=%fused_computation.37 | convolution fusion | flops 11553619968 | bytes 20643840 | tf_op jit(solution)/shard_map/dot_general | solution.py:301
  351.4 131.0 %shard_map.187 = bf16[1088,2304]{1,0:T(8,128)(2,1)S(1)} custom-call(bf16[1088,2304]{1,0:T(8,128)(2,1)} %convolution_convert_fusion.3.x_ref), custom_call_target="tpu_custom_call" | custom-call | flops 2506752 | bytes 209715200 | tf_op jit(solution)/shard_map/pallas_call | solution.py:126
  483.5 9.4 fusion.44
  492.9 4.3 fusion.18
  497.3 20.6 %convolution_convert_fusion.2 = bf16[2304,2304]{1,0:T(8,128)(2,1)} fusion(bf16[1088,2304]{1,0:T(8,128)(2,1)} %get-tuple-element.114, bf16[1088,2304]{1,0:T(8,128)(2,1)} %fusion.18), kind=kOutput, calls=%fused_computation.2 | convolution fusion | flops 11556421632 | bytes 20643840 | tf_op jit(solution)/shard_map/rf,rd->fd/dot_general | solution.py:308
  517.9 24.4 %multiply_convert_fusion = (bf16[1088,2304]{1,0:T(8,128)(2,1)S(1)}, bf16[1088,2304]{1,0:T(8,128)(2,1)}) fusion(f32[1088,2304]{1,0:T(8,128)} %fusion.111, f32[1088,2304]{1,0:T(8,128)} %get-tuple-element.115, bf16[1088,2304]{1,0:T(8,128)(2,1)S(1)} %copy-done.16, bf16[2304,2304]{0,1:T(8,128)(2,1)} %all-gather.14.cloned.1.call-done), kind=kOutput, calls=%fused_computation.69 | convolution fusion | flops 11611275264 | bytes 45711360 | tf_op jit(solution)/shard_map/rd,fd->rf/dot_general | solution.py:309
  542.3 2.2 copy-done.70
  544.5 17.3 %convolution_convert_fusion = bf16[2304,2304]{1,0:T(8,128)(2,1)} fusion(bf16[1088,2304]{1,0:T(8,128)(2,1)S(1)} %bitcast.163, bf16[1088,2304]{1,0:T(8,128)(2,1)S(1)} %get-tuple-element.82), kind=kOutput, calls=%fused_computation | convolution fusion | flops 11556421632 | bytes 20643840 | tf_op jit(solution)/shard_map/rd,rf->df/dot_general | solution.py:314
  561.8 19.8 %convolution_convert_fusion.1 = bf16[2304,2304]{1,0:T(8,128)(2,1)} fusion(bf16[1088,2304]{1,0:T(8,128)(2,1)} %multiply_convert_fusion.2, bf16[1088,2304]{1,0:T(8,128)(2,1)} %get-tuple-element.83), kind=kOutput, calls=%fused_computation.1 | convolution fusion | flops 11556421632 | bytes 20643840 | tf_op jit(solution)/shard_map/rd,rf->df/dot_general | solution.py:313
  581.6 17.7 %fusion.112 = f32[1088,2304]{1,0:T(8,128)} fusion(bf16[1088,2304]{1,0:T(8,128)(2,1)} %get-tuple-element.83, bf16[2304,2304]{1,0:T(8,128)(2,1)} %all-gather.10.cloned.1.call-done), kind=kOutput, calls=%fused_computation.227 | convolution fusion | flops 11551113216 | bytes 25657344 | tf_op jit(solution)/shard_map/rf,df->rd/dot_general | solution.py:315
  599.3 19.7 %fusion.14.x_ref = bf16[1088,2304]{1,0:T(8,128)(2,1)} fusion(f32[1088,2304]{1,0:T(8,128)} %fusion.112, bf16[1088,2304]{1,0:T(8,128)(2,1)} %copy-done.70, bf16[2304,2304]{1,0:T(8,128)(2,1)} %all-gather.12.cloned.1.call-done), kind=kOutput, calls=%fused_computation.35 | convolution fusion | flops 11556126720 | bytes 30670848 | tf_op jit(solution)/shard_map/rf,df->rd/dot_general | solution.py:317
  619.1 14.6 %copy.52 = bf16[2304,2304]{0,1:T(8,128)(2,1)} copy(bf16[2304,2304]{1,0:T(8,128)(2,1)} %convolution_convert_fusion.2) | data formatting | bytes 21233664
  635.2 126.5 %shard_map.188 = bf16[1088,2304]{1,0:T(8,128)(2,1)S(1)} custom-call(bf16[1088,2304]{1,0:T(8,128)(2,1)} %fusion.14.x_ref), custom_call_target="tpu_custom_call" | custom-call | flops 2506752 | bytes 209715200 | tf_op jit(solution)/shard_map/pallas_call | solution.py:126
  761.7 2.3 copy-done.3
  764.1 2.1 copy.53
  768.4 8.8 fusion.35
  777.2 15.5 %convert_add_fusion = (f32[1088,2304]{1,0:T(8,128)}, bf16[1088,2304]{1,0:T(8,128)(2,1)}) fusion(bf16[1088,2304]{1,0:T(8,128)(2,1)} %copy-done.3, f32[1088,2304]{1,0:T(8,128)} %copy-done.4, f32[1088]{0:T(1024)S(1)} %broadcast_multiply_fusion.3, f32[2304]{0:T(1024)S(1)} %copy-done.35, f32[1088]{0:T(1024)S(1)} %copy-done.43, ...), kind=kLoop, calls=%fused_computation.4 | loop fusion | flops 32587776 | bytes 40139520 | tf_op jit(solution)/shard_map/add | solution.py:337
  792.7 6.4 fusion.29
  799.2 5.8 fusion.28
  805.0 2.5 copy-done.15
  807.6 2.8 convolution_convert_fusion.9
  812.4 11.2 fusion.48
  823.6 8.6 fusion.54
  833.9 12.7 %multiply_reduce_fusion.3 = (f32[1088]{0:T(1024)S(1)}, f32[1088]{0:T(1024)S(1)}, f32[1088,2112]{1,0:T(8,128)}) fusion(f32[1088]{0:T(1024)S(1)} %log_add_fusion.1, f32[1088,2112]{1,0:T(8,128)} %copy-done.13, s32[1088]{0:T(1024)S(1)} %copy-done.41, s32[2112]{0:T(1024)S(1)} %copy-done.51, s32[1088]{0:T(1024)S(1)} %copy-done.55, s32[1088]{0:T(1024)S(1)} %copy-done.53, ...), kind=kOutput, calls=%fused_computation.80 | convolution fusion | flops 1217726464 | bytes 38451456 | tf_op jit(solution)/shard_map/rd,kd->rk/dot_general | solution.py:353
  846.6 15.0 %multiply_convert_fusion.6 = (bf16[1088,2112]{1,0:T(8,128)(2,1)}, bf16[1088,2112]{1,0:T(8,128)(2,1)S(1)}) fusion(f32[1088,2112]{1,0:T(8,128)} %copy-done.13, f32[1088,2112]{1,0:T(8,128)} %get-tuple-element.116, f32[1088]{0:T(1024)S(1)} %get-tuple-element.78, f32[1088]{0:T(1024)S(1)} %log_add_fusion.1, s32[1088]{0:T(1024)S(1)} %copy-done.41, ...), kind=kLoop, calls=%fused_computation.79 | loop fusion | flops 62042112 | bytes 46004480 | tf_op jit(solution)/shard_map/convert_element_type | solution.py:357
  861.5 4.1 fusion.91
  875.6 7.5 convolution_convert_fusion.5
  883.2 3.1 convert_element_type.271
  886.2 9.2 reduce-scatter.8.cloned.1.call-done
  895.4 3.0 convert_element_type.267
  898.4 4.8 fusion.66
  903.2 7.6 convolution_convert_fusion.6
  912.9 3.7 fusion.80
  916.6 3.7 fusion.79
  920.4 2.9 convolution_convert_fusion.8
  923.3 2.8 convolution_add_fusion.1
  926.2 5.2 fusion.15.x_ref
  931.4 2.8 convolution_convert_fusion.7
  934.3 136.0 %shard_map.189 = bf16[1088,2304]{1,0:T(8,128)(2,1)S(1)} custom-call(bf16[1088,2304]{1,0:T(8,128)(2,1)} %fusion.15.x_ref), custom_call_target="tpu_custom_call" | custom-call | flops 2506752 | bytes 209715200 | tf_op jit(solution)/shard_map/pallas_call | solution.py:126
  1070.4 4.5 fusion.36
  1075.3 4.4 fusion.47
  1081.7 2.3 copy.50
  1084.7 15.4 %fusion.21 = f32[1088,2304]{1,0:T(8,128)} fusion(f32[1088,2304]{1,0:T(8,128)} %get-tuple-element.84, bf16[1088,2304]{1,0:T(8,128)(2,1)} %copy-done.2, f32[1088]{0:T(1024)S(1)} %broadcast_multiply_fusion.1, f32[2304]{0:T(1024)S(1)} %copy-done.29, f32[1088]{0:T(1024)} %copy-done.44, bf16[2,1,544,2304]{3,2,1,0:T(8,128)(2,1)} %param.11), kind=kLoop, calls=%fused_computation.45 | loop fusion | flops 20054016 | bytes 30098944 | tf_op jit(solution)/shard_map/add | solution.py:424
  1102.1 32.5 %reduce-scatter.12.cloned.1.call-done = bf16[288,1152]{1,0:T(8,128)(2,1)} async-done(((bf16[2304,1152]{1,0:T(8,128)(2,1)}), bf16[288,1152]{1,0:T(8,128)(2,1)}) %reduce-scatter.12.cloned.1.call-update) | async-done | bytes 663568 | tf_op jit(solution)/shard_map/reduce_scatter | solution.py:327
  (316 shorter events, 50.7 us)
Async XLA Ops:
  7.2 47.4 %all-gather.6.cloned.1.call-start = ((), (), s32[]{:S(2)}) async-start(), calls=%async_computation.5 | async-start | bytes 5971968 | tf_op jit(solution)/shard_map/all_gather | solution.py:228
  10.1 124.9 %all-gather.8.cloned.1.call-start = ((), (), s32[]{:S(2)}) async-start(), calls=%async_computation.6 | async-start | bytes 2654208 | tf_op jit(solution)/shard_map/all_gather | solution.py:233
  10.8 283.5 %all-gather.10.cloned.1.call-start = ((), (), s32[]{:S(2)}) async-start(), calls=%async_computation.7 | async-start | bytes 11943936 | tf_op jit(solution)/shard_map/all_gather | solution.py:234
  11.6 300.2 %all-gather.12.cloned.1.call-start = ((), (), s32[]{:S(2)}) async-start(), calls=%async_computation.8 | async-start | bytes 11943936 | tf_op jit(solution)/shard_map/all_gather | solution.py:235
  12.2 322.1 %all-gather.14.cloned.1.call-start = ((), (), s32[]{:S(2)}) async-start(), calls=%async_computation.9 | async-start | bytes 11943936 | tf_op jit(solution)/shard_map/all_gather | solution.py:236
  12.7 751.4 %reduce-scatter.16.cloned.1.call-start = ((), (), s32[]{:S(2)}) async-start(), calls=%async_computation.14 | async-start | bytes 11943936
  13.2 117.2 %copy-start.40 = (s32[1088]{0:T(1024)}, s32[1088]{0:T(1024)S(1)}, u32[]{:S(2)}) copy-start(s32[1088]{0:T(1024)S(1)} %le.16) | copy-start | bytes 13060
  17.1 47.3 %copy-start.44 = (f32[1088]{0:T(1024)}, f32[1088]{0:T(1024)S(1)}, u32[]{:S(2)}) copy-start(f32[1088]{0:T(1024)S(1)} %rsqrt.41) | copy-start | bytes 13060
  18.1 112.3 %copy-start.52 = (s32[1088]{0:T(1024)}, s32[1088]{0:T(1024)S(1)}, u32[]{:S(2)}) copy-start(s32[1088]{0:T(1024)S(1)} %get-tuple-element.107) | copy-start | bytes 13060
  18.1 112.3 %copy-start.54 = (s32[1088]{0:T(1024)}, s32[1088]{0:T(1024)S(1)}, u32[]{:S(2)}) copy-start(s32[1088]{0:T(1024)S(1)} %get-tuple-element.108) | copy-start | bytes 13060
  18.1 112.3 %copy-start.48 = (s32[2112]{0:T(1024)}, s32[2112]{0:T(1024)S(1)}, u32[]{:S(2)}) copy-start(s32[2112]{0:T(1024)S(1)} %get-tuple-element.117) | copy-start | bytes 25348
  18.1 112.3 %copy-start.50 = (s32[2112]{0:T(1024)}, s32[2112]{0:T(1024)S(1)}, u32[]{:S(2)}) copy-start(s32[2112]{0:T(1024)S(1)} %get-tuple-element.118) | copy-start | bytes 25348
  55.7 8.6 slice-start.4
  58.3 223.6 %copy-start.30 = (f32[2304]{0:T(1024)}, f32[2304]{0:T(1024)S(1)}, u32[]{:S(2)}) copy-start(f32[2304]{0:T(1024)S(1)} %get-tuple-element.76) | copy-start | bytes 27652
  58.3 229.8 %copy-start.34 = (f32[2304]{0:T(1024)}, f32[2304]{0:T(1024)S(1)}, u32[]{:S(2)}) copy-start(f32[2304]{0:T(1024)S(1)} %get-tuple-element.75) | copy-start | bytes 27652
  67.1 63.4 %copy-start.38 = (bf16[2,32,256]{2,1,0:T(8,128)(2,1)}, bf16[2,32,256]{2,1,0:T(8,128)(2,1)S(1)}, u32[]{:S(2)}) copy-start(bf16[2,32,256]{2,1,0:T(8,128)(2,1)S(1)} %slice.161) | copy-start | bytes 98308
  72.8 13.4 %copy-start.9 = (f32[1088,256]{1,0:T(8,128)}, f32[1088,256]{1,0:T(8,128)S(1)}, u32[]{:S(2)}) copy-start(f32[1088,256]{1,0:T(8,128)S(1)} %get-tuple-element.104) | copy-start | bytes 3342340
  72.9 13.4 %copy-start.11 = (f32[1088,256]{1,0:T(8,128)}, f32[1088,256]{1,0:T(8,128)S(1)}, u32[]{:S(2)}) copy-start(f32[1088,256]{1,0:T(8,128)S(1)} %get-tuple-element.103) | copy-start | bytes 3342340
  72.9 43.6 %copy-start.61 = (bf16[2,32,256]{2,1,0:T(8,128)(2,1)}, bf16[2,32,256]{2,1,0:T(8,128)(2,1)S(1)}, u32[]{:S(2)}) copy-start(bf16[2,32,256]{2,1,0:T(8,128)(2,1)S(1)} %slice.160) | copy-start | bytes 98308
  79.3 32.9 %collective-permute-start = (bf16[2,512,512]{2,1,0:T(8,128)(2,1)S(1)}, bf16[2,512,512]{2,1,0:T(8,128)(2,1)S(1)}, u32[]{:S(2)}, u32[]{:S(2)}) collective-permute-start(bf16[2,512,512]{2,1,0:T(8,128)(2,1)S(1)} %pad_maximum_fusion.9), channel_id=1, source_target_pairs={{0,4},{4,0},{1,5},{5,1},{2,6},{6,2},{3,7},{7,3},{8,12},{12,8},{9,1... | collective-permute-start | bytes 3145736 | tf_op jit(solution)/shard_map/ppermute | solution.py:254
  86.8 29.7 %copy-start.24 = (bf16[1088,2,256]{2,0,1:T(8,128)(2,1)}, bf16[1088,2,256]{2,0,1:T(8,128)(2,1)S(1)}, u32[]{:S(2)}) copy-start(bf16[1088,2,256]{2,0,1:T(8,128)(2,1)S(1)} %fusion.64) | copy-start | bytes 3342340
  112.7 17.7 %copy-start.17 = (bf16[2,1024,256]{2,1,0:T(8,128)(2,1)}, bf16[2,1024,256]{2,1,0:T(8,128)(2,1)S(1)}, u32[]{:S(2)}) copy-start(bf16[2,1024,256]{2,1,0:T(8,128)(2,1)S(1)} %get-tuple-element.90) | copy-start | bytes 3145732
  116.5 14.0 %copy-start.13 = (f32[1088,2112]{1,0:T(8,128)}, f32[1088,2112]{1,0:T(8,128)S(1)}, u32[]{:S(2)}) copy-start(f32[1088,2112]{1,0:T(8,128)S(1)} %get-tuple-element.112) | copy-start | bytes 27574276
  116.5 14.0 %copy-start.64 = (f32[1088]{0:T(1024)}, f32[1088]{0:T(1024)S(1)}, u32[]{:S(2)}) copy-start(f32[1088]{0:T(1024)S(1)} %get-tuple-element.111) | copy-start | bytes 13060
  122.2 8.2 copy-start.5
  122.2 8.2 copy-start.57
  122.2 8.3 copy-start.66
  482.4 10.6 copy-start.1
  482.4 10.5 slice-start.8
  483.5 9.5 copy-start.46
  483.5 9.4 slice-start.9
  497.3 20.6 %copy-start.16 = (bf16[1088,2304]{1,0:T(8,128)(2,1)S(1)}, bf16[1088,2304]{1,0:T(8,128)(2,1)}, u32[]{:S(2)}) copy-start(bf16[1088,2304]{1,0:T(8,128)(2,1)} %fusion.18) | copy-start | bytes 15040516
  497.3 47.2 %slice-start.15 = ((s8[5013504]{0:T(1024)(128)(4,1)}), s8[4194304]{0:T(1024)(128)(4,1)S(1)}, s32[]{:S(2)}) async-start(s8[5013504]{0:T(1024)(128)(4,1)} %bitcast.162), calls=%async_computation.30 | async-start | bytes 8388608
  517.9 26.7 %slice-start.16 = ((s8[5013504]{0:T(1024)(128)(4,1)}), s8[819200]{0:T(1024)(128)(4,1)S(1)}, s32[]{:S(2)}) async-start(s8[5013504]{0:T(1024)(128)(4,1)} %bitcast.162), calls=%async_computation.31 | async-start | bytes 1638400
  633.7 249.4 %reduce-scatter.10.cloned.1.call-start = ((), (), s32[]{:S(2)}) async-start(), calls=%async_computation.11 | async-start | bytes 11943936 | tf_op jit(solution)/shard_map/reduce_scatter | solution.py:327
  634.5 260.9 %reduce-scatter.8.cloned.1.call-start = ((), (), s32[]{:S(2)}) async-start(), calls=%async_computation.10 | async-start | bytes 11943936 | tf_op jit(solution)/shard_map/reduce_scatter | solution.py:327
  764.0 336.1 %reduce-scatter.14.cloned.1.call-start = ((), (), s32[]{:S(2)}) async-start(), calls=%async_computation.13 | async-start | bytes 2654208 | tf_op jit(solution)/shard_map/reduce_scatter | solution.py:327
  766.3 10.9 slice-start.2
  768.3 8.8 slice-start.3
  768.3 8.8 copy-start.33
  768.3 8.8 copy-start.47
  768.3 24.3 %slice-start = ((s8[5013504]{0:T(1024)(128)(4,1)}), s8[4194304]{0:T(1024)(128)(4,1)S(1)}, s32[]{:S(2)}) async-start(s8[5013504]{0:T(1024)(128)(4,1)} %bitcast.139), calls=%async_computation.15 | async-start | bytes 8388608
  777.2 15.5 %slice-start.1 = ((s8[5013504]{0:T(1024)(128)(4,1)}), s8[819200]{0:T(1024)(128)(4,1)S(1)}, s32[]{:S(2)}) async-start(s8[5013504]{0:T(1024)(128)(4,1)} %bitcast.139), calls=%async_computation.16 | async-start | bytes 1638400
  777.2 15.5 %copy-start.31 = (f32[2304]{0:T(1024)S(1)}, f32[2304]{0:T(1024)}, u32[]{:S(2)}) copy-start(f32[2304]{0:T(1024)} %copy-done.30) | copy-start | bytes 27652
  777.2 15.5 %copy-start.37 = (f32[1088]{0:T(1024)S(1)}, f32[1088]{0:T(1024)}, u32[]{:S(2)}) copy-start(f32[1088]{0:T(1024)} %copy-done.36) | copy-start | bytes 13060
  799.2 8.4 copy-start.69
  812.3 11.2 copy-start.23
  812.3 21.5 %slice-start.10 = ((s8[9469952]{0:T(1024)(128)(4,1)}), s8[4194304]{0:T(1024)(128)(4,1)S(1)}, s32[]{:S(2)}) async-start(s8[9469952]{0:T(1024)(128)(4,1)} %bitcast.152), calls=%async_computation.25 | async-start | bytes 8388608
  812.3 21.5 %slice-start.11 = ((s8[9469952]{0:T(1024)(128)(4,1)}), s8[4194304]{0:T(1024)(128)(4,1)S(1)}, s32[]{:S(2)}) async-start(s8[9469952]{0:T(1024)(128)(4,1)} %bitcast.152), calls=%async_computation.26 | async-start | bytes 8388608
  823.5 8.8 copy-start.18
  823.5 8.8 copy-start.39
  823.6 10.3 slice-start.12
  846.6 15.0 %copy-start.25 = (bf16[1088,2,256]{2,0,1:T(8,128)(2,1)S(1)}, bf16[1088,2,256]{2,0,1:T(8,128)(2,1)}, u32[]{:S(2)}) copy-start(bf16[1088,2,256]{2,0,1:T(8,128)(2,1)} %copy-done.24) | copy-start | bytes 3342340
  869.3 41.6 %collective-permute-start.1 = (bf16[2,512,512]{2,1,0:T(8,128)(2,1)}, bf16[2,512,512]{2,1,0:T(8,128)(2,1)}, u32[]{:S(2)}, u32[]{:S(2)}) collective-permute-start(bf16[2,512,512]{2,1,0:T(8,128)(2,1)} %select_convert_fusion), channel_id=1, source_target_pairs={{0,4},{4,0},{1,5},{5,1},{2,6},{6,2},{3,7},{7,3},{8,12},{12,8},{9,1... | collective-permute-start | bytes 3145736 | tf_op jit(solution)/shard_map/ppermute | solution.py:380
  883.1 15.4 %copy-start.22 = (bf16[1088,2,256]{0,2,1:T(8,128)(2,1)S(1)}, bf16[1088,2,256]{0,2,1:T(8,128)(2,1)}, u32[]{:S(2)}) copy-start(bf16[1088,2,256]{0,2,1:T(8,128)(2,1)} %copy.46) | copy-start | bytes 3342340
  883.1 251.5 %reduce-scatter.12.cloned.1.call-start = ((), (), s32[]{:S(2)}) async-start(), calls=%async_computation.12 | async-start | bytes 5971968 | tf_op jit(solution)/shard_map/reduce_scatter | solution.py:327
  903.2 7.6 copy-start.7
  912.6 7.7 slice-start.17
  920.4 11.1 slice-start.19
  923.3 8.1 slice-start.20
  926.2 144.1 %slice-start.6 = ((s8[5013504]{0:T(1024)(128)(4,1)}), s8[4194304]{0:T(1024)(128)(4,1)S(1)}, s32[]{:S(2)}) async-start(s8[5013504]{0:T(1024)(128)(4,1)} %bitcast.145), calls=%async_computation.21 | async-start | bytes 8388608
  931.4 138.9 %slice-start.7 = ((s8[5013504]{0:T(1024)(128)(4,1)}), s8[819200]{0:T(1024)(128)(4,1)S(1)}, s32[]{:S(2)}) async-start(s8[5013504]{0:T(1024)(128)(4,1)} %bitcast.145), calls=%async_computation.22 | async-start | bytes 1638400
  934.3 136.1 %copy-start.29 = (f32[2304]{0:T(1024)S(1)}, f32[2304]{0:T(1024)}, u32[]{:S(2)}) copy-start(f32[2304]{0:T(1024)} %copy-done.28) | copy-start | bytes 27652
  934.3 136.1 %copy-start.45 = (f32[1088]{0:T(1024)S(1)}, f32[1088]{0:T(1024)}, u32[]{:S(2)}) copy-start(f32[1088]{0:T(1024)} %copy-done.44) | copy-start | bytes 13060
  (43 other events, 141.4 us)
Sparse Core Ops, SparseCore 0:
  10.5 44.0 all-gather.5
  56.5 30.8 all-gather.7
  89.2 69.5 all-gather.9
  160.6 63.7 all-gather.11
  226.1 63.7 all-gather.13
  633.8 78.0 reduce-scatter.15
  715.4 82.2 reduce-scatter.9
  801.2 94.2 reduce-scatter.7
  898.8 42.5 reduce-scatter.13
  1079.8 54.7 reduce-scatter.11

commit v4 on v3

--- a/solution.py
+++ b/solution.py
@@ -11,6 +11,7 @@
 
 HEAD = 256
 CONT = 32
+BLOCK = 16
 
 
 EPS = 1e-06
@@ -133,6 +134,420 @@
         compiler_params=pltpu.CompilerParams(collective_id=cid, has_side_effects=True, vmem_limit_bytes=48 * 2**20),
         cost_estimate=pl.CostEstimate(flops=rows*cols, bytes_accessed=200*2**20, transcendentals=0),
     )(x)
+
+
+TILE = 256
+STAGES = 6
+LAG = 2
+PACE = 1
+
+
+def chain_place(size):
+    place = lax.axis_index("tensor")
+    dp, seq = lax.axis_index("dp"), lax.axis_index("seq")
+    down = (dp, seq, jnp.maximum(place - 1, 0))
+    up = (dp, seq, jnp.minimum(place + 1, size - 1))
+    return place, down, up, place == 0, place == size - 1
+
+
+def greet_line(down, up, first, last):
+    barrier = pltpu.get_barrier_semaphore()
+
+    @pl.when(jnp.logical_not(first))
+    def _():
+        pl.semaphore_signal(barrier, inc=1, device_id=down, device_id_type=MESH)
+
+    @pl.when(jnp.logical_not(last))
+    def _():
+        pl.semaphore_signal(barrier, inc=1, device_id=up, device_id_type=MESH)
+
+    pl.semaphore_wait(barrier, 2 - first.astype(jnp.int32) - last.astype(jnp.int32))
+
+
+def gelu_parts(gate):
+    square = gate * gate
+    slope = 0.7978845608028654
+    curve = jnp.tanh(gate * (slope + (slope * 0.044715) * square))
+    half = 0.5 + 0.5 * curve
+    rise = (0.5 * gate) * (1.0 - curve * curve) * (slope + (3.0 * slope * 0.044715) * square)
+    return gate * half, half + rise
+
+
+def ffn_kernel(
+    size, width, bases, schedule,
+    part_ref, token_ref, cot_ref, gate_ref, up_ref, down_ref, gain_ref,
+    sum_ref, out_ref, ffn_in_ref, hidden_ref, d_ffn_ref, d_gate_ref, d_up_ref, gain_grad_ref,
+    parts, landing, act_a, act_b, stage_t, stage_a, stage_f, stage_c, cols, rows_w,
+    pass_in, pass_out, share_in, share_out, local_done, col_sem, row_sem, io_sem,
+):
+    micro, rows, depth = parts.shape
+    units = gate_ref.shape[1]
+    half = rows // 2
+    chunks = depth // width
+    place, down, up, first, last = chain_place(size)
+    greet_line(down, up, first, last)
+
+    def side(which):
+        toward, back = ((down, up), (up, down))[which]
+        start, end = ((last, first), (first, last))[which]
+        rank = (size - 1 - place, place)[which]
+        span = pl.ds(which * half, half)
+
+        def where_at(u):
+            q = jnp.int32(0)
+            base = jnp.int32(bases[0])
+            for k in range(1, STAGES):
+                past = (u >= bases[k]).astype(jnp.int32)
+                q = q + past
+                base = base + past * (bases[k] - bases[k - 1])
+            c = u - base
+            return q, c, (c >= 0) & (c < chunks)
+
+        def columns(c):
+            return pl.ds(pl.multiple_of(c * width, 128), width)
+
+        def passing(q, c, source):
+            return pltpu.make_async_remote_copy(
+                source, landing.at[which, q, c], pass_out.at[which, q, c], pass_in.at[which, q, c],
+                device_id=toward, device_id_type=MESH)
+
+        def sharing(q, c, source):
+            return pltpu.make_async_remote_copy(
+                source, sum_ref.at[q, span, columns(c)], share_out.at[which, q, c], share_in.at[which, q, c],
+                device_id=back, device_id_type=MESH)
+
+        def local(q, c):
+            return pltpu.make_async_copy(
+                landing.at[which, q, c], sum_ref.at[q, span, columns(c)], local_done.at[which, q, c])
+
+        def reduce_step(s):
+            q, c, ok = where_at(s - LAG * rank)
+            m = lax.rem(q, 2)
+
+            @pl.when(ok & start)
+            def _():
+                passing(q, c, parts.at[m, span, columns(c)]).start()
+
+            @pl.when(ok & jnp.logical_not(start))
+            def _():
+                passing(q, c, landing.at[which, q, c]).wait_recv()
+                mine = parts[m, span, columns(c)].astype(jnp.float32)
+                landing[which, q, c] = (landing[which, q, c].astype(jnp.float32) + mine).astype(jnp.bfloat16)
+
+                @pl.when(end)
+                def _():
+                    sharing(q, c, landing.at[which, q, c]).start()
+                    local(q, c).start()
+
+                @pl.when(jnp.logical_not(end))
+                def _():
+                    passing(q, c, landing.at[which, q, c]).start()
+
+        def share_step(s):
+            q, c, ok = where_at(s - LAG * (2 * (size - 1) - rank))
+
+            @pl.when(ok & jnp.logical_not(end))
+            def _():
+                view = sum_ref.at[q, span, columns(c)]
+                sharing(q, c, view).wait_recv()
+
+                @pl.when(jnp.logical_not(start))
+                def _():
+                    sharing(q, c, view).start()
+
+        def settle(q):
+            @pl.when(end)
+            def _():
+                @pl.loop(0, chunks)
+                def _(c):
+                    local(q, c).wait()
+
+        def sent(q):
+            @pl.when(jnp.logical_not(end))
+            def _():
+                @pl.loop(0, chunks)
+                def _(c):
+                    passing(q, c, landing.at[which, q, c]).wait_send()
+
+        def shared(q):
+            @pl.when(jnp.logical_not(start))
+            def _():
+                @pl.loop(0, chunks)
+                def _(c):
+                    sharing(q, c, landing.at[which, q, c]).wait_send()
+
+        return reduce_step, share_step, settle, sent, shared
+
+    sides = (side(0), side(1))
+
+    def tick(s):
+        for one in sides:
+            one[0](s)
+        for one in sides:
+            one[1](s)
+
+    def settle(q):
+        for one in sides:
+            one[2](q)
+
+    def sent(q):
+        for one in sides:
+            one[3](q)
+
+    def ticks(low, high):
+        @pl.loop(low, high)
+        def _(s):
+            tick(s)
+
+    def col_copy(kind, source, i, slot):
+        return pltpu.make_async_copy(
+            source.at[:, pl.ds(pl.multiple_of(i * TILE, TILE), TILE)], cols.at[kind, slot], col_sem.at[kind, slot])
+
+    def row_copy(kind, source, i, slot):
+        return pltpu.make_async_copy(
+            source.at[pl.ds(pl.multiple_of(i * TILE, TILE), TILE)], rows_w.at[kind, slot], row_sem.at[kind, slot])
+
+    def tiles(copy, sources, steps, body, clock):
+        @pl.loop(0, steps)
+        def _(i):
+            slot = lax.rem(i, 2)
+
+            @pl.when(i + 1 < steps)
+            def _():
+                for kind, source in enumerate(sources):
+                    copy(kind, source, i + 1, 1 - slot).start()
+
+            for kind, source in enumerate(sources):
+                copy(kind, source, i, slot).wait()
+            body(i, slot)
+
+            @pl.when((lax.rem(i, PACE) == PACE - 1) | (i + 1 == steps))
+            def _():
+                tick(clock + i // PACE)
+
+    def prime(copy, sources):
+        for kind, source in enumerate(sources):
+            copy(kind, source, 0, 0).start()
+
+    def span_of(i):
+        return pl.ds(pl.multiple_of(i * TILE, TILE), TILE)
+
+    def io(index, source, target):
+        return pltpu.make_async_copy(source, target, io_sem.at[index])
+
+    def row_blocks(body, clock):
+        count = rows // BLOCK
+        for low, high, s in ((0, count // 2, clock), (count // 2, count, clock + 1)):
+            @pl.loop(low, high)
+            def _(b):
+                body(pl.ds(pl.multiple_of(b * BLOCK, BLOCK), BLOCK))
+            tick(s)
+
+    def gain(k):
+        return gain_ref[k : k + 1, :]
+
+    def inverse(values):
+        return lax.rsqrt(jnp.mean(values * values, axis=-1, keepdims=True) + EPS)
+
+    def middle_of(span):
+        attn = stage_a[span, :].astype(jnp.float32)
+        return stage_t[span, :].astype(jnp.float32) + attn * inverse(attn) * gain(1)
+
+    forward = ((gate_ref, up_ref), (down_ref,))
+
+    def norm_before(m, clock):
+        def body(span):
+            middle = middle_of(span)
+            stage_f[span, :] = (middle * inverse(middle) * gain(2)).astype(jnp.bfloat16)
+        row_blocks(body, clock)
+
+    def gate_and_up(m, clock):
+        def body(i, slot):
+            at = span_of(i)
+            gate = jnp.dot(stage_f[...], cols[0, slot], preferred_element_type=jnp.float32)
+            up_val = jnp.dot(stage_f[...], cols[1, slot], preferred_element_type=jnp.float32)
+            active, slope = gelu_parts(gate)
+            stage_c[:, at] = (active * up_val).astype(jnp.bfloat16)
+            act_a[m, :, at] = active.astype(jnp.bfloat16)
+            act_b[m, :, at] = (up_val * slope).astype(jnp.bfloat16)
+        tiles(col_copy, (gate_ref, up_ref), units // TILE, body, clock)
+
+    def down_proj(m, clock):
+        def body(i, slot):
+            parts[m, :, span_of(i)] = lax.dot_general(
+                stage_c[...], rows_w[0, slot], (((1,), (1,)), ((), ())),
+                preferred_element_type=jnp.float32).astype(jnp.bfloat16)
+        tiles(row_copy, (down_ref,), depth // TILE, body, clock)
+
+    def norm_after(m, clock):
+        def body(span):
+            middle = middle_of(span)
+            ffn = stage_f[span, :].astype(jnp.float32)
+            above = stage_c[span, :].astype(jnp.float32)
+            inv = inverse(ffn)
+            normed = ffn * inv
+            stage_f[span, :] = (middle + normed * gain(3)).astype(jnp.bfloat16)
+            scaled = above * gain(3)
+            d_ffn = inv * (scaled - normed * jnp.mean(scaled * normed, axis=-1, keepdims=True))
+            stage_c[span, :] = d_ffn.astype(jnp.bfloat16)
+            term = above * normed
+            gain_grad_ref[...] += term[:8] + term[8:]
+        row_blocks(body, clock)
+
+    def d_hidden(m, clock):
+        def body(i, slot):
+            at = span_of(i)
+            d_hid = jnp.dot(stage_c[...], cols[0, slot], preferred_element_type=jnp.float32)
+            act_a[m, :, at] = (d_hid * act_a[m, :, at].astype(jnp.float32)).astype(jnp.bfloat16)
+            act_b[m, :, at] = (d_hid * act_b[m, :, at].astype(jnp.float32)).astype(jnp.bfloat16)
+        tiles(col_copy, (down_ref,), units // TILE, body, clock)
+
+    def d_input(m, clock):
+        def body(i, slot):
+            dims = (((1,), (1,)), ((), ()))
+            parts[m, :, span_of(i)] = (
+                lax.dot_general(act_b[m], rows_w[0, slot], dims, preferred_element_type=jnp.float32)
+                + lax.dot_general(act_a[m], rows_w[1, slot], dims, preferred_element_type=jnp.float32)
+            ).astype(jnp.bfloat16)
+        tiles(row_copy, (gate_ref, up_ref), depth // TILE, body, clock)
+
+    gain_grad_ref[...] = jnp.zeros_like(gain_grad_ref)
+    for m in range(micro):
+        io(m, part_ref.at[m], parts.at[m]).start()
+    io(2, token_ref.at[0], stage_t).start()
+    prime(col_copy, (gate_ref, up_ref))
+    for m in range(micro):
+        io(m, part_ref.at[m], parts.at[m]).wait()
+    ticks(0, schedule["attn"][0])
+    for m in range(micro):
+        norm_s, gate_s, down_s, end_s = schedule["forward"][m]
+        settle(m)
+        io(3, sum_ref.at[m], stage_a).start()
+        if m:
+            io(2, token_ref.at[m], stage_t).start()
+            io(6, stage_f, ffn_in_ref.at[m - 1]).wait()
+            io(7, stage_c, hidden_ref.at[m - 1]).wait()
+        io(2, token_ref.at[m], stage_t).wait()
+        io(3, sum_ref.at[m], stage_a).wait()
+        norm_before(m, norm_s)
+        io(6, stage_f, ffn_in_ref.at[m]).start()
+        prime(row_copy, (down_ref,))
+        gate_and_up(m, gate_s)
+        io(7, stage_c, hidden_ref.at[m]).start()
+        sent(m)
+        if m + 1 < micro:
+            prime(col_copy, (gate_ref, up_ref))
+        else:
+            prime(col_copy, (down_ref,))
+            io(2, token_ref.at[0], stage_t).start()
+            io(3, sum_ref.at[0], stage_a).start()
+        down_proj(m, down_s)
+        ticks(down_s + -(-depth // (TILE * PACE)), end_s)
+    io(6, stage_f, ffn_in_ref.at[micro - 1]).wait()
+    io(7, stage_c, hidden_ref.at[micro - 1]).wait()
+    for m in range(micro):
+        norm_s, dh_s, di_s, end_s = schedule["backward"][m]
+        settle(micro + m)
+        io(4, sum_ref.at[micro + m], stage_f).start()
+        io(5, cot_ref.at[m], stage_c).start()
+        io(2, token_ref.at[m], stage_t).wait()
+        io(3, sum_ref.at[m], stage_a).wait()
+        io(4, sum_ref.at[micro + m], stage_f).wait()
+        io(5, cot_ref.at[m], stage_c).wait()
+        norm_after(m, norm_s)
+        io(6, stage_f, out_ref.at[m]).start()
+        io(7, stage_c, d_ffn_ref.at[m]).start()
+        prime(row_copy, (gate_ref, up_ref))
+        d_hidden(m, dh_s)
+        io(8, act_b.at[m], d_gate_ref.at[m]).start()
+        io(9, act_a.at[m], d_up_ref.at[m]).start()
+        sent(micro + m)
+        if m + 1 < micro:
+            prime(col_copy, (down_ref,))
+            io(2, token_ref.at[m + 1], stage_t).start()
+            io(3, sum_ref.at[m + 1], stage_a).start()
+        d_input(m, di_s)
+        ticks(di_s + -(-depth // (TILE * PACE)), end_s)
+        io(6, stage_f, out_ref.at[m]).wait()
+        io(7, stage_c, d_ffn_ref.at[m]).wait()
+        io(8, act_b.at[m], d_gate_ref.at[m]).wait()
+        io(9, act_a.at[m], d_up_ref.at[m]).wait()
+    for q in (STAGES - 2, STAGES - 1):
+        settle(q)
+        sent(q)
+
+    @pl.loop(0, STAGES)
+    def _(q):
+        for one in sides:
+            one[4](q)
+
+
+def ffn_schedule(chunks, tiles, hops):
+    whole = chunks + hops
+    bases = [0, chunks]
+    at = whole
+    attn = (at,)
+    forward = []
+    for m in range(2):
+        norm_s = at
+        gate_s = norm_s + 2
+        down_s = gate_s + tiles
+        bases.append(max(down_s, bases[-1] + chunks))
+        at = max(down_s + tiles, bases[m + 1] + whole)
+        forward.append((norm_s, gate_s, down_s, at))
+    backward = []
+    for m in range(2):
+        norm_s = at
+        dh_s = norm_s + 2
+        di_s = dh_s + tiles
+        bases.append(max(di_s, bases[-1] + chunks))
+        at = max(di_s + tiles, bases[m + 3] + whole)
+        backward.append((norm_s, dh_s, di_s, at))
+    last = backward[-1]
+    backward[-1] = last[:3] + (max(last[3], bases[-1] + whole),)
+    return tuple(bases), {"attn": attn, "forward": tuple(forward), "backward": tuple(backward)}
+
+
+def ffn_block(parts, tokens, cotangent, gate, up, down, gains, cid, width=128):
+    size = lax.axis_size("tensor")
+    micro, rows, depth = tokens.shape
+    units = gate.shape[1]
+    chunks = depth // width
+    bases, schedule = ffn_schedule(chunks, -(-units // (TILE * PACE)), 2 * LAG * (size - 1))
+    bf16 = jnp.bfloat16
+    any_spec = pl.BlockSpec(memory_space=pl.ANY)
+    vmem_spec = pl.BlockSpec(memory_space=pltpu.VMEM)
+    stack = jax.ShapeDtypeStruct((micro, rows, depth), bf16)
+    wide = jax.ShapeDtypeStruct((micro, rows, units), bf16)
+    dma = pltpu.SemaphoreType.DMA
+    flops = 2 * micro * rows * depth * units * 6
+    return pl.pallas_call(
+        functools.partial(ffn_kernel, size, width, bases, schedule),
+        out_shape=(
+            jax.ShapeDtypeStruct((STAGES, rows, depth), bf16),
+            stack, stack, wide, stack, wide, wide,
+            jax.ShapeDtypeStruct((8, depth), jnp.float32),
+        ),
+        in_specs=[any_spec] * 6 + [vmem_spec],
+        out_specs=(any_spec,) * 7 + (vmem_spec,),
+        scratch_shapes=[
+            pltpu.VMEM((micro, rows, depth), bf16),
+            pltpu.VMEM((2, STAGES, chunks, rows // 2, width), bf16),
+            pltpu.VMEM((micro, rows, units), bf16),
+            pltpu.VMEM((micro, rows, units), bf16),
+            pltpu.VMEM((rows, depth), bf16),
+            pltpu.VMEM((rows, depth), bf16),
+            pltpu.VMEM((rows, depth), bf16),
+            pltpu.VMEM((rows, depth), bf16),
+            pltpu.VMEM((2, 2, depth, TILE), bf16),
+            pltpu.VMEM((2, 2, TILE, units), bf16),
+        ]
+        + [dma((2, STAGES, chunks))] * 5
+        + [dma((2, 2)), dma((2, 2)), dma((10,))],
+        compiler_params=pltpu.CompilerParams(
+            collective_id=cid, has_side_effects=True, vmem_limit_bytes=60 * 2**20),
+        cost_estimate=pl.CostEstimate(flops=flops, bytes_accessed=2**30, transcendentals=micro * rows * units),
+    )(parts, tokens, cotangent, gate, up, down, gains)
 
 
 def normalize(values):
@@ -233,7 +648,7 @@
     full_out = lax.all_gather(out_weight, axes, axis=1, tiled=True)
     full_gate = lax.all_gather(gate_weight, axes, axis=0, tiled=True)
     full_up = lax.all_gather(up_weight, axes, axis=0, tiled=True)
-    full_down = lax.all_gather(down_weight, axes, axis=1, tiled=True)
+    full_down = lax.all_gather(down_weight.T, axes, axis=0, tiled=True)
     gain_float = gain_rows.astype(jnp.float32)
     inputs = tokens.reshape(total_rows, model_width).astype(jnp.float32)
     normed_in = (normalize(inputs) * gain_float[0]).astype(jnp.bfloat16)
@@ -285,59 +700,52 @@
         contexts.append(jnp.dot(probs, value_rows, preferred_element_type=jnp.float32))
         log_sums.append(row_peak + jnp.log(summed))
     context = jnp.stack(contexts, axis=1).reshape(total_rows, -1).astype(jnp.bfloat16)
-    attn = chain_sum(
-        jnp.dot(context, full_out, preferred_element_type=jnp.float32).astype(jnp.bfloat16),
+    attn_part = jnp.dot(context, full_out, preferred_element_type=jnp.float32).astype(jnp.bfloat16)
+    gain_pad = jnp.pad(gain_float, ((0, 4), (0, 0)))
+    sums, result, ffn_in, hidden, d_ffn, d_gate, d_up, gain_fourth = ffn_block(
+        attn_part.reshape(tokens.shape[0], row_count, model_width),
+        tokens[:, 0],
+        cotangent[:, 0],
+        full_gate,
+        full_up,
+        full_down,
+        gain_pad,
         0,
-    ).astype(jnp.float32)
+    )
+    gain_fourth = jnp.sum(gain_fourth, axis=0)
+    attn = sums[:micro_count].reshape(total_rows, model_width).astype(jnp.float32)
+    d_ffn_in = sums[2 * micro_count :].reshape(total_rows, model_width)
     middle = inputs + normalize(attn) * gain_float[1]
-    ffn_in = (normalize(middle) * gain_float[2]).astype(jnp.bfloat16)
-    gate = jnp.dot(ffn_in, full_gate, preferred_element_type=jnp.float32)
-    up_val = jnp.dot(ffn_in, full_up, preferred_element_type=jnp.float32)
-    hidden_act, glu_pull = jax.vjp(
-        lambda gate_in, up_in: jax.nn.gelu(gate_in, approximate=True) * up_in, gate, up_val
-    )
-    hidden = hidden_act.astype(jnp.bfloat16)
-    ffn = chain_sum(
-        jnp.dot(hidden, full_down, preferred_element_type=jnp.float32).astype(jnp.bfloat16),
-        1,
-    ).astype(jnp.float32)
-    result = middle + normalize(ffn) * gain_float[3]
     upstream = cotangent.reshape(total_rows, model_width).astype(jnp.float32)
-    d_ffn, gain_fourth = norm_back(ffn, gain_float[3], upstream)
-    d_ffn = d_ffn.astype(jnp.bfloat16)
-    grad_down = jnp.einsum("rf,rd->fd", hidden, d_ffn, preferred_element_type=jnp.float32)
-    d_hidden = jnp.einsum("rd,fd->rf", d_ffn, full_down, preferred_element_type=jnp.float32)
-    d_gate, d_up = glu_pull(d_hidden)
-    d_gate = d_gate.astype(jnp.bfloat16)
-    d_up = d_up.astype(jnp.bfloat16)
+    ffn_in, hidden, d_ffn, d_gate, d_up = (
+        kept.reshape(total_rows, -1) for kept in (ffn_in, hidden, d_ffn, d_gate, d_up)
+    )
+
+    def scatter(grad, axis):
+        return lax.psum_scatter(
+            grad.astype(jnp.bfloat16), axes, scatter_dimension=axis, tiled=True
+        ).astype(jnp.float32)
+
+    grad_down = jnp.einsum("rd,rf->df", d_ffn, hidden, preferred_element_type=jnp.float32)
     grad_gate = jnp.einsum("rd,rf->df", ffn_in, d_gate, preferred_element_type=jnp.float32)
     grad_up = jnp.einsum("rd,rf->df", ffn_in, d_up, preferred_element_type=jnp.float32)
-    ffn_part = jnp.einsum(
-        "rf,df->rd", d_gate, full_gate, preferred_element_type=jnp.float32
-    ) + jnp.einsum("rf,df->rd", d_up, full_up, preferred_element_type=jnp.float32)
-    ffn_part, grad_down, grad_gate, grad_up = lax.optimization_barrier(
+    d_ffn_in, grad_down, grad_gate, grad_up = lax.optimization_barrier(
         (
-            ffn_part.astype(jnp.bfloat16),
+            d_ffn_in,
             grad_down.astype(jnp.bfloat16),
             grad_gate.astype(jnp.bfloat16),
             grad_up.astype(jnp.bfloat16),
         )
     )
-    def scatter(grad, axis):
-        return lax.psum_scatter(
-            grad.astype(jnp.bfloat16), axes, scatter_dimension=axis, tiled=True
-        ).astype(jnp.float32)
-
-    d_ffn_in = chain_sum(ffn_part, 2)
-    share_down = scatter(grad_down, 1)
-    d_ffn_in, share_down = lax.optimization_barrier((d_ffn_in, share_down))
     d_ffn_in = d_ffn_in.astype(jnp.float32)
+    share_down = scatter(grad_down, 0).T
     share_gate = scatter(grad_gate, 0)
     d_mid_norm, gain_third = norm_back(middle, gain_float[2], d_ffn_in)
     d_middle = upstream + d_mid_norm
     d_attn, gain_second = norm_back(attn, gain_float[1], d_middle)
     d_attn = d_attn.astype(jnp.bfloat16)
     grad_out = jnp.einsum("rc,rd->cd", context, d_attn, preferred_element_type=jnp.float32)
+    d_attn, share_down = lax.optimization_barrier((d_attn, share_down))
     d_context = (
         jnp.einsum("rd,cd->rc", d_attn, full_out, preferred_element_type=jnp.float32)
         .astype(jnp.bfloat16)

time: 1160 us -> 1260 us (1.086)
  waiting for transfers between devices: 107 us -> 363 us
  matrix products: 288 us -> 169 us
  Pallas kernels: 532 us -> 513 us
  local copies, waits for them, and re-layouts: 53.2 us -> 38.6 us
    pallas_call x4 -> x1, Pallas kernels: 532 us -> 136 us  [chain_sum(): pl.pallas_call(functools.partial(chain_kernel, size, width), out_shape=ja...]
    pallas_call x0 -> x1, Pallas kernels: none -> 377 us  [ffn_block(): pl.pallas_call(functools.partial(ffn_kernel, size, width, bases, schedule...]
    dot_general x7 -> x1, matrix products: 139 us -> 20.3 us  [per_device(): jnp.einsum('rd,rf->df', d_ffn, hidden, preferred_element_type=jnp.float32)]
    reduce_scatter x4 -> x5, waiting for transfers between devices: 41.8 us -> 157 us  [scatter(): lax.psum_scatter(grad.astype(jnp.bfloat16), axes, scatter_dimension=axis,...]
    all_gather x1, waiting for transfers between devices: 0.01 us -> 65.6 us  [per_device(): full_up = lax.all_gather(up_weight, axes, axis=0, tiled=True)]
    all_gather x1, waiting for transfers between devices: 0.01 us -> 65.6 us  [per_device(): full_down = lax.all_gather(down_weight.T, axes, axis=0, tiled=True)]
    unnamed x197 -> x156, local copies, waits for them, and re-layouts: 34.5 us -> 12.3 us
    add x1 -> x0, other arithmetic: 15.5 us -> none  [per_device(): d_middle = upstream + d_mid_norm]
  transfers between devices with their start and end apart: 12 -> 12, of which waited for: 4 -> 9; matrix products, arithmetic and copies ran while one was open for 26% -> 22% of each run, Pallas kernels for 35% -> 11%
where the time goes in v4:
time: 1260 us; the launch traced here: 1250 us
  Pallas kernels  513 us (41%)
  waiting for transfers between devices  363 us (29%)
  matrix products  169 us (13%)
  other arithmetic  147 us (12%)
  local copies, waits for them, and re-layouts  38.6 us (3%)
  between operations  15.9 us (1%)
    pallas_call x1, Pallas kernels, ffn_block(): pl.pallas_call(functools.partial(ffn_kernel, size, width, bases, schedule...  377 us
    reduce_scatter x5, waiting for transfers between devices, scatter(): lax.psum_scatter(grad.astype(jnp.bfloat16), axes, scatter_dimension=axis,...  157 us
    pallas_call x1, Pallas kernels, chain_sum(): pl.pallas_call(functools.partial(chain_kernel, size, width), out_shape=ja...  136 us
    all_gather x1, waiting for transfers between devices, per_device(): full_up = lax.all_gather(up_weight, axes, axis=0, tiled=True)  65.6 us
    all_gather x1, waiting for transfers between devices, per_device(): full_down = lax.all_gather(down_weight.T, axes, axis=0, tiled=True)  65.6 us
    all_gather x1, waiting for transfers between devices, per_device(): full_side = lax.all_gather(side_weights, axes, axis=0, tiled=True)  31.6 us
  transfers between devices with their start and end apart: 12, of which 9 were waited for; matrix products, arithmetic and copies ran while one was open for 22% of the time, Pallas kernels for 11%

profile of v4, /device:TPU:0, one launch (start us, length us, event | category | flops | bytes accessed | tf_op | source)
XLA Modules:
  0.0 1249.5 jit_solution(15026318656192972165)
XLA Ops:
  8.0 2.0 fusion.60
  12.9 3.6 multiply_reduce_fusion.3
  16.7 4.5 bitcast_convert_fusion.3
  23.0 31.6 %all-gather.6.cloned.1.call-done = bf16[2304,1152]{1,0:T(8,128)(2,1)} async-done(((bf16[288,1152]{1,0:T(8,128)(2,1)}), bf16[2304,1152]{1,0:T(8,128)(2,1)}) %all-gather.6.cloned.1.call-update) | async-done | bytes 5308432 | tf_op jit(solution)/shard_map/all_gather | solution.py:643
  56.8 4.7 multiply_convert_fusion.1
  61.5 2.7 convolution_convert_fusion.6
  64.3 2.7 fusion.58
  67.2 4.1 fusion.46
  72.2 3.2 slice_bitcast_fusion
  75.4 4.5 copy.46
  81.6 3.7 multiply_convert_fusion.2
  85.3 2.8 fusion.84
  88.8 24.3 %collective-permute-done = bf16[2,512,512]{2,1,0:T(8,128)(2,1)S(1)} collective-permute-done((bf16[2,512,512]{2,1,0:T(8,128)(2,1)S(1)}, bf16[2,512,512]{2,1,0:T(8,128)(2,1)S(1)}, u32[]{:S(2)}, u32[]{:S(2)}) %collective-permute-start) | collective-permute-done | bytes 1048608 | tf_op jit(solution)/shard_map/ppermute | solution.py:669
  113.7 3.8 fusion.30
  117.5 6.0 fusion.18
  123.5 4.3 fusion.19
  127.9 3.6 fusion.35
  131.7 3.6 fusion.34
  136.4 7.4 convolution_convert_fusion
  143.8 15.0 %all-gather.10.cloned.1.call-done.gate_ref = bf16[2304,2304]{1,0:T(8,128)(2,1)} async-done(((bf16[288,2304]{1,0:T(8,128)(2,1)}), bf16[2304,2304]{1,0:T(8,128)(2,1)}) %all-gather.10.cloned.1.call-update) | async-done | bytes 10616848 | tf_op jit(solution)/shard_map/all_gather | solution.py:649
  158.8 65.6 %all-gather.12.cloned.1.call-done.up_ref = bf16[2304,2304]{1,0:T(8,128)(2,1)} async-done(((bf16[288,2304]{1,0:T(8,128)(2,1)}), bf16[2304,2304]{1,0:T(8,128)(2,1)}) %all-gather.12.cloned.1.call-update) | async-done | bytes 10616848 | tf_op jit(solution)/shard_map/all_gather | solution.py:650
  224.4 65.6 %all-gather.14.cloned.1.call-done.down_ref = bf16[2304,2304]{1,0:T(8,128)(2,1)} async-done(((bf16[288,2304]{1,0:T(8,128)(2,1)}), bf16[2304,2304]{1,0:T(8,128)(2,1)}) %all-gather.14.cloned.1.call-update) | async-done | bytes 10616848 | tf_op jit(solution)/shard_map/all_gather | solution.py:651
  290.0 377.0 %shard_map.186 = (bf16[6,544,2304]{2,1,0:T(8,128)(2,1)}, bf16[2,544,2304]{2,1,0:T(8,128)(2,1)}, bf16[2,544,2304]{2,1,0:T(8,128)(2,1)}, bf16[2,544,2304]{2,1,0:T(...) custom-call(bf16[2,544,2304]{2,1,0:T(8,128)(2,1)} %bitcast.217, ...), custom_call_target="tpu_custom_call" | custom-call | flops 69306679296 | bytes 1073741824 | tf_op jit(solution)/shard_map/pallas_call | solution.py:524
  667.0 5.4 slice.132
  674.2 16.7 %bitcast_convert_fusion.1 = bf16[2304,2304]{1,0:T(8,128)(2,1)} fusion(bf16[2,544,2304]{2,1,0:T(8,128)(2,1)S(1)} %copy-done.60, bf16[2,544,2304]{2,1,0:T(8,128)(2,1)S(1)} %copy-done.61), kind=kOutput, calls=%fused_computation.1 | convolution fusion | flops 11556421632 | bytes 20643840 | tf_op jit(solution)/shard_map/rd,rf->df/dot_general | solution.py:730
  690.9 20.1 %bitcast_convert_fusion = bf16[2304,2304]{1,0:T(8,128)(2,1)} fusion(bf16[2,544,2304]{2,1,0:T(8,128)(2,1)} %get-tuple-element.35, bf16[2,544,2304]{2,1,0:T(8,128)(2,1)} %get-tuple-element.37), kind=kOutput, calls=%fused_computation | convolution fusion | flops 11556421632 | bytes 20643840 | tf_op jit(solution)/shard_map/rd,rf->df/dot_general | solution.py:731
  710.9 20.3 %bitcast_convert_fusion.2 = bf16[2304,2304]{1,0:T(8,128)(2,1)} fusion(bf16[2,544,2304]{2,1,0:T(8,128)(2,1)} %get-tuple-element.33, bf16[2,544,2304]{2,1,0:T(8,128)(2,1)} %get-tuple-element.34), kind=kOutput, calls=%fused_computation.2 | convolution fusion | flops 11556421632 | bytes 20643840 | tf_op jit(solution)/shard_map/rd,rf->df/dot_general | solution.py:729
  733.1 3.7 multiply_reduce_fusion.2
  736.9 8.8 fusion.17
  746.5 13.6 %bitcast_add_fusion.1 = (f32[1088,2304]{1,0:T(8,128)}, f32[1088,2304]{1,0:T(8,128)}) fusion(bf16[2,1,544,2304]{3,2,1,0:T(8,128)(2,1)} %param.11, f32[2304]{0:T(1024)S(1)} %copy-done.27, f32[1088]{0:T(1024)S(1)} %rsqrt.42, bf16[6,544,2304]{2,1,0:T(8,128)(2,1)} %get-tuple-element.32), kind=kLoop, calls=%fused_computation.33 | loop fusion | flops 12533760 | bytes 30094592 | tf_op jit(solution)/shard_map/add | solution.py:718
  760.1 8.7 fusion.14
  769.3 11.8 multiply_reduce_fusion
  781.9 6.8 multiply_convert_fusion
  788.7 2.3 copy-done.13
  790.9 4.6 convolution_convert_fusion.1
  795.6 16.6 %reduce-scatter.6.cloned.1.call-done = bf16[288,2304]{1,0:T(8,128)(2,1)} async-done(((bf16[2304,2304]{1,0:T(8,128)(2,1)}), bf16[288,2304]{1,0:T(8,128)(2,1)}) %reduce-scatter.6.cloned.1.call-update) | async-done | bytes 1327120 | tf_op jit(solution)/shard_map/reduce_scatter | solution.py:725
  812.2 3.0 convert_bitcast_fusion
  815.2 5.9 convolution_convert_fusion.5
  823.4 12.1 fusion.21
  835.6 8.4 fusion.27
  845.8 12.5 %multiply_reduce_fusion.5 = (f32[1088]{0:T(1024)S(1)}, f32[1088]{0:T(1024)S(1)}, f32[1088,2112]{1,0:T(8,128)}) fusion(f32[1088]{0:T(1024)S(1)} %log_add_fusion.1, f32[1088,2112]{1,0:T(8,128)} %copy-done.11, s32[1088]{0:T(1024)S(1)} %copy-done.35, s32[2112]{0:T(1024)S(1)} %copy-done.39, s32[1088]{0:T(1024)S(1)} %copy-done.44, s32[1088]{0:T(1024)S(1)} %copy-done.42, ...), kind=kOutput, calls=%fused_computation.45 | convolution fusion | flops 1217726464 | bytes 38451456 | tf_op jit(solution)/shard_map/rd,kd->rk/dot_general | solution.py:761
  858.3 15.3 %multiply_convert_fusion.4 = (bf16[1088,2112]{1,0:T(8,128)(2,1)}, bf16[1088,2112]{1,0:T(8,128)(2,1)S(1)}) fusion(f32[1088,2112]{1,0:T(8,128)} %copy-done.11, f32[1088,2112]{1,0:T(8,128)} %get-tuple-element.126, f32[1088]{0:T(1024)S(1)} %get-tuple-element.88, f32[1088]{0:T(1024)S(1)} %log_add_fusion.1, s32[1088]{0:T(1024)S(1)} %copy-done.35, ...), kind=kLoop, calls=%fused_computation.44 | loop fusion | flops 62042112 | bytes 46004480 | tf_op jit(solution)/shard_map/convert_element_type | solution.py:765
  873.6 4.0 convolution_bitcast_fusion.1
  888.0 19.1 %reduce-scatter.10.cloned.1.call-done = bf16[288,2304]{1,0:T(8,128)(2,1)} async-done(((bf16[2304,2304]{1,0:T(8,128)(2,1)}), bf16[288,2304]{1,0:T(8,128)(2,1)}) %reduce-scatter.10.cloned.1.call-update) | async-done | bytes 1327120 | tf_op jit(solution)/shard_map/reduce_scatter | solution.py:725
  907.1 3.0 convert_element_type.233
  910.1 83.0 %reduce-scatter.8.cloned.1.call-done = bf16[288,2304]{1,0:T(8,128)(2,1)} async-done(((bf16[2304,2304]{1,0:T(8,128)(2,1)}), bf16[288,2304]{1,0:T(8,128)(2,1)}) %reduce-scatter.8.cloned.1.call-update) | async-done | bytes 1327120 | tf_op jit(solution)/shard_map/reduce_scatter | solution.py:725
  993.1 3.0 convert_element_type.229
  996.1 4.8 fusion.39
  1000.9 7.6 convolution_convert_fusion.2
  1010.6 3.7 fusion.53
  1014.3 3.7 fusion.52
  1018.1 1.8 convolution_convert_fusion.4
  1020.0 3.0 convolution_add_fusion.1
  1023.0 5.1 fusion.6.x_ref
  1028.1 2.8 convolution_convert_fusion.3
  1030.9 136.2 %shard_map.187 = bf16[1088,2304]{1,0:T(8,128)(2,1)S(1)} custom-call(bf16[1088,2304]{1,0:T(8,128)(2,1)} %fusion.6.x_ref), custom_call_target="tpu_custom_call" | custom-call | flops 2506752 | bytes 209715200 | tf_op jit(solution)/shard_map/pallas_call | solution.py:127
  1167.2 3.9 fusion.15
  1171.5 5.0 fusion.20
  1176.5 1.8 convert_element_type.237
  1178.4 15.5 %fusion.10 = f32[1088,2304]{1,0:T(8,128)} fusion(f32[1088,2304]{1,0:T(8,128)} %copy-done.2, bf16[1088,2304]{1,0:T(8,128)(2,1)} %copy-done, f32[1088]{0:T(1024)S(1)} %broadcast_multiply_fusion.1, f32[2304]{0:T(1024)S(1)} %copy-done.29, f32[1088]{0:T(1024)S(1)} %copy-done.31, f32[2,1,544,2304]{3,2,0,1:T(8,128)} %bitcast_convert_fusion.3), kind=kLoop, calls=%fused_computation.23 | loop fusion | flops 17547264 | bytes 35112448 | tf_op jit(solution)/shard_map/add | solution.py:832
  1193.9 37.9 %reduce-scatter.12.cloned.1.call-done = bf16[288,1152]{1,0:T(8,128)(2,1)} async-done(((bf16[2304,1152]{1,0:T(8,128)(2,1)}), bf16[288,1152]{1,0:T(8,128)(2,1)}) %reduce-scatter.12.cloned.1.call-update) | async-done | bytes 663568 | tf_op jit(solution)/shard_map/reduce_scatter | solution.py:725
  1233.7 1.8 slice.177
  1235.6 1.8 fusion.82
  1237.4 5.0 copy.74
  (260 shorter events, 36.9 us)
Async XLA Ops:
  7.2 47.4 %all-gather.6.cloned.1.call-start = ((), (), s32[]{:S(2)}) async-start(), calls=%async_computation.5 | async-start | bytes 5971968 | tf_op jit(solution)/shard_map/all_gather | solution.py:643
  10.1 126.3 %all-gather.8.cloned.1.call-start = ((), (), s32[]{:S(2)}) async-start(), calls=%async_computation.6 | async-start | bytes 2654208 | tf_op jit(solution)/shard_map/all_gather | solution.py:648
  10.8 148.0 %all-gather.10.cloned.1.call-start = ((), (), s32[]{:S(2)}) async-start(), calls=%async_computation.7 | async-start | bytes 11943936 | tf_op jit(solution)/shard_map/all_gather | solution.py:649
  11.6 212.9 %all-gather.12.cloned.1.call-start = ((), (), s32[]{:S(2)}) async-start(), calls=%async_computation.8 | async-start | bytes 11943936 | tf_op jit(solution)/shard_map/all_gather | solution.py:650
  12.1 277.8 %all-gather.14.cloned.1.call-start = ((), (), s32[]{:S(2)}) async-start(), calls=%async_computation.9 | async-start | bytes 11943936 | tf_op jit(solution)/shard_map/all_gather | solution.py:651
  12.7 799.4 %reduce-scatter.6.cloned.1.call-start = ((), (), s32[]{:S(2)}) async-start(), calls=%async_computation.10 | async-start | bytes 11943936 | tf_op jit(solution)/shard_map/reduce_scatter | solution.py:725
  16.7 4.9 copy-start.59
  21.6 110.0 %copy-start.34 = (s32[1088]{0:T(1024)}, s32[1088]{0:T(1024)S(1)}, u32[]{:S(2)}) copy-start(s32[1088]{0:T(1024)S(1)} %le.16) | copy-start | bytes 13060
  21.9 39.6 %copy-start.30 = (f32[1088]{0:T(1024)}, f32[1088]{0:T(1024)S(1)}, u32[]{:S(2)}) copy-start(f32[1088]{0:T(1024)S(1)} %rsqrt.38) | copy-start | bytes 13060
  21.9 109.6 %copy-start.36 = (s32[2112]{0:T(1024)}, s32[2112]{0:T(1024)S(1)}, u32[]{:S(2)}) copy-start(s32[2112]{0:T(1024)S(1)} %get-tuple-element.127) | copy-start | bytes 25348
  22.0 109.6 %copy-start.38 = (s32[2112]{0:T(1024)}, s32[2112]{0:T(1024)S(1)}, u32[]{:S(2)}) copy-start(s32[2112]{0:T(1024)S(1)} %get-tuple-element.128) | copy-start | bytes 25348
  22.0 109.6 %copy-start.41 = (s32[1088]{0:T(1024)}, s32[1088]{0:T(1024)S(1)}, u32[]{:S(2)}) copy-start(s32[1088]{0:T(1024)S(1)} %get-tuple-element.119) | copy-start | bytes 13060
  22.0 109.6 %copy-start.43 = (s32[1088]{0:T(1024)}, s32[1088]{0:T(1024)S(1)}, u32[]{:S(2)}) copy-start(s32[1088]{0:T(1024)S(1)} %get-tuple-element.120) | copy-start | bytes 13060
  56.8 24.8 %copy-start.28 = (f32[2304]{0:T(1024)}, f32[2304]{0:T(1024)S(1)}, u32[]{:S(2)}) copy-start(f32[2304]{0:T(1024)S(1)} %get-tuple-element.94) | copy-start | bytes 27652
  64.3 67.3 %copy-start.32 = (bf16[2,32,256]{2,1,0:T(8,128)(2,1)}, bf16[2,32,256]{2,1,0:T(8,128)(2,1)S(1)}, u32[]{:S(2)}) copy-start(bf16[2,32,256]{2,1,0:T(8,128)(2,1)S(1)} %slice.163) | copy-start | bytes 98308
  71.3 16.9 %copy-start.7 = (f32[1088,256]{1,0:T(8,128)}, f32[1088,256]{1,0:T(8,128)S(1)}, u32[]{:S(2)}) copy-start(f32[1088,256]{1,0:T(8,128)S(1)} %get-tuple-element.116) | copy-start | bytes 3342340
  71.3 16.9 %copy-start.9 = (f32[1088,256]{1,0:T(8,128)}, f32[1088,256]{1,0:T(8,128)S(1)}, u32[]{:S(2)}) copy-start(f32[1088,256]{1,0:T(8,128)S(1)} %get-tuple-element.115) | copy-start | bytes 3342340
  71.4 46.1 %copy-start.53 = (bf16[2,32,256]{2,1,0:T(8,128)(2,1)}, bf16[2,32,256]{2,1,0:T(8,128)(2,1)S(1)}, u32[]{:S(2)}) copy-start(bf16[2,32,256]{2,1,0:T(8,128)(2,1)S(1)} %slice.162) | copy-start | bytes 98308
  80.0 5.3 copy-start.17
  80.0 33.1 %collective-permute-start = (bf16[2,512,512]{2,1,0:T(8,128)(2,1)S(1)}, bf16[2,512,512]{2,1,0:T(8,128)(2,1)S(1)}, u32[]{:S(2)}, u32[]{:S(2)}) collective-permute-start(bf16[2,512,512]{2,1,0:T(8,128)(2,1)S(1)} %pad_maximum_fusion.9), channel_id=1, source_target_pairs={{0,4},{4,0},{1,5},{5,1},{2,6},{6,2},{3,7},{7,3},{8,12},{12,8},{9,1... | collective-permute-start | bytes 3145736 | tf_op jit(solution)/shard_map/ppermute | solution.py:669
  88.8 28.6 %copy-start.23 = (bf16[1088,2,256]{2,0,1:T(8,128)(2,1)}, bf16[1088,2,256]{2,0,1:T(8,128)(2,1)S(1)}, u32[]{:S(2)}) copy-start(bf16[1088,2,256]{2,0,1:T(8,128)(2,1)S(1)} %fusion.37) | copy-start | bytes 3342340
  113.7 18.0 %copy-start.15 = (bf16[2,1024,256]{2,1,0:T(8,128)(2,1)}, bf16[2,1024,256]{2,1,0:T(8,128)(2,1)S(1)}, u32[]{:S(2)}) copy-start(bf16[2,1024,256]{2,1,0:T(8,128)(2,1)S(1)} %get-tuple-element.102) | copy-start | bytes 3145732
  117.4 14.2 %copy-start.11 = (f32[1088,2112]{1,0:T(8,128)}, f32[1088,2112]{1,0:T(8,128)S(1)}, u32[]{:S(2)}) copy-start(f32[1088,2112]{1,0:T(8,128)S(1)} %get-tuple-element.124) | copy-start | bytes 27574276
  117.4 14.2 %copy-start.55 = (f32[1088]{0:T(1024)}, f32[1088]{0:T(1024)S(1)}, u32[]{:S(2)}) copy-start(f32[1088]{0:T(1024)S(1)} %get-tuple-element.123) | copy-start | bytes 13060
  123.5 8.0 copy-start.4
  123.5 8.0 copy-start.49
  123.5 8.1 copy-start.57
  136.3 7.5 copy-start.19
  667.0 5.5 copy-start.60
  667.0 7.2 copy-start.61
  731.3 175.9 %reduce-scatter.10.cloned.1.call-start = ((), (), s32[]{:S(2)}) async-start(), calls=%async_computation.12 | async-start | bytes 11943936 | tf_op jit(solution)/shard_map/reduce_scatter | solution.py:725
  732.1 261.1 %reduce-scatter.8.cloned.1.call-start = ((), (), s32[]{:S(2)}) async-start(), calls=%async_computation.11 | async-start | bytes 11943936 | tf_op jit(solution)/shard_map/reduce_scatter | solution.py:725
  732.8 4.1 copy-start.27
  732.8 443.7 %reduce-scatter.14.cloned.1.call-start = ((), (), s32[]{:S(2)}) async-start(), calls=%async_computation.14 | async-start | bytes 2654208 | tf_op jit(solution)/shard_map/reduce_scatter | solution.py:725
  736.9 8.9 copy-start.45
  746.5 13.6 %copy-start.40 = (f32[2304]{0:T(1024)S(1)}, f32[2304]{0:T(1024)}, u32[]{:S(2)}) copy-start(f32[2304]{0:T(1024)} %get-tuple-element.92) | copy-start | bytes 27652
  760.1 9.3 copy-start.3
  781.2 7.4 copy-start.2
  781.9 9.1 copy-start.20
  795.6 436.2 %reduce-scatter.12.cloned.1.call-start = ((), (), s32[]{:S(2)}) async-start(), calls=%async_computation.13 | async-start | bytes 5971968 | tf_op jit(solution)/shard_map/reduce_scatter | solution.py:725
  823.3 12.2 copy-start.22
  823.4 22.3 %slice-start.3 = ((s8[9469952]{0:T(1024)(128)(4,1)}), s8[4194304]{0:T(1024)(128)(4,1)S(1)}, s32[]{:S(2)}) async-start(s8[9469952]{0:T(1024)(128)(4,1)} %bitcast.159), calls=%async_computation.18 | async-start | bytes 8388608
  823.4 22.3 %slice-start.4 = ((s8[9469952]{0:T(1024)(128)(4,1)}), s8[4194304]{0:T(1024)(128)(4,1)S(1)}, s32[]{:S(2)}) async-start(s8[9469952]{0:T(1024)(128)(4,1)} %bitcast.159), calls=%async_computation.19 | async-start | bytes 8388608
  835.6 8.6 copy-start.16
  835.6 8.6 copy-start.33
  835.6 10.2 slice-start.5
  858.3 15.3 %copy-start.26 = (bf16[2,1024,256]{2,1,0:T(8,128)(2,1)S(1)}, bf16[2,1024,256]{2,1,0:T(8,128)(2,1)}, u32[]{:S(2)}) copy-start(bf16[2,1024,256]{2,1,0:T(8,128)(2,1)} %copy-done.25) | copy-start | bytes 3145732
  858.3 15.3 %copy-start.54 = (bf16[2,32,256]{2,1,0:T(8,128)(2,1)S(1)}, bf16[2,32,256]{2,1,0:T(8,128)(2,1)}, u32[]{:S(2)}) copy-start(bf16[2,32,256]{2,1,0:T(8,128)(2,1)} %copy-done.53) | copy-start | bytes 98308
  873.6 4.1 slice-start.10
  873.6 4.1 copy-start.24
  873.6 4.1 slice-start.11
  884.2 124.4 %collective-permute-start.1 = (bf16[2,512,512]{2,1,0:T(8,128)(2,1)}, bf16[2,512,512]{2,1,0:T(8,128)(2,1)}, u32[]{:S(2)}, u32[]{:S(2)}) collective-permute-start(bf16[2,512,512]{2,1,0:T(8,128)(2,1)} %select_convert_fusion), channel_id=1, source_target_pairs={{0,4},{4,0},{1,5},{5,1},{2,6},{6,2},{3,7},{7,3},{8,12},{12,8},{9,1... | collective-permute-start | bytes 3145736 | tf_op jit(solution)/shard_map/ppermute | solution.py:788
  888.0 108.1 %copy-start.21 = (bf16[1088,2,256]{0,2,1:T(8,128)(2,1)S(1)}, bf16[1088,2,256]{0,2,1:T(8,128)(2,1)}, u32[]{:S(2)}) copy-start(bf16[1088,2,256]{0,2,1:T(8,128)(2,1)} %copy.50) | copy-start | bytes 3342340
  1000.9 7.6 copy-start.6
  1010.3 7.7 slice-start.6
  1010.5 7.5 slice-start.7
  1018.1 10.0 slice-start.8
  1019.9 8.1 slice-start.9
  1028.1 139.0 %slice-start = ((s8[10027008]{0:T(1024)(128)(4,1)}), s8[4194304]{0:T(1024)(128)(4,1)S(1)}, s32[]{:S(2)}) async-start(s8[10027008]{0:T(1024)(128)(4,1)} %bitcast.153), calls=%async_computation.15 | async-start | bytes 8388608
  1028.1 139.0 %slice-start.1 = ((s8[10027008]{0:T(1024)(128)(4,1)}), s8[4194304]{0:T(1024)(128)(4,1)S(1)}, s32[]{:S(2)}) async-start(s8[10027008]{0:T(1024)(128)(4,1)} %bitcast.153), calls=%async_computation.16 | async-start | bytes 8388608
  1030.9 136.2 %slice-start.2 = ((s8[10027008]{0:T(1024)(128)(4,1)}), s8[1638400]{0:T(1024)(128)(4,1)S(1)}, s32[]{:S(2)}) async-start(s8[10027008]{0:T(1024)(128)(4,1)} %bitcast.153), calls=%async_computation.17 | async-start | bytes 3276800
  1030.9 136.2 %copy-start.29 = (f32[2304]{0:T(1024)S(1)}, f32[2304]{0:T(1024)}, u32[]{:S(2)}) copy-start(f32[2304]{0:T(1024)} %copy-done.28) | copy-start | bytes 27652
  1030.9 136.3 %copy-start.31 = (f32[1088]{0:T(1024)S(1)}, f32[1088]{0:T(1024)}, u32[]{:S(2)}) copy-start(f32[1088]{0:T(1024)} %copy-done.30) | copy-start | bytes 13060
  1167.1 4.0 copy-start
  (23 other events, 57.0 us)
Sparse Core Ops, SparseCore 0:
  10.5 44.0 all-gather.5
  56.5 30.0 all-gather.7
  88.4 70.3 all-gather.9
  160.6 63.7 all-gather.11
  226.2 63.7 all-gather.13
  731.4 80.7 reduce-scatter.5
  815.7 91.4 reduce-scatter.9
  910.7 82.4 reduce-scatter.7
  996.5 42.4 reduce-scatter.13
  1176.6 55.1 reduce-scatter.11

commit v5 on v4

--- a/solution.py
+++ b/solution.py
@@ -150,8 +150,16 @@
     return place, down, up, place == 0, place == size - 1
 
 
-def greet_line(down, up, first, last):
+def plane_partners():
+    dp, seq, place = (lax.axis_index(name) for name in ("dp", "seq", "tensor"))
+    x, core = dp // 2, lax.rem(dp, 2)
+    return ((1 - x) * 2 + core, seq, place), (dp, 1 - seq, place), (x * 2 + 1 - core, seq, place)
+
+
+def greet_line(down, up, first, last, others=()):
     barrier = pltpu.get_barrier_semaphore()
+    for partner in others:
+        pl.semaphore_signal(barrier, inc=1, device_id=partner, device_id_type=MESH)
 
     @pl.when(jnp.logical_not(first))
     def _():
@@ -161,7 +169,7 @@
     def _():
         pl.semaphore_signal(barrier, inc=1, device_id=up, device_id_type=MESH)
 
-    pl.semaphore_wait(barrier, 2 - first.astype(jnp.int32) - last.astype(jnp.int32))
+    pl.semaphore_wait(barrier, 2 + len(others) - first.astype(jnp.int32) - last.astype(jnp.int32))
 
 
 def gelu_parts(gate):
@@ -173,19 +181,12 @@
     return gate * half, half + rise
 
 
-def ffn_kernel(
-    size, width, bases, schedule,
-    part_ref, token_ref, cot_ref, gate_ref, up_ref, down_ref, gain_ref,
-    sum_ref, out_ref, ffn_in_ref, hidden_ref, d_ffn_ref, d_gate_ref, d_up_ref, gain_grad_ref,
-    parts, landing, act_a, act_b, stage_t, stage_a, stage_f, stage_c, cols, rows_w,
-    pass_in, pass_out, share_in, share_out, local_done, col_sem, row_sem, io_sem,
-):
-    micro, rows, depth = parts.shape
-    units = gate_ref.shape[1]
+def line_stream(size, width, bases, parts, landing, sum_ref, sems, spot):
+    place, down, up, first, last = spot
+    pass_in, pass_out, share_in, share_out, local_done = sems
+    _, rows, depth = parts.shape
     half = rows // 2
     chunks = depth // width
-    place, down, up, first, last = chain_place(size)
-    greet_line(down, up, first, last)
 
     def side(which):
         toward, back = ((down, up), (up, down))[which]
@@ -196,7 +197,7 @@
         def where_at(u):
             q = jnp.int32(0)
             base = jnp.int32(bases[0])
-            for k in range(1, STAGES):
+            for k in range(1, len(bases)):
                 past = (u >= bases[k]).astype(jnp.int32)
                 q = q + past
                 base = base + past * (bases[k] - bases[k - 1])
@@ -294,10 +295,38 @@
         for one in sides:
             one[3](q)
 
+    def shared():
+        @pl.loop(0, len(bases))
+        def _(q):
+            for one in sides:
+                one[4](q)
+
     def ticks(low, high):
         @pl.loop(low, high)
         def _(s):
             tick(s)
+
+    return tick, ticks, settle, sent, shared
+
+
+def ffn_kernel(
+    size, width, bases, schedule, gather,
+    part_ref, token_ref, cot_ref, gate_ref, up_own, down_own, gain_ref,
+    sum_ref, out_ref, ffn_in_ref, hidden_ref, d_ffn_ref, d_attn_ref, d_middle_ref,
+    grad_gate_ref, grad_up_ref, grad_down_ref, full_ref, gain_grad_ref,
+    parts, landing, act_a, act_b, stage, cols, rows_w,
+    pass_in, pass_out, share_in, share_out, local_done, col_sem, row_sem, io_sem, gather_in, gather_out, own_done,
+):
+    micro, rows, depth = parts.shape
+    units = gate_ref.shape[1]
+    stage_t, stage_a, stage_f, stage_c = (stage.at[pl.ds(k * rows, rows)] for k in range(4))
+    up_ref, down_ref = (full_ref.at[0], full_ref.at[1]) if gather else (up_own, down_own)
+    spot = place, down, up, first, last = chain_place(size)
+    greet_line(down, up, first, last, plane_partners() if gather else ())
+
+    tick, ticks, settle, sent, shared = line_stream(
+        size, width, bases, parts, landing, sum_ref,
+        (pass_in, pass_out, share_in, share_out, local_done), spot)
 
     def col_copy(kind, source, i, slot):
         return pltpu.make_async_copy(
@@ -343,6 +372,9 @@
                 body(pl.ds(pl.multiple_of(b * BLOCK, BLOCK), BLOCK))
             tick(s)
 
+    def own_rows(m):
+        return pl.ds(m * rows, rows)
+
     def gain(k):
         return gain_ref[k : k + 1, :]
 
@@ -352,8 +384,6 @@
     def middle_of(span):
         attn = stage_a[span, :].astype(jnp.float32)
         return stage_t[span, :].astype(jnp.float32) + attn * inverse(attn) * gain(1)
-
-    forward = ((gate_ref, up_ref), (down_ref,))
 
     def norm_before(m, clock):
         def body(span):
@@ -368,8 +398,8 @@
             up_val = jnp.dot(stage_f[...], cols[1, slot], preferred_element_type=jnp.float32)
             active, slope = gelu_parts(gate)
             stage_c[:, at] = (active * up_val).astype(jnp.bfloat16)
-            act_a[m, :, at] = active.astype(jnp.bfloat16)
-            act_b[m, :, at] = (up_val * slope).astype(jnp.bfloat16)
+            act_a[own_rows(m), at] = active.astype(jnp.bfloat16)
+            act_b[own_rows(m), at] = (up_val * slope).astype(jnp.bfloat16)
         tiles(col_copy, (gate_ref, up_ref), units // TILE, body, clock)
 
     def down_proj(m, clock):
@@ -391,95 +421,296 @@
             d_ffn = inv * (scaled - normed * jnp.mean(scaled * normed, axis=-1, keepdims=True))
             stage_c[span, :] = d_ffn.astype(jnp.bfloat16)
             term = above * normed
-            gain_grad_ref[...] += term[:8] + term[8:]
+            gain_grad_ref[16:24, :] += term[:8] + term[8:]
         row_blocks(body, clock)
 
     def d_hidden(m, clock):
         def body(i, slot):
             at = span_of(i)
             d_hid = jnp.dot(stage_c[...], cols[0, slot], preferred_element_type=jnp.float32)
-            act_a[m, :, at] = (d_hid * act_a[m, :, at].astype(jnp.float32)).astype(jnp.bfloat16)
-            act_b[m, :, at] = (d_hid * act_b[m, :, at].astype(jnp.float32)).astype(jnp.bfloat16)
+            mine = own_rows(m)
+            act_a[mine, at] = (d_hid * act_a[mine, at].astype(jnp.float32)).astype(jnp.bfloat16)
+            act_b[mine, at] = (d_hid * act_b[mine, at].astype(jnp.float32)).astype(jnp.bfloat16)
         tiles(col_copy, (down_ref,), units // TILE, body, clock)
 
     def d_input(m, clock):
         def body(i, slot):
             dims = (((1,), (1,)), ((), ()))
             parts[m, :, span_of(i)] = (
-                lax.dot_general(act_b[m], rows_w[0, slot], dims, preferred_element_type=jnp.float32)
-                + lax.dot_general(act_a[m], rows_w[1, slot], dims, preferred_element_type=jnp.float32)
+                lax.dot_general(act_b[own_rows(m), :], rows_w[0, slot], dims, preferred_element_type=jnp.float32)
+                + lax.dot_general(act_a[own_rows(m), :], rows_w[1, slot], dims, preferred_element_type=jnp.float32)
             ).astype(jnp.bfloat16)
         tiles(row_copy, (gate_ref, up_ref), depth // TILE, body, clock)
 
+    def norm_back_middle(m, clock):
+        def body(span):
+            attn = stage_a[span, :].astype(jnp.float32)
+            attn_inv = inverse(attn)
+            attn_normed = attn * attn_inv
+            middle = stage_t[span, :].astype(jnp.float32) + attn_normed * gain(1)
+            inv = inverse(middle)
+            normed = middle * inv
+            below = stage_f[span, :].astype(jnp.float32)
+            scaled = below * gain(2)
+            d_middle = stage_c[span, :].astype(jnp.float32) + inv * (
+                scaled - normed * jnp.mean(scaled * normed, axis=-1, keepdims=True))
+            term = below * normed
+            gain_grad_ref[8:16, :] += term[:8] + term[8:]
+            stage_c[span, :] = d_middle.astype(jnp.bfloat16)
+            scaled = d_middle * gain(1)
+            d_attn = attn_inv * (scaled - attn_normed * jnp.mean(scaled * attn_normed, axis=-1, keepdims=True))
+            stage_f[span, :] = d_attn.astype(jnp.bfloat16)
+            term = d_middle * attn_normed
+            gain_grad_ref[0:8, :] += term[:8] + term[8:]
+        row_blocks(body, clock)
+
+    def tall_copy(source, i, slot, m):
+        return pltpu.make_async_copy(
+            source.at[m, :, span_of(i)], cols.at[0, slot, own_rows(m)], col_sem.at[m, slot])
+
+    def weight_grads(source, pairs, steps, clock):
+        def put(kind, target, i, slot):
+            return pltpu.make_async_copy(rows_w.at[kind, slot], target.at[span_of(i)], row_sem.at[kind, slot])
+
+        @pl.loop(0, steps)
+        def _(i):
+            slot = lax.rem(i, 2)
+
+            @pl.when(i + 1 < steps)
+            def _():
+                for m in range(micro):
+                    tall_copy(source, i + 1, 1 - slot, m).start()
+
+            for m in range(micro):
+                tall_copy(source, i, slot, m).wait()
+
+            @pl.when(i >= 2)
+            def _():
+                for kind, (_, target) in enumerate(pairs):
+                    put(kind, target, i - 2, slot).wait()
+
+            left = cols[0, slot, : micro * rows, :]
+            for kind, (right, target) in enumerate(pairs):
+                for low in range(0, units, 3 * TILE):
+                    high = min(units, low + 3 * TILE)
+                    rows_w[kind, slot, :, low:high] = lax.dot_general(
+                        left, right[: micro * rows, low:high], (((0,), (0,)), ((), ())),
+                        preferred_element_type=jnp.float32).astype(jnp.bfloat16)
+                put(kind, target, i, slot).start()
+            tick(clock + i)
+
+        for i in (steps - 2, steps - 1):
+            for kind, (_, target) in enumerate(pairs):
+                put(kind, target, i, i % 2).wait()
+
+    if gather:
+        share = up_own.shape[0]
+        piece = share // 2
+        dp, seq, _ = (lax.axis_index(name) for name in ("dp", "seq", "tensor"))
+        x, core = dp // 2, lax.rem(dp, 2)
+        over_x, over_y, over_core = plane_partners()
+
+        def block(dx, dy, dc, u):
+            nx, ny, nc = (jnp.abs(now - flip) for now, flip in ((x, dx), (seq, dy), (core, dc)))
+            row = ((nx * 2 + nc) * 2 + ny) * share + (u % 2) * piece
+            return pl.ds(pl.multiple_of(row, 16), piece)
+
+        left_half, right_half = pl.ds(0, units // 2), pl.ds(units // 2, units // 2)
+        everything = pl.ds(0, units)
+
+        def view(u, dx, dy, dc, across=everything):
+            return full_ref.at[u // 2, block(dx, dy, dc, u), across]
+
+        def own(u):
+            return (up_own, down_own)[u // 2].at[pl.ds((u % 2) * piece, piece)]
+
+        def hop(u, kind, source, target, device):
+            return pltpu.make_async_remote_copy(
+                source, target, gather_out.at[u, kind], gather_in.at[u, kind],
+                device_id=device, device_id_type=MESH)
+
+        routes = (
+            ((0, 0, 0), everything, over_x, (1, 0, 0)),
+            ((0, 0, 0), everything, over_y, (0, 1, 0)),
+            ((0, 0, 0), everything, over_core, (0, 0, 1)),
+            ((1, 0, 0), left_half, over_y, (1, 1, 0)),
+            ((0, 1, 0), right_half, over_x, (1, 1, 0)),
+            ((1, 0, 0), everything, over_core, (1, 0, 1)),
+            ((0, 1, 0), everything, over_core, (0, 1, 1)),
+            ((1, 1, 0), left_half, over_core, (1, 1, 1)),
+            ((1, 1, 0), right_half, over_core, (1, 1, 1)),
+        )
+
+        def send(u, kind):
+            at, across, device, _ = routes[kind]
+            source = own(u) if kind < 3 else view(u, *at, across)
+            hop(u, kind, source, view(u, *at, across), device).start()
+
+        def arrive(u, kind):
+            _, across, device, at = routes[kind]
+            target = view(u, *at, across)
+            hop(u, kind, target, target, device).wait_recv()
+
+        def own_copy(u):
+            return pltpu.make_async_copy(own(u), view(u, 0, 0, 0), own_done.at[u])
+
+        def gather_first(u):
+            for kind in (0, 1, 2):
+                send(u, kind)
+            own_copy(u).start()
+
+        def gather_second(u):
+            arrive(u, 0)
+            send(u, 3)
+            send(u, 5)
+            arrive(u, 1)
+            send(u, 4)
+            send(u, 6)
+
+        def gather_third(u):
+            arrive(u, 3)
+            send(u, 7)
+            arrive(u, 4)
+            send(u, 8)
+
+        def gather_last(u):
+            own_copy(u).wait()
+            for kind in (2, 5, 6, 7, 8):
+                arrive(u, kind)
+
+        def gather_sent():
+            for u in range(4):
+                for kind, (at, across, device, _) in enumerate(routes):
+                    source = view(u, *at, across)
+                    hop(u, kind, source, source, device).wait_send()
+
     gain_grad_ref[...] = jnp.zeros_like(gain_grad_ref)
-    for m in range(micro):
-        io(m, part_ref.at[m], parts.at[m]).start()
-    io(2, token_ref.at[0], stage_t).start()
-    prime(col_copy, (gate_ref, up_ref))
-    for m in range(micro):
-        io(m, part_ref.at[m], parts.at[m]).wait()
-    ticks(0, schedule["attn"][0])
+
+    def load(index, source, target):
+        return pltpu.make_async_copy(source, target, io_sem.at[index])
+
+    def bring(m, third=None, fourth=None):
+        found = [load(2, token_ref.at[m], stage_t), load(3, sum_ref.at[m], stage_a)]
+        if third is not None:
+            found += [load(4, third, stage_f), load(5, fourth, stage_c)]
+        return found
+
+    def start(copies):
+        for copy in copies:
+            copy.start()
+
+    def wait(copies):
+        for copy in copies:
+            copy.wait()
+
+    whole = schedule["attn"][0]
+    entry = [load(m, part_ref.at[m], parts.at[m]) for m in range(micro)]
+    start(entry)
+    if gather:
+        gather_first(0)
+        gather_first(1)
+    wait(entry)
+    if gather:
+        ticks(0, 7)
+        gather_second(0)
+        gather_first(2)
+        ticks(7, 14)
+        gather_second(1)
+        gather_third(0)
+        gather_first(3)
+        ticks(14, 21)
+        gather_second(2)
+        gather_third(1)
+        ticks(21, 28)
+        gather_second(3)
+        gather_third(2)
+        ticks(28, whole)
+    else:
+        ticks(0, whole)
+    kept = []
     for m in range(micro):
         norm_s, gate_s, down_s, end_s = schedule["forward"][m]
         settle(m)
-        io(3, sum_ref.at[m], stage_a).start()
-        if m:
-            io(2, token_ref.at[m], stage_t).start()
-            io(6, stage_f, ffn_in_ref.at[m - 1]).wait()
-            io(7, stage_c, hidden_ref.at[m - 1]).wait()
-        io(2, token_ref.at[m], stage_t).wait()
-        io(3, sum_ref.at[m], stage_a).wait()
+        wait(kept)
+        loads = bring(m)
+        start(loads)
+        wait(loads)
         norm_before(m, norm_s)
-        io(6, stage_f, ffn_in_ref.at[m]).start()
+        kept = [load(6, stage_f, ffn_in_ref.at[m]), load(7, stage_c, hidden_ref.at[m])]
+        kept[0].start()
+        if gather and m == 0:
+            gather_third(3)
+            gather_last(0)
+            gather_last(1)
+        if m == 0:
+            prime(col_copy, (gate_ref, up_ref))
+        gate_and_up(m, gate_s)
+        kept[1].start()
+        sent(m)
+        if gather and m == 0:
+            gather_last(2)
+            gather_last(3)
         prime(row_copy, (down_ref,))
-        gate_and_up(m, gate_s)
-        io(7, stage_c, hidden_ref.at[m]).start()
-        sent(m)
-        if m + 1 < micro:
-            prime(col_copy, (gate_ref, up_ref))
-        else:
-            prime(col_copy, (down_ref,))
-            io(2, token_ref.at[0], stage_t).start()
-            io(3, sum_ref.at[0], stage_a).start()
+        prime(col_copy, (gate_ref, up_ref) if m + 1 < micro else (down_ref,))
         down_proj(m, down_s)
         ticks(down_s + -(-depth // (TILE * PACE)), end_s)
-    io(6, stage_f, ffn_in_ref.at[micro - 1]).wait()
-    io(7, stage_c, hidden_ref.at[micro - 1]).wait()
+    wait(kept)
     for m in range(micro):
         norm_s, dh_s, di_s, end_s = schedule["backward"][m]
         settle(micro + m)
-        io(4, sum_ref.at[micro + m], stage_f).start()
-        io(5, cot_ref.at[m], stage_c).start()
-        io(2, token_ref.at[m], stage_t).wait()
-        io(3, sum_ref.at[m], stage_a).wait()
-        io(4, sum_ref.at[micro + m], stage_f).wait()
-        io(5, cot_ref.at[m], stage_c).wait()
+        if m:
+            wait(kept)
+        loads = bring(m, sum_ref.at[micro + m], cot_ref.at[m])
+        start(loads)
+        wait(loads)
         norm_after(m, norm_s)
-        io(6, stage_f, out_ref.at[m]).start()
-        io(7, stage_c, d_ffn_ref.at[m]).start()
+        kept = [load(6, stage_f, out_ref.at[m]), load(7, stage_c, d_ffn_ref.at[m])]
+        start(kept)
         prime(row_copy, (gate_ref, up_ref))
         d_hidden(m, dh_s)
-        io(8, act_b.at[m], d_gate_ref.at[m]).start()
-        io(9, act_a.at[m], d_up_ref.at[m]).start()
         sent(micro + m)
         if m + 1 < micro:
             prime(col_copy, (down_ref,))
-            io(2, token_ref.at[m + 1], stage_t).start()
-            io(3, sum_ref.at[m + 1], stage_a).start()
         d_input(m, di_s)
         ticks(di_s + -(-depth // (TILE * PACE)), end_s)
-        io(6, stage_f, out_ref.at[m]).wait()
-        io(7, stage_c, d_ffn_ref.at[m]).wait()
-        io(8, act_b.at[m], d_gate_ref.at[m]).wait()
-        io(9, act_a.at[m], d_up_ref.at[m]).wait()
-    for q in (STAGES - 2, STAGES - 1):
-        settle(q)
-        sent(q)
-
-    @pl.loop(0, STAGES)
-    def _(q):
-        for one in sides:
-            one[4](q)
+    wait(kept)
+    norm_s, grads_s, down_s, end_s = schedule["grads"]
+    settle(2 * micro)
+    loads = bring(0, sum_ref.at[2 * micro], cot_ref.at[0])
+    start(loads)
+    for m in range(micro):
+        tall_copy(ffn_in_ref, 0, 0, m).start()
+    wait(loads)
+    norm_back_middle(0, norm_s)
+    kept = [load(6, stage_f, d_attn_ref.at[0]), load(7, stage_c, d_middle_ref.at[0])]
+    start(kept)
+    hidden_loads = [load(2 + m, hidden_ref.at[m], stage.at[own_rows(m)]) for m in range(micro)]
+    start(hidden_loads)
+    steps = depth // TILE
+    weight_grads(ffn_in_ref, ((act_b, grad_gate_ref), (act_a, grad_up_ref)), steps, grads_s)
+    for m in range(micro):
+        tall_copy(d_ffn_ref, 0, 0, m).start()
+    wait(hidden_loads)
+    weight_grads(d_ffn_ref, ((stage, grad_down_ref),), steps, down_s)
+    wait(kept)
+    tail = bring(1, None)
+    tail.append(load(5, cot_ref.at[1], stage_c))
+    start(tail)
+    ticks(down_s + steps, end_s)
+    settle(2 * micro + 1)
+    tail.append(load(4, sum_ref.at[2 * micro + 1], stage_f))
+    tail[-1].start()
+    wait(tail)
+    norm_back_middle(1, end_s)
+    kept = [load(6, stage_f, d_attn_ref.at[1]), load(7, stage_c, d_middle_ref.at[1])]
+    start(kept)
+    sent(STAGES - 2)
+    sent(STAGES - 1)
+    if gather:
+        gather_sent()
+    wait(kept)
+
+    shared()
 
 
 def ffn_schedule(chunks, tiles, hops):
@@ -503,9 +734,11 @@
         bases.append(max(di_s, bases[-1] + chunks))
         at = max(di_s + tiles, bases[m + 3] + whole)
         backward.append((norm_s, dh_s, di_s, at))
-    last = backward[-1]
-    backward[-1] = last[:3] + (max(last[3], bases[-1] + whole),)
-    return tuple(bases), {"attn": attn, "forward": tuple(forward), "backward": tuple(backward)}
+    grads_s = at + 2
+    grads = (at, grads_s, grads_s + tiles, max(grads_s + 2 * tiles, bases[-1] + whole))
+    return tuple(bases), {
+        "attn": attn, "forward": tuple(forward), "backward": tuple(backward), "grads": grads
+    }
 
 
 def ffn_block(parts, tokens, cotangent, gate, up, down, gains, cid, width=128):
@@ -517,37 +750,315 @@
     bf16 = jnp.bfloat16
     any_spec = pl.BlockSpec(memory_space=pl.ANY)
     vmem_spec = pl.BlockSpec(memory_space=pltpu.VMEM)
+    gather = up.shape[0] != depth
     stack = jax.ShapeDtypeStruct((micro, rows, depth), bf16)
     wide = jax.ShapeDtypeStruct((micro, rows, units), bf16)
+    grad = jax.ShapeDtypeStruct((depth, units), bf16)
+    full = jax.ShapeDtypeStruct((2, depth, units) if gather else (2, 16, 128), bf16)
     dma = pltpu.SemaphoreType.DMA
-    flops = 2 * micro * rows * depth * units * 6
-    return pl.pallas_call(
-        functools.partial(ffn_kernel, size, width, bases, schedule),
+    flops = 2 * micro * rows * depth * units * 9
+    found = pl.pallas_call(
+        functools.partial(ffn_kernel, size, width, bases, schedule, gather),
         out_shape=(
             jax.ShapeDtypeStruct((STAGES, rows, depth), bf16),
-            stack, stack, wide, stack, wide, wide,
-            jax.ShapeDtypeStruct((8, depth), jnp.float32),
+            stack, stack, wide, stack, stack, stack, grad, grad, grad, full,
+            jax.ShapeDtypeStruct((24, depth), jnp.float32),
         ),
         in_specs=[any_spec] * 6 + [vmem_spec],
-        out_specs=(any_spec,) * 7 + (vmem_spec,),
+        out_specs=(any_spec,) * 11 + (vmem_spec,),
         scratch_shapes=[
             pltpu.VMEM((micro, rows, depth), bf16),
             pltpu.VMEM((2, STAGES, chunks, rows // 2, width), bf16),
-            pltpu.VMEM((micro, rows, units), bf16),
-            pltpu.VMEM((micro, rows, units), bf16),
-            pltpu.VMEM((rows, depth), bf16),
-            pltpu.VMEM((rows, depth), bf16),
-            pltpu.VMEM((rows, depth), bf16),
-            pltpu.VMEM((rows, depth), bf16),
+            pltpu.VMEM((micro * rows, units), bf16),
+            pltpu.VMEM((micro * rows, units), bf16),
+            pltpu.VMEM((4 * rows, depth), bf16),
             pltpu.VMEM((2, 2, depth, TILE), bf16),
             pltpu.VMEM((2, 2, TILE, units), bf16),
         ]
         + [dma((2, STAGES, chunks))] * 5
-        + [dma((2, 2)), dma((2, 2)), dma((10,))],
+        + [dma((2, 2)), dma((2, 2)), dma((8,)), dma((4, 9)), dma((4, 9)), dma((4,))],
         compiler_params=pltpu.CompilerParams(
             collective_id=cid, has_side_effects=True, vmem_limit_bytes=60 * 2**20),
-        cost_estimate=pl.CostEstimate(flops=flops, bytes_accessed=2**30, transcendentals=micro * rows * units),
+        cost_estimate=pl.CostEstimate(
+            flops=flops, bytes_accessed=2**30, transcendentals=micro * rows * units),
     )(parts, tokens, cotangent, gate, up, down, gains)
+    return {
+        "attn": found[0][:micro], "out": found[1], "d_attn": found[5], "d_middle": found[6],
+        "grad_gate": found[7], "grad_up": found[8], "grad_down": found[9], "gain_grad": found[11],
+        "sums": found[0], "ffn_in": found[2], "hidden": found[3], "d_ffn": found[4],
+    }
+
+SIDE_PAD = 128
+
+
+def tail_kernel(
+    size, width, bases,
+    part_ref, up_grad_ref, normed_ref, d_attn_ref, d_qkv_ref, context_ref, gain_ref,
+    sum_ref, up_share_ref, side_share_ref, gain_share_ref,
+    parts, landing, up_acc, side_acc, up_first, side_first, up_second, side_second, up_third, side_third,
+    cols, d_qkv, context, gain_in,
+    pass_in, pass_out, share_in, share_out, local_done, col_sem, io_sem, hop_in, hop_out, gain_got, gain_sent,
+):
+    micro, rows, depth = parts.shape
+    spot = place, down, up, first, last = chain_place(size)
+    over_x, over_y, over_core = plane_partners()
+    dp, seq = lax.axis_index("dp"), lax.axis_index("seq")
+    x, core = dp // 2, lax.rem(dp, 2)
+    others = [(dp, seq, lax.rem(place + k, size)) for k in range(1, size)]
+    greet_plane(over_x, over_y, over_core, others)
+    tick, ticks, settle, sent, shared = line_stream(
+        size, width, bases, parts, landing, sum_ref,
+        (pass_in, pass_out, share_in, share_out, local_done), spot)
+    share = up_share_ref.shape[0]
+    piece = share // 2
+    widths = (up_share_ref.shape[1], side_share_ref.shape[1])
+    qkv_width = d_qkv.shape[1]
+
+    def load(index, source, target):
+        return pltpu.make_async_copy(source, target, io_sem.at[index])
+
+    def halves(p):
+        all_columns = widths[p // 2]
+        low = -(-all_columns // 256) * 128
+        return (pl.ds(0, low), pl.ds(low, all_columns - low))
+
+    def block_rows(bx, by, bc, p):
+        return pl.ds(pl.multiple_of(((bx * 2 + bc) * 2 + by) * share + (p % 2) * piece, 16), piece)
+
+    def acc(p, bx, by, across):
+        if p < 2:
+            return up_acc.at[bx * 2 + by, pl.ds((p % 2) * piece, piece), across]
+        return side_acc.at[block_rows(bx, by, core, p), across]
+
+    def whole(p):
+        return pl.ds(0, widths[p // 2])
+
+    first_buf, second_buf, third_buf = (up_first, side_first), (up_second, side_second), (up_third, side_third)
+
+    def land(step, p, k, across):
+        buf = (first_buf, second_buf, third_buf)[step][p // 2]
+        return buf.at[p % 2, k, :, across]
+
+    def hop(p, k, source, target, device):
+        return pltpu.make_async_remote_copy(
+            source, target, hop_out.at[p, k], hop_in.at[p, k], device_id=device, device_id_type=MESH)
+
+    def hops(p):
+        left, right = halves(p)
+        found = []
+        for k in range(4):
+            bx, by = k // 2, k % 2
+            if p < 2:
+                source = up_grad_ref.at[block_rows(bx, by, 1 - core, p), :]
+            else:
+                source = side_acc.at[block_rows(bx, by, 1 - core, p), :]
+            found.append((source, land(0, p, k, whole(p)), over_core))
+        for k in range(2):
+            found.append((acc(p, 1 - x, k, left), land(1, p, k, left), over_x))
+        for k in range(2):
+            found.append((acc(p, k, 1 - seq, right), land(1, p, k, right), over_y))
+        found.append((acc(p, x, 1 - seq, left), land(2, p, 0, left), over_y))
+        found.append((acc(p, 1 - x, seq, right), land(2, p, 0, right), over_x))
+        return found
+
+    def go(p, k):
+        source, target, device = hops(p)[k]
+        hop(p, k, source, target, device).start()
+
+    def got(p, k):
+        _, target, device = hops(p)[k]
+        hop(p, k, target, target, device).wait_recv()
+        return target
+
+    def add(p, bx, by, across, arrived):
+        mine = acc(p, bx, by, across)
+
+        @pl.loop(0, piece // BLOCK)
+        def _(b):
+            span = pl.ds(pl.multiple_of(b * BLOCK, BLOCK), BLOCK)
+            mine[span, :] = (
+                mine[span, :].astype(jnp.float32) + arrived[span, :].astype(jnp.float32)
+            ).astype(jnp.bfloat16)
+
+    def scatter_first(p):
+        for k in range(4):
+            go(p, k)
+
+    def scatter_second(p):
+        for k in range(4):
+            add(p, k // 2, k % 2, whole(p), got(p, k))
+        for k in (4, 5, 6, 7):
+            go(p, k)
+
+    def scatter_third(p):
+        left, right = halves(p)
+        for k in range(2):
+            add(p, x, k, left, got(p, 4 + k))
+        go(p, 8)
+        for k in range(2):
+            add(p, k, seq, right, got(p, 6 + k))
+        go(p, 9)
+
+    def scatter_last(p):
+        left, right = halves(p)
+        add(p, x, seq, left, got(p, 8))
+        add(p, x, seq, right, got(p, 9))
+        put(p).start()
+
+    def put(p):
+        target = (up_share_ref, side_share_ref)[p // 2].at[pl.ds((p % 2) * piece, piece)]
+        return load(12 + p, acc(p, x, seq, whole(p)), target)
+
+    def scatter_sent(p):
+        for k, (source, target, device) in enumerate(hops(p)):
+            hop(p, k, source, target, device).wait_send()
+        put(p).wait()
+
+    def tile_copy(kind, i, slot):
+        source = (normed_ref, d_attn_ref)[kind].at[:, pl.ds(pl.multiple_of(i * TILE, TILE), TILE)]
+        return pltpu.make_async_copy(source, cols.at[kind, slot], col_sem.at[kind, slot])
+
+    def side_grads(clock):
+        steps = depth // TILE
+
+        @pl.loop(0, steps)
+        def _(i):
+            slot = lax.rem(i, 2)
+
+            @pl.when(i + 1 < steps)
+            def _():
+                tile_copy(0, i + 1, 1 - slot).start()
+                tile_copy(1, i + 1, 1 - slot).start()
+
+            tile_copy(0, i, slot).wait()
+            tile_copy(1, i, slot).wait()
+            span = pl.ds(pl.multiple_of(i * TILE, TILE), TILE)
+            for kind, right, low in ((0, d_qkv, 0), (1, context, qkv_width)):
+                side_acc[span, low : low + right.shape[1]] = lax.dot_general(
+                    cols[kind, slot], right[...], (((0,), (0,)), ((), ())),
+                    preferred_element_type=jnp.float32).astype(jnp.bfloat16)
+            tick(clock + i)
+
+    entry = [load(m, part_ref.at[m], parts.at[m]) for m in range(micro)]
+    up_loads = [
+        load(4 + k, up_grad_ref.at[pl.ds(pl.multiple_of(((k // 2 * 2 + core) * 2 + k % 2) * share, 16), share)], up_acc.at[k])
+        for k in range(4)
+    ]
+    side_loads = [
+        load(2, d_qkv_ref, d_qkv),
+        load(3, context_ref, context),
+        load(8, gain_ref, side_acc.at[:, pl.ds(widths[1] - SIDE_PAD, SIDE_PAD)]),
+    ]
+    for copy in entry:
+        copy.start()
+    scatter_first(0)
+    scatter_first(1)
+    for copy in side_loads + up_loads:
+        copy.start()
+    tile_copy(0, 0, 0).start()
+    tile_copy(1, 0, 0).start()
+    for copy in entry:
+        copy.wait()
+    ticks(0, 1)
+    for copy in side_loads + up_loads:
+        copy.wait()
+    side_grads(1)
+    clock = 1 + depth // TILE
+    scatter_first(2)
+    scatter_first(3)
+    plan = (
+        (0, (scatter_second, 0)), (1, (scatter_second, 1)), (3, (scatter_third, 0)), (3, (scatter_second, 2)),
+        (4, (scatter_last, 0)), (2, (scatter_second, 3)), (3, (scatter_third, 1)), (4, (scatter_last, 1)),
+        (3, (scatter_third, 2)), (4, (scatter_last, 2)), (3, (scatter_third, 3)), (4, (scatter_last, 3)),
+    )
+    for pause, (step, p) in plan:
+        if pause:
+            ticks(clock, clock + pause)
+            clock += pause
+        step(p)
+
+    mine = side_acc.at[pl.ds(pl.multiple_of(((x * 2 + core) * 2 + seq) * share, 16), share), pl.ds(widths[1] - SIDE_PAD, SIDE_PAD)]
+
+    def gain_hop(k):
+        return pltpu.make_async_remote_copy(
+            mine, gain_in.at[k], gain_sent.at[k], gain_got.at[k], device_id=others[k], device_id_type=MESH)
+
+    for k in range(size - 1):
+        gain_hop(k).start()
+    ticks(clock, clock + 2)
+    clock += 2
+    for k in range(size - 1):
+        gain_hop(k).wait_recv()
+    total = mine[...].astype(jnp.float32)
+    for k in range(size - 1):
+        total = total + gain_in[k].astype(jnp.float32)
+    gain_share_ref[...] = total
+    ticks(clock, max(clock, bases[-1] + depth // width + 2 * LAG * (size - 1)))
+    for q in range(micro):
+        settle(q)
+        sent(q)
+    shared()
+    for p in range(4):
+        scatter_sent(p)
+    for k in range(size - 1):
+        gain_hop(k).wait_send()
+
+
+def greet_plane(over_x, over_y, over_core, others):
+    barrier = pltpu.get_barrier_semaphore()
+    partners = (over_x, over_y, over_core, *others)
+    for partner in partners:
+        pl.semaphore_signal(barrier, inc=1, device_id=partner, device_id_type=MESH)
+    pl.semaphore_wait(barrier, len(partners))
+
+
+def tail_block(parts, up_grad, normed, d_attn, d_qkv, context, gain_cols, cid, width=128):
+    size = lax.axis_size("tensor")
+    micro, rows, depth = parts.shape
+    units = up_grad.shape[1]
+    chunks = depth // width
+    total = micro * rows
+    share = depth // (lax.axis_size("dp") * lax.axis_size("seq"))
+    piece = share // 2
+    side = d_qkv.shape[1] + context.shape[1] + SIDE_PAD
+    bases = (0, chunks)
+    bf16 = jnp.bfloat16
+    any_spec = pl.BlockSpec(memory_space=pl.ANY)
+    vmem_spec = pl.BlockSpec(memory_space=pltpu.VMEM)
+    dma = pltpu.SemaphoreType.DMA
+    return pl.pallas_call(
+        functools.partial(tail_kernel, size, width, bases),
+        out_shape=(
+            jax.ShapeDtypeStruct((micro, rows, depth), bf16),
+            jax.ShapeDtypeStruct((share, units), bf16),
+            jax.ShapeDtypeStruct((share, side), bf16),
+            jax.ShapeDtypeStruct((share, SIDE_PAD), jnp.float32),
+        ),
+        in_specs=[any_spec] * 7,
+        out_specs=(any_spec,) * 3 + (vmem_spec,),
+        scratch_shapes=[
+            pltpu.VMEM((micro, rows, depth), bf16),
+            pltpu.VMEM((2, 2, chunks, rows // 2, width), bf16),
+            pltpu.VMEM((4, share, units), bf16),
+            pltpu.VMEM((depth, side), bf16),
+            pltpu.VMEM((2, 4, piece, units), bf16),
+            pltpu.VMEM((2, 4, piece, side), bf16),
+            pltpu.VMEM((2, 2, piece, units), bf16),
+            pltpu.VMEM((2, 2, piece, side), bf16),
+            pltpu.VMEM((2, 1, piece, units), bf16),
+            pltpu.VMEM((2, 1, piece, side), bf16),
+            pltpu.VMEM((2, 2, total, TILE), bf16),
+            pltpu.VMEM(d_qkv.shape, bf16),
+            pltpu.VMEM(context.shape, bf16),
+            pltpu.VMEM((size - 1, share, SIDE_PAD), bf16),
+        ]
+        + [dma((2, 2, chunks))] * 5
+        + [dma((2, 2)), dma((16,)), dma((4, 10)), dma((4, 10)), dma((size - 1,)), dma((size - 1,))],
+        compiler_params=pltpu.CompilerParams(
+            collective_id=cid, has_side_effects=True, vmem_limit_bytes=60 * 2**20),
+        cost_estimate=pl.CostEstimate(
+            flops=2 * total * depth * side, bytes_accessed=400 * 2**20, transcendentals=0),
+    )(parts, up_grad, normed, d_attn, d_qkv, context, gain_cols)
 
 
 def normalize(values):
@@ -558,8 +1069,16 @@
     inverse = lax.rsqrt(jnp.mean(values * values, axis=-1, keepdims=True) + EPS)
     normed = values * inverse
     scaled = upstream * gain
-    backed = inverse * (scaled - normed * jnp.mean(scaled * normed, axis=-1, keepdims=True))
-    return (backed, jnp.sum(upstream * normed, axis=0))
+    return inverse * (scaled - normed * jnp.mean(scaled * normed, axis=-1, keepdims=True))
+
+
+def turn_back(values, places):
+    half_width = values.shape[-1] // 2
+    spectrum = THETA ** (-2.0 * jnp.arange(half_width, dtype=jnp.float32) / values.shape[-1])
+    angles = places.astype(jnp.float32)[..., None] * spectrum
+    angles = jnp.concatenate([angles, angles], axis=-1)[..., None, :]
+    turned = jnp.concatenate([values[..., half_width:], -values[..., :half_width]], axis=-1)
+    return values * jnp.cos(angles) + turned * jnp.sin(angles)
 
 
 def rotate(values, places):
@@ -626,42 +1145,40 @@
     prompt_all = prompt_dev * seq_count
     total_rows = micro_count * row_count
     score_scale = HEAD ** (-0.5)
+    axes = ("dp", "seq")
+    planar = lax.axis_size("dp") == 4 and seq_count == 2
+    query_width = query_weight.shape[1]
+    qkv_width = query_width + 2 * HEAD
+    f32, bf16 = jnp.float32, jnp.bfloat16
     visible, places = visibility(
         micro_count, row_count, prompt_dev, prompt_all, CONT, seq_pos, prompt_of[:, 0]
     )
-    axes = ("dp", "seq")
-    query_width = query_weight.shape[1]
     side_weights = jnp.concatenate(
         [
             query_weight,
             key_weight,
             value_weight,
-            jnp.pad(norm_gains.T, ((0, 0), (0, 128 - norm_gains.shape[0]))),
+            jnp.pad(norm_gains.T, ((0, 0), (0, SIDE_PAD - norm_gains.shape[0]))),
         ],
         axis=1,
     )
     full_side = lax.all_gather(side_weights, axes, axis=0, tiled=True)
-    full_query = full_side[:, :query_width]
-    full_key = full_side[:, query_width : query_width + HEAD]
-    full_value = full_side[:, query_width + HEAD : query_width + 2 * HEAD]
-    gain_rows = full_side[:, query_width + 2 * HEAD : query_width + 2 * HEAD + 4].T
+    full_qkv = full_side[:, :qkv_width]
+    gain_float = full_side[:, qkv_width : qkv_width + 4].T.astype(f32)
     full_out = lax.all_gather(out_weight, axes, axis=1, tiled=True)
     full_gate = lax.all_gather(gate_weight, axes, axis=0, tiled=True)
-    full_up = lax.all_gather(up_weight, axes, axis=0, tiled=True)
-    full_down = lax.all_gather(down_weight.T, axes, axis=0, tiled=True)
-    gain_float = gain_rows.astype(jnp.float32)
-    inputs = tokens.reshape(total_rows, model_width).astype(jnp.float32)
-    normed_in = (normalize(inputs) * gain_float[0]).astype(jnp.bfloat16)
-    query_heads = jnp.dot(normed_in, full_query, preferred_element_type=jnp.float32).reshape(
-        total_rows, -1, HEAD
-    )
-    key_heads = jnp.dot(normed_in, full_key, preferred_element_type=jnp.float32).reshape(
-        total_rows, 1, HEAD
-    )
-    value_raw = jnp.dot(normed_in, full_value, preferred_element_type=jnp.float32)
-    query_rows = rotate(query_heads, places).astype(jnp.bfloat16)
-    key_local = rotate(key_heads, places)[:, 0].astype(jnp.bfloat16)
-    value_local = value_raw.astype(jnp.bfloat16)
+    down_turned = down_weight.T
+    if planar:
+        full_up, full_down = up_weight, down_turned
+    else:
+        full_up = lax.all_gather(up_weight, axes, axis=0, tiled=True)
+        full_down = lax.all_gather(down_turned, axes, axis=0, tiled=True)
+    inputs = tokens.reshape(total_rows, model_width).astype(f32)
+    normed_in = (normalize(inputs) * gain_float[0]).astype(bf16)
+    key_value = jnp.dot(normed_in, full_qkv[:, query_width:], preferred_element_type=f32)
+    key_heads = key_value[:, :HEAD].reshape(total_rows, 1, HEAD)
+    key_local = rotate(key_heads, places)[:, 0].astype(bf16)
+    value_local = key_value[:, HEAD:].astype(bf16)
     key_grid = key_local.reshape(micro_count, row_count, HEAD)
     value_grid = value_local.reshape(micro_count, row_count, HEAD)
     own_pair = jnp.concatenate([key_grid[:, :prompt_dev], value_grid[:, :prompt_dev]], axis=2)
@@ -673,6 +1190,10 @@
         )
     else:
         prompt_pair = lax.all_gather(own_pair, "seq", axis=1, tiled=True)
+    query_heads = jnp.dot(
+        normed_in, full_qkv[:, :query_width], preferred_element_type=f32
+    ).reshape(total_rows, -1, HEAD)
+    query_rows = rotate(query_heads, places).astype(bf16)
     prompt_keys, prompt_values = prompt_pair[..., :HEAD], prompt_pair[..., HEAD:]
     key_rows = jnp.concatenate(
         [
@@ -696,81 +1217,57 @@
         row_peak = jnp.max(masked, axis=-1, keepdims=True)
         weights = jnp.exp(masked - row_peak)
         summed = jnp.sum(weights, axis=-1, keepdims=True)
-        probs = (weights / summed).astype(jnp.bfloat16)
-        contexts.append(jnp.dot(probs, value_rows, preferred_element_type=jnp.float32))
+        probs = (weights / summed).astype(bf16)
+        contexts.append(jnp.dot(probs, value_rows, preferred_element_type=f32))
         log_sums.append(row_peak + jnp.log(summed))
-    context = jnp.stack(contexts, axis=1).reshape(total_rows, -1).astype(jnp.bfloat16)
-    attn_part = jnp.dot(context, full_out, preferred_element_type=jnp.float32).astype(jnp.bfloat16)
-    gain_pad = jnp.pad(gain_float, ((0, 4), (0, 0)))
-    sums, result, ffn_in, hidden, d_ffn, d_gate, d_up, gain_fourth = ffn_block(
-        attn_part.reshape(tokens.shape[0], row_count, model_width),
+    context = jnp.stack(contexts, axis=1).reshape(total_rows, -1).astype(bf16)
+    attn_part = jnp.dot(context, full_out, preferred_element_type=f32).astype(bf16)
+    block = ffn_block(
+        attn_part.reshape(micro_count, row_count, model_width),
         tokens[:, 0],
         cotangent[:, 0],
         full_gate,
         full_up,
         full_down,
-        gain_pad,
+        jnp.pad(gain_float, ((0, 4), (0, 0))),
         0,
     )
-    gain_fourth = jnp.sum(gain_fourth, axis=0)
-    attn = sums[:micro_count].reshape(total_rows, model_width).astype(jnp.float32)
-    d_ffn_in = sums[2 * micro_count :].reshape(total_rows, model_width)
-    middle = inputs + normalize(attn) * gain_float[1]
-    upstream = cotangent.reshape(total_rows, model_width).astype(jnp.float32)
-    ffn_in, hidden, d_ffn, d_gate, d_up = (
-        kept.reshape(total_rows, -1) for kept in (ffn_in, hidden, d_ffn, d_gate, d_up)
-    )
+    gain_sums = jnp.sum(block["gain_grad"].reshape(3, 8, model_width), axis=1)
+    d_middle = block["d_middle"].reshape(total_rows, model_width).astype(f32)
+    d_attn = block["d_attn"].reshape(total_rows, model_width)
 
     def scatter(grad, axis):
         return lax.psum_scatter(
-            grad.astype(jnp.bfloat16), axes, scatter_dimension=axis, tiled=True
-        ).astype(jnp.float32)
-
-    grad_down = jnp.einsum("rd,rf->df", d_ffn, hidden, preferred_element_type=jnp.float32)
-    grad_gate = jnp.einsum("rd,rf->df", ffn_in, d_gate, preferred_element_type=jnp.float32)
-    grad_up = jnp.einsum("rd,rf->df", ffn_in, d_up, preferred_element_type=jnp.float32)
-    d_ffn_in, grad_down, grad_gate, grad_up = lax.optimization_barrier(
-        (
-            d_ffn_in,
-            grad_down.astype(jnp.bfloat16),
-            grad_gate.astype(jnp.bfloat16),
-            grad_up.astype(jnp.bfloat16),
-        )
-    )
-    d_ffn_in = d_ffn_in.astype(jnp.float32)
-    share_down = scatter(grad_down, 0).T
-    share_gate = scatter(grad_gate, 0)
-    d_mid_norm, gain_third = norm_back(middle, gain_float[2], d_ffn_in)
-    d_middle = upstream + d_mid_norm
-    d_attn, gain_second = norm_back(attn, gain_float[1], d_middle)
-    d_attn = d_attn.astype(jnp.bfloat16)
-    grad_out = jnp.einsum("rc,rd->cd", context, d_attn, preferred_element_type=jnp.float32)
-    d_attn, share_down = lax.optimization_barrier((d_attn, share_down))
+            grad.astype(bf16), axes, scatter_dimension=axis, tiled=True
+        ).astype(f32)
+
+    share_down = scatter(block["grad_down"], 0).T
+    share_gate = scatter(block["grad_gate"], 0)
     d_context = (
-        jnp.einsum("rd,cd->rc", d_attn, full_out, preferred_element_type=jnp.float32)
-        .astype(jnp.bfloat16)
+        jnp.einsum("rd,cd->rc", d_attn, full_out, preferred_element_type=f32)
+        .astype(bf16)
         .reshape(total_rows, head_count, HEAD)
     )
-    key_grad = jnp.zeros((key_rows.shape[0], HEAD), jnp.float32)
-    value_grad = jnp.zeros((key_rows.shape[0], HEAD), jnp.float32)
+    key_grad = jnp.zeros((key_rows.shape[0], HEAD), f32)
+    value_grad = jnp.zeros((key_rows.shape[0], HEAD), f32)
     query_grads = []
     for head_pos in range(head_count):
         curved, masked = scores_for(query_rows[:, head_pos], key_rows, visible, score_scale)
         probs = jnp.where(visible, jnp.exp(masked - log_sums[head_pos]), 0.0)
-        probs_low = probs.astype(jnp.bfloat16)
+        probs_low = probs.astype(bf16)
         d_probs = jnp.einsum(
-            "rd,kd->rk", d_context[:, head_pos], value_rows, preferred_element_type=jnp.float32
+            "rd,kd->rk", d_context[:, head_pos], value_rows, preferred_element_type=f32
         )
         inner_sum = jnp.sum(probs * d_probs, axis=-1, keepdims=True)
         d_scores = (probs * (d_probs - inner_sum) * score_scale * (1.0 - curved * curved)).astype(
-            jnp.bfloat16
+            bf16
         )
-        query_grads.append(jnp.dot(d_scores, key_rows, preferred_element_type=jnp.float32))
+        query_grads.append(jnp.dot(d_scores, key_rows, preferred_element_type=f32))
         key_grad = key_grad + jnp.einsum(
-            "rk,rd->kd", d_scores, query_rows[:, head_pos], preferred_element_type=jnp.float32
+            "rk,rd->kd", d_scores, query_rows[:, head_pos], preferred_element_type=f32
         )
         value_grad = value_grad + jnp.einsum(
-            "rk,rd->kd", probs_low, d_context[:, head_pos], preferred_element_type=jnp.float32
+            "rk,rd->kd", probs_low, d_context[:, head_pos], preferred_element_type=f32
         )
     split_at = micro_count * prompt_all
     pair_grad = jnp.concatenate(
@@ -783,13 +1280,13 @@
     if seq_count == 2:
         low_part, high_part = pair_grad[:, :prompt_dev], pair_grad[:, prompt_dev:]
         early = seq_pos == 0
-        sent = jnp.where(early, high_part, low_part).astype(jnp.bfloat16)
+        sent = jnp.where(early, high_part, low_part).astype(bf16)
         kept = jnp.where(early, low_part, high_part)
-        pair_grad = kept + lax.ppermute(sent, "seq", [(0, 1), (1, 0)]).astype(jnp.float32)
+        pair_grad = kept + lax.ppermute(sent, "seq", [(0, 1), (1, 0)]).astype(f32)
     else:
         pair_grad = lax.psum_scatter(
-            pair_grad.astype(jnp.bfloat16), "seq", scatter_dimension=1, tiled=True
-        ).astype(jnp.float32)
+            pair_grad.astype(bf16), "seq", scatter_dimension=1, tiled=True
+        ).astype(f32)
     prompt_key_grad, prompt_value_grad = pair_grad[..., :HEAD], pair_grad[..., HEAD:]
     own_keys = jnp.concatenate(
         [prompt_key_grad, key_grad[split_at:].reshape(micro_count, CONT, HEAD)], axis=1
@@ -797,73 +1294,56 @@
     own_values = jnp.concatenate(
         [prompt_value_grad, value_grad[split_at:].reshape(micro_count, CONT, HEAD)], axis=1
     ).reshape(total_rows, HEAD)
-    unused_query, unturn_query = jax.vjp(lambda turned_in: rotate(turned_in, places), query_heads)
-    d_query = (
-        unturn_query(jnp.stack(query_grads, axis=1))[0].reshape(total_rows, -1).astype(jnp.bfloat16)
-    )
-    unused_key, unturn_key = jax.vjp(lambda turned_in: rotate(turned_in, places), key_heads)
-    d_key = unturn_key(own_keys[:, None, :])[0].reshape(total_rows, HEAD).astype(jnp.bfloat16)
-    d_value = own_values.astype(jnp.bfloat16)
-    grad_query = jnp.einsum("rd,rc->dc", normed_in, d_query, preferred_element_type=jnp.float32)
-    grad_key = jnp.einsum("rd,rc->dc", normed_in, d_key, preferred_element_type=jnp.float32)
-    grad_value = jnp.einsum("rd,rc->dc", normed_in, d_value, preferred_element_type=jnp.float32)
-    attn_part = jnp.einsum("rc,dc->rd", d_query, full_query, preferred_element_type=jnp.float32)
-    attn_part = attn_part + jnp.einsum(
-        "rc,dc->rd", d_key, full_key, preferred_element_type=jnp.float32
-    )
-    attn_part = attn_part + jnp.einsum(
-        "rc,dc->rd", d_value, full_value, preferred_element_type=jnp.float32
-    )
-    share_up = scatter(grad_up, 0)
-    share_out = scatter(grad_out, 1)
-    attn_part, share_gate, grad_query, grad_key, grad_value = lax.optimization_barrier(
-        (
-            attn_part.astype(jnp.bfloat16),
-            share_gate,
-            grad_query.astype(jnp.bfloat16),
-            grad_key.astype(jnp.bfloat16),
-            grad_value.astype(jnp.bfloat16),
+    d_query = turn_back(jnp.stack(query_grads, axis=1), places).reshape(total_rows, -1)
+    d_key = turn_back(own_keys[:, None, :], places).reshape(total_rows, HEAD)
+    d_qkv = jnp.concatenate([d_query, d_key, own_values], axis=1).astype(bf16)
+    attn_part = jnp.einsum("rc,dc->rd", d_qkv, full_qkv, preferred_element_type=f32)
+    gain_first = jnp.sum(attn_part * normalize(inputs), axis=0)
+    grad_gains = jnp.concatenate(
+        [gain_first[None], jnp.where(lax.axis_index("tensor") == 0, gain_sums, 0.0)], axis=0
+    )
+    gain_cols = jnp.pad(grad_gains.T, ((0, 0), (0, SIDE_PAD - grad_gains.shape[0])))
+    attn_part = attn_part.astype(bf16)
+    if planar:
+        d_normed, share_up, share_side, share_gains = tail_block(
+            attn_part.reshape(micro_count, row_count, model_width),
+            block["grad_up"],
+            normed_in,
+            d_attn,
+            d_qkv,
+            context,
+            gain_cols.astype(bf16),
+            1,
         )
-    )
-    d_normed = chain_sum(attn_part, 3)
-    d_normed, share_up = lax.optimization_barrier((d_normed, share_up))
-    d_normed = d_normed.astype(jnp.float32)
-    d_in_norm, gain_first = norm_back(inputs, gain_float[0], d_normed)
+        d_normed, share_gate, share_down = lax.optimization_barrier(
+            (d_normed, share_gate, share_down)
+        )
+        d_normed = d_normed.reshape(total_rows, model_width)
+        share_up, share_side = share_up.astype(f32), share_side.astype(f32)
+        share_out = share_side[:, qkv_width : qkv_width + query_width].T
+        share_gains = share_gains[:, :4].T
+    else:
+        share_up = scatter(block["grad_up"], 0)
+        share_out = scatter(
+            jnp.einsum("rc,rd->cd", context, d_attn, preferred_element_type=f32), 1
+        )
+        side_grad = jnp.einsum("rd,rc->dc", normed_in, d_qkv, preferred_element_type=f32)
+        d_normed = chain_sum(attn_part, 1)
+        share_side = scatter(jnp.concatenate([side_grad, gain_cols], axis=1), 0)
+        share_gains = lax.psum(share_side[:, qkv_width : qkv_width + 4].T, "tensor")
+    d_in_norm = norm_back(inputs, gain_float[0], d_normed.astype(f32))
     input_grad = d_middle + d_in_norm
-    grad_gains = jnp.stack([gain_first, gain_second, gain_third, gain_fourth], axis=0)
-    side_grad = scatter(
-        jnp.concatenate(
-            [
-                grad_query,
-                grad_key,
-                grad_value,
-                jnp.pad(grad_gains.T, ((0, 0), (0, 128 - grad_gains.shape[0]))),
-            ],
-            axis=1,
-        ),
-        0,
-    )
-    shares = (
-        side_grad[:, :query_width],
-        side_grad[:, query_width : query_width + HEAD],
-        side_grad[:, query_width + HEAD : query_width + 2 * HEAD],
+    return (
+        block["out"].reshape(tokens.shape),
+        input_grad.reshape(tokens.shape),
+        share_side[:, :query_width],
+        share_side[:, query_width : query_width + HEAD],
+        share_side[:, query_width + HEAD : qkv_width],
         share_out,
         share_gate,
         share_up,
         share_down,
-        side_grad[:, query_width + 2 * HEAD : query_width + 2 * HEAD + 4].T,
-    )
-    return (
-        result.reshape(tokens.shape).astype(jnp.bfloat16),
-        input_grad.reshape(tokens.shape),
-        shares[0],
-        shares[1],
-        shares[2],
-        shares[3],
-        shares[4],
-        shares[5],
-        shares[6],
-        shares[7],
+        share_gains,
     )
 
 

time: 1260 us -> 917 us (0.73)
  waiting for transfers between devices: 363 us -> 103 us
  Pallas kernels: 513 us -> 595 us
  matrix products: 169 us -> 94.9 us
  other arithmetic: 147 us -> 73.8 us
    reduce_scatter x5 -> x2, waiting for transfers between devices: 157 us -> 0.01 us  [scatter(): lax.psum_scatter(grad.astype(bf16), axes, scatter_dimension=axis, tiled=T...]
    all_gather x2 -> x0, waiting for transfers between devices: 131 us -> none  [the longest x1 65.6 us: per_device(): full_up = lax.all_gather(up_weight, axes, axis=0, tiled=True)]
    dot_general x19 -> x9, matrix products: 121 us -> 42.3 us  [the longest x1 10.6 us: per_device(): jnp.einsum('rc,dc->rd', d_qkv, full_qkv, preferred_element_type=f32)]
    pallas_call x1, Pallas kernels: 377 us -> 432 us  [ffn_block(): pl.pallas_call(functools.partial(ffn_kernel, size, width, bases, schedule...]
    add x3 -> x1, other arithmetic: 30.8 us -> 0.43 us  [per_device(): pair_grad = kept + lax.ppermute(sent, 'seq', [(0, 1), (1, 0)]).astype(f32)]
    pallas_call x1, Pallas kernels: 136 us -> 164 us  [tail_block(): pl.pallas_call(functools.partial(tail_kernel, size, width, bases), out_sh...]
    reduce_sum x5 -> x2, other arithmetic: 33.2 us -> 6.21 us  [the longest x1 6.14 us: norm_back(): jnp.mean(scaled * normed, axis=-1, keepdims=True)]
    ppermute x1, waiting for transfers between devices: 0.01 us -> 20.4 us  [per_device(): pair_grad = kept + lax.ppermute(sent, 'seq', [(0, 1), (1, 0)]).astype(f32)]
  transfers between devices with their start and end apart: 12 -> 7, of which waited for: 9 -> 4; matrix products, arithmetic and copies ran while one was open for 22% -> 18% of each run, Pallas kernels for 11% -> 18%
where the time goes in v5:
time: 917 us; the launch traced here: 911 us
  Pallas kernels  595 us (65%)
  waiting for transfers between devices  103 us (11%)
  matrix products  94.9 us (10%)
  other arithmetic  73.8 us (8%)
  local copies, waits for them, and re-layouts  27.4 us (3%)
  between operations  15.3 us (2%)
    pallas_call x1, Pallas kernels, ffn_block(): pl.pallas_call(functools.partial(ffn_kernel, size, width, bases, schedule...  432 us
    pallas_call x1, Pallas kernels, tail_block(): pl.pallas_call(functools.partial(tail_kernel, size, width, bases), out_sh...  164 us
    all_gather x1, waiting for transfers between devices, per_device(): full_side = lax.all_gather(side_weights, axes, axis=0, tiled=True)  38.4 us
    ppermute x1, waiting for transfers between devices, per_device(): other_pair = lax.ppermute(own_pair, 'seq', [(0, 1), (1, 0)])  24.5 us
    dot_general x2, matrix products, per_device(): jnp.einsum('rd,kd->rk', d_context[:, head_pos], value_rows, preferred_ele...  23 us
    ppermute x1, waiting for transfers between devices, per_device(): pair_grad = kept + lax.ppermute(sent, 'seq', [(0, 1), (1, 0)]).astype(f32)  20.4 us
  transfers between devices with their start and end apart: 7, of which 4 were waited for; matrix products, arithmetic and copies ran while one was open for 18% of the time, Pallas kernels for 18%

profile of v5, /device:TPU:0, one launch (start us, length us, event | category | flops | bytes accessed | tf_op | source)
XLA Modules:
  0.0 911.4 jit_solution(11952053459495497716)
XLA Ops:
  7.2 0.8 copy.43
  8.0 2.0 fusion.43
  10.1 0.7 all-gather.6.cloned.1.call-update
  10.9 0.7 all-gather.8.cloned.1.call-update
  11.7 3.5 multiply_reduce_fusion.2
  16.2 38.4 %all-gather.4.cloned.1.call-done = bf16[2304,1152]{1,0:T(8,128)(2,1)} async-done(((bf16[288,1152]{1,0:T(8,128)(2,1)}), bf16[2304,1152]{1,0:T(8,128)(2,1)}) %all-gather.4.cloned.1.call-update) | async-done | bytes 5308432 | tf_op jit(solution)/shard_map/all_gather | solution.py:1165
  54.6 1.1 slice_convert_fusion.2
  56.2 3.6 multiply_convert_fusion.normed_ref
  59.8 6.2 fusion.23
  66.4 4.1 fusion.38
  70.6 0.8 pad.14.gain_ref
  71.4 3.2 slice_bitcast_fusion
  74.6 4.8 copy.45
  79.5 1.2 collective-permute-start
  80.8 3.7 multiply_convert_fusion.1
  84.4 2.8 fusion.62
  87.4 0.6 fusion.29
  88.0 24.5 %collective-permute-done = bf16[2,512,512]{2,1,0:T(8,128)(2,1)S(1)} collective-permute-done((bf16[2,512,512]{2,1,0:T(8,128)(2,1)S(1)}, bf16[2,512,512]{2,1,0:T(8,128)(2,1)S(1)}, u32[]{:S(2)}, u32[]{:S(2)}) %collective-permute-start) | collective-permute-done | bytes 1048608 | tf_op jit(solution)/shard_map/ppermute | solution.py:1186
  112.5 0.4 broadcast_select_fusion
  113.1 3.7 fusion.17
  116.9 5.8 fusion.4
  122.7 4.3 fusion.5
  127.0 3.6 fusion.22
  130.7 3.6 fusion.21
  134.5 6.5 convolution_convert_fusion
  141.0 17.8 %all-gather.8.cloned.1.call-done.gate_ref = bf16[2304,2304]{1,0:T(8,128)(2,1)} async-done(((bf16[288,2304]{1,0:T(8,128)(2,1)}), bf16[2304,2304]{1,0:T(8,128)(2,1)}) %all-gather.8.cloned.1.call-update) | async-done | bytes 10616848 | tf_op jit(solution)/shard_map/all_gather | solution.py:1169
  158.8 431.7 %shard_map.186 = (bf16[6,544,2304]{2,1,0:T(8,128)(2,1)}, bf16[2,544,2304]{2,1,0:T(8,128)(2,1)}, bf16[2,544,2304]{2,1,0:T(8,128)(2,1)}, bf16[2,544,2304]{2,1,0:T(...) custom-call(bf16[2,544,2304]{2,1,0:T(8,128)(2,1)} %bitcast.193, ...), custom_call_target="tpu_custom_call" | custom-call | flops 103960018944 | bytes 1073741824 | tf_op jit(solution)/shard_map/pallas_call | solution.py:760
  590.7 5.9 convolution_convert_fusion.1
  596.6 0.5 reshape.356
  597.1 2.4 fusion.59
  599.5 6.7 fusion.47
  606.3 8.0 fusion.6
  614.3 16.3 %multiply_reduce_fusion.3 = (f32[1088]{0:T(1024)S(1)}, f32[1088]{0:T(1024)S(1)}, f32[1088,2112]{1,0:T(8,128)}) fusion(f32[1088]{0:T(1024)S(1)} %log_add_fusion, f32[1088,2112]{1,0:T(8,128)} %copy-done, s32[1088]{0:T(1024)S(1)} %le.16, s32[2112]{0:T(1024)S(1)} %get-tuple-element.103, s32[1088]{0:T(1024)S(1)} %get-tuple-element.96, ...), kind=kOutput, calls=%fused_computation.17 | convolution fusion | flops 1217726464 | bytes 38451456 | tf_op jit(solution)/shard_map/rd,kd->rk/dot_general | solution.py:1258
  630.6 8.7 fusion.14
  639.6 15.0 %multiply_convert_fusion.2 = (bf16[1088,2112]{1,0:T(8,128)(2,1)}, bf16[1088,2112]{1,0:T(8,128)(2,1)S(1)}) fusion(f32[1088,2112]{1,0:T(8,128)S(1)} %bitcast.142, f32[1088,2112]{1,0:T(8,128)} %get-tuple-element.100, f32[1088]{0:T(1024)S(1)} %get-tuple-element.68, f32[1088]{0:T(1024)S(1)} %log_add_fusion, s32[1088]{0:T(1024)S(1)} %le.16, ...), kind=kLoop, calls=%fused_computation.16 | loop fusion | flops 62042112 | bytes 46004480 | tf_op jit(solution)/shard_map/convert_element_type | solution.py:1262
  654.6 1.7 fusion.46
  656.3 0.6 copy-done.10
  656.9 1.7 convolution_add_fusion
  659.0 1.0 copy-done.12
  660.0 0.7 collective-permute-start.1
  660.7 1.5 convolution_bitcast_fusion
  662.2 1.5 convolution_bitcast_fusion.1
  663.8 1.1 copy-done.2
  665.2 0.6 fusion.41
  665.9 0.8 copy-done.21
  666.9 20.4 %collective-permute-done.1 = bf16[2,512,512]{2,1,0:T(8,128)(2,1)S(1)} collective-permute-done((bf16[2,512,512]{2,1,0:T(8,128)(2,1)S(1)}, bf16[2,512,512]{2,1,0:T(8,128)(2,1)S(1)}, u32[]{:S(2)}, u32[]{:S(2)}) %collective-permute-start.1) | collective-permute-done | bytes 1048608 | tf_op jit(solution)/shard_map/ppermute | solution.py:1285
  688.0 0.6 slice-done.12
  688.7 0.5 copy-done.8
  689.2 4.1 fusion.40
  693.3 10.6 %multiply_reduce_fusion.1 = (bf16[2304]{0:T(1024)(128)(2,1)S(1)}, bf16[1088,2304]{1,0:T(8,128)(2,1)}) fusion(bf16[2,1,544,2304]{3,2,1,0:T(8,128)(2,1)S(1)} %bitcast.136, f32[1088]{0:T(1024)S(1)} %copy-done.26, bf16[2304,1152]{1,0:T(8,128)(2,1)} %all-gather.4.cloned.1.call-done, bf16[1088,256]{1,0:T(8,128)(2,1)S(1)} %bitcast.160, ...), kind=kOutput, calls=%fused_computation.12 | convolution fusion | flops 5153044480 | bytes 16982784 | tf_op jit(solution)/shard_map/rc,dc->rd/dot_general | solution.py:1300
  704.3 0.9 pad.15.gain_ref
  705.2 1.7 pad_maximum_fusion.1.d_qkv_ref
  706.9 163.6 %shard_map.187 = (bf16[2,544,2304]{2,1,0:T(8,128)(2,1)}, bf16[288,2304]{1,0:T(8,128)(2,1)}, bf16[288,1664]{1,0:T(8,128)(2,1)}, f32[288,128]{1,0:T(8,128)}) custom-call(bf16[2,544,2304]{2,1,0:T(8,128)(2,1)} %bitcast.192, bf16[2304,2304]{1,0:T(8,128)(2,1)} %get-tuple-element.27.up_grad_ref, bf16[1088,2304]{1,0:T(8,128)(2,1)} %copy-done.6, ...), custom_call_target="tpu_custom_call" | custom-call | flops 8342470656 | bytes 419430400 | tf_op jit(solution)/shard_map/pallas_call | solution.py:1029
  870.5 1.9 slice.199
  872.4 1.3 convert_element_type.144
  873.8 0.7 copy.53
  874.5 3.0 convert_element_type.145
  877.5 0.9 fusion.60
  878.3 0.9 slice_bitcast_fusion.2
  879.2 3.0 convert_bitcast_fusion
  882.2 3.0 convert_element_type.141
  885.2 6.1 multiply_reduce_fusion
  891.4 10.7 %fusion.2 = f32[2,1,544,2304]{3,2,1,0:T(8,128)} fusion(bf16[2,544,2304]{2,1,0:T(8,128)(2,1)} %get-tuple-element.32, bf16[2,544,2304]{2,1,0:T(8,128)(2,1)} %get-tuple-element.25, bf16[2,1,544,2304]{3,2,1,0:T(8,128)(2,1)S(1)} %bitcast.138, f32[2,544]{1,0:T(2,128)S(1)} %broadcast_multiply_fusion.1, f32[2304]{0:T(1024)S(1)} %copy-done.20, f32[2,544]{1,0:T(2,128)S(1)} %copy-done.24), kind=kLoop, calls=%fused_computation.6 | loop fusion | flops 22560768 | bytes 25085440
  902.1 2.3 copy.75
  (156 shorter events, 5.0 us)
Async XLA Ops:
  7.2 47.4 %all-gather.4.cloned.1.call-start = ((), (), s32[]{:S(2)}) async-start(), calls=%async_computation.2 | async-start | bytes 5971968 | tf_op jit(solution)/shard_map/all_gather | solution.py:1165
  10.1 124.4 %all-gather.6.cloned.1.call-start = ((), (), s32[]{:S(2)}) async-start(), calls=%async_computation.3 | async-start | bytes 2654208 | tf_op jit(solution)/shard_map/all_gather | solution.py:1168
  10.8 148.0 %all-gather.8.cloned.1.call-start = ((), (), s32[]{:S(2)}) async-start(), calls=%async_computation.4 | async-start | bytes 11943936 | tf_op jit(solution)/shard_map/all_gather | solution.py:1169
  11.6 867.6 %reduce-scatter.5.cloned.1.call-start = ((), (), s32[]{:S(2)}) async-start(), calls=%async_computation.6 | async-start | bytes 11943936 | tf_op jit(solution)/shard_map/reduce_scatter | solution.py:1240
  11.7 3.9 copy-start.29
  15.2 65.6 %copy-start.23 = (f32[2,544]{1,0:T(2,128)}, f32[2,544]{1,0:T(2,128)S(1)}, u32[]{:S(2)}) copy-start(f32[2,544]{1,0:T(2,128)S(1)} %add_rsqrt_fusion) | copy-start | bytes 13060
  15.9 43.9 %copy-start.25 = (f32[1088]{0:T(1024)}, f32[1088]{0:T(1024)S(1)}, u32[]{:S(2)}) copy-start(f32[1088]{0:T(1024)S(1)} %rsqrt.15) | copy-start | bytes 13060
  16.2 50.2 %copy-start.7 = (f32[1088,128]{1,0:T(8,128)}, f32[1088,128]{1,0:T(8,128)S(1)}, u32[]{:S(2)}) copy-start(f32[1088,128]{1,0:T(8,128)S(1)} %broadcast_multiply_fusion) | copy-start | bytes 1671172
  56.1 24.6 %copy-start.19 = (f32[2304]{0:T(1024)}, f32[2304]{0:T(1024)S(1)}, u32[]{:S(2)}) copy-start(f32[2304]{0:T(1024)S(1)} %slice_reduce_fusion) | copy-start | bytes 27652
  59.8 6.3 copy-start.6
  70.6 16.9 %copy-start.1 = (f32[1088,256]{1,0:T(8,128)}, f32[1088,256]{1,0:T(8,128)S(1)}, u32[]{:S(2)}) copy-start(f32[1088,256]{1,0:T(8,128)S(1)} %get-tuple-element.91) | copy-start | bytes 3342340
  70.6 16.9 %copy-start.3 = (f32[1088,256]{1,0:T(8,128)}, f32[1088,256]{1,0:T(8,128)S(1)}, u32[]{:S(2)}) copy-start(f32[1088,256]{1,0:T(8,128)S(1)} %get-tuple-element.92) | copy-start | bytes 3342340
  70.6 46.3 %copy-start.27 = (bf16[2,32,256]{2,1,0:T(8,128)(2,1)}, bf16[2,32,256]{2,1,0:T(8,128)(2,1)S(1)}, u32[]{:S(2)}) copy-start(bf16[2,32,256]{2,1,0:T(8,128)(2,1)S(1)} %slice.179) | copy-start | bytes 98308
  79.5 4.9 copy-start.11
  79.5 33.0 %collective-permute-start = (bf16[2,512,512]{2,1,0:T(8,128)(2,1)S(1)}, bf16[2,512,512]{2,1,0:T(8,128)(2,1)S(1)}, u32[]{:S(2)}, u32[]{:S(2)}) collective-permute-start(bf16[2,512,512]{2,1,0:T(8,128)(2,1)S(1)} %pad_maximum_fusion.8), channel_id=1, source_target_pairs={{0,4},{4,0},{1,5},{5,1},{2,6},{6,2},{3,7},{7,3},{8,12},{12,8},{9,1... | collective-permute-start | bytes 3145736 | tf_op jit(solution)/shard_map/ppermute | solution.py:1186
  88.0 28.9 %copy-start.15 = (bf16[1088,2,256]{2,0,1:T(8,128)(2,1)}, bf16[1088,2,256]{2,0,1:T(8,128)(2,1)S(1)}, u32[]{:S(2)}) copy-start(bf16[1088,2,256]{2,0,1:T(8,128)(2,1)S(1)} %fusion.29) | copy-start | bytes 3342340
  113.1 3.8 copy-start.17
  116.9 13.8 %copy-start.5 = (f32[1088,2112]{1,0:T(8,128)}, f32[1088,2112]{1,0:T(8,128)S(1)}, u32[]{:S(2)}) copy-start(f32[1088,2112]{1,0:T(8,128)S(1)} %get-tuple-element.98) | copy-start | bytes 27574276
  122.7 4.3 copy-start
  134.5 6.6 copy-start.13
  590.6 291.6 %reduce-scatter.3.cloned.1.call-start = ((), (), s32[]{:S(2)}) async-start(), calls=%async_computation.5 | async-start | bytes 11943936 | tf_op jit(solution)/shard_map/reduce_scatter | solution.py:1240
  606.2 8.0 slice-start.4
  606.2 8.0 slice-start.5
  606.3 8.0 slice-start.6
  606.3 8.0 copy-start.14
  614.3 25.2 %slice-start.7 = ((s8[9469952]{0:T(1024)(128)(4,1)}), s8[4194304]{0:T(1024)(128)(4,1)S(1)}, s32[]{:S(2)}) async-start(s8[9469952]{0:T(1024)(128)(4,1)} %bitcast.141), calls=%async_computation.14 | async-start | bytes 8388608
  614.3 25.2 %slice-start.8 = ((s8[9469952]{0:T(1024)(128)(4,1)}), s8[1081344]{0:T(1024)(128)(4,1)S(1)}, s32[]{:S(2)}) async-start(s8[9469952]{0:T(1024)(128)(4,1)} %bitcast.141), calls=%async_computation.15 | async-start | bytes 2162688
  630.6 8.9 slice-start.9
  639.5 15.0 %copy-start.16 = (bf16[1088,2,256]{2,0,1:T(8,128)(2,1)S(1)}, bf16[1088,2,256]{2,0,1:T(8,128)(2,1)}, u32[]{:S(2)}) copy-start(bf16[1088,2,256]{2,0,1:T(8,128)(2,1)} %copy-done.15) | copy-start | bytes 3342340
  654.6 2.4 copy-start.10
  658.6 1.3 copy-start.12
  658.8 1.9 copy-start.18
  658.8 1.9 copy-start.28
  660.0 27.3 %collective-permute-start.1 = (bf16[2,512,512]{2,1,0:T(8,128)(2,1)S(1)}, bf16[2,512,512]{2,1,0:T(8,128)(2,1)S(1)}, u32[]{:S(2)}, u32[]{:S(2)}) collective-permute-start(bf16[2,512,512]{2,1,0:T(8,128)(2,1)S(1)} %select_convert_fusion), channel_id=1, source_target_pairs={{0,4},{4,0},{1,5},{5,1},{2,6},{6,2},{3,7},{7,3},{8,12},{12,8},{9,1... | collective-permute-start | bytes 3145736 | tf_op jit(solution)/shard_map/ppermute | solution.py:1285
  663.7 1.3 copy-start.2
  663.7 1.6 copy-start.4
  665.8 0.9 copy-start.21
  687.7 0.8 slice-start.12
  687.7 5.6 slice-start
  687.9 1.2 copy-start.8
  688.5 4.7 slice-start.1
  688.6 4.7 copy-start.26
  870.5 3.2 copy-start.22
  873.7 3.7 copy-start.9
  882.2 3.0 copy-start.20
  882.2 3.0 copy-start.24
  885.2 6.2 slice-start.2
  885.2 6.2 slice-start.3
  891.4 10.7 %slice-start.10 = ((s8[5013504]{0:T(1024)(128)(4,1)}), s8[4194304]{0:T(1024)(128)(4,1)S(1)}, s32[]{:S(2)}) async-start(s8[5013504]{0:T(1024)(128)(4,1)} %bitcast.148), calls=%async_computation.17 | async-start | bytes 8388608
  891.4 10.7 %slice-start.11 = ((s8[5013504]{0:T(1024)(128)(4,1)}), s8[819200]{0:T(1024)(128)(4,1)S(1)}, s32[]{:S(2)}) async-start(s8[5013504]{0:T(1024)(128)(4,1)} %bitcast.148), calls=%async_computation.18 | async-start | bytes 1638400
Sparse Core Ops, SparseCore 0:
  10.5 44.0 all-gather.3
  56.5 30.5 all-gather.5
  89.0 69.8 all-gather.7
  590.7 91.4 reduce-scatter.4
  685.5 107.9 reduce-scatter.2

commit v6 on v5

--- a/solution.py
+++ b/solution.py
@@ -181,6 +181,93 @@
     return gate * half, half + rise
 
 
+def plane_gather(full_ref, own_ref, pieces, sems_in, sems_out, own_done):
+    share = own_ref.shape[0]
+    dp, seq = lax.axis_index("dp"), lax.axis_index("seq")
+    x, core = dp // 2, lax.rem(dp, 2)
+    over_x, over_y, over_core = plane_partners()
+    routes = (
+        ((0, 0, 0), 0, over_x, (1, 0, 0)),
+        ((0, 0, 0), 0, over_y, (0, 1, 0)),
+        ((0, 0, 0), 0, over_core, (0, 0, 1)),
+        ((1, 0, 0), 1, over_y, (1, 1, 0)),
+        ((0, 1, 0), 2, over_x, (1, 1, 0)),
+        ((1, 0, 0), 0, over_core, (1, 0, 1)),
+        ((0, 1, 0), 0, over_core, (0, 1, 1)),
+        ((1, 1, 0), 1, over_core, (1, 1, 1)),
+        ((1, 1, 0), 2, over_core, (1, 1, 1)),
+    )
+
+    def across(u, part):
+        _, _, low, count, left = pieces[u]
+        return (pl.ds(low, count), pl.ds(low, left), pl.ds(low + left, count - left))[part]
+
+    def live(u, kind):
+        _, _, _, count, left = pieces[u]
+        return routes[kind][1] != 2 or left < count
+
+    def view(u, at, part):
+        nx, ny, nc = (jnp.abs(now - flip) for now, flip in zip((x, seq, core), at))
+        row = ((nx * 2 + nc) * 2 + ny) * share + pieces[u][0]
+        return full_ref.at[pl.ds(pl.multiple_of(row, 16), pieces[u][1]), across(u, part)]
+
+    def own(u):
+        return own_ref.at[pl.ds(pieces[u][0], pieces[u][1]), across(u, 0)]
+
+    def hop(u, kind, source, target):
+        return pltpu.make_async_remote_copy(
+            source, target, sems_out.at[u, kind], sems_in.at[u, kind],
+            device_id=routes[kind][2], device_id_type=MESH)
+
+    def send(u, kind):
+        if live(u, kind):
+            at, part, _, _ = routes[kind]
+            target = view(u, at, part)
+            hop(u, kind, own(u) if kind < 3 else target, target).start()
+
+    def arrive(u, kind):
+        if live(u, kind):
+            _, part, _, at = routes[kind]
+            target = view(u, at, part)
+            hop(u, kind, target, target).wait_recv()
+
+    def own_copy(u):
+        return pltpu.make_async_copy(own(u), view(u, (0, 0, 0), 0), own_done.at[u])
+
+    def first(u):
+        for kind in (0, 1, 2):
+            send(u, kind)
+        own_copy(u).start()
+
+    def second(u):
+        arrive(u, 0)
+        send(u, 3)
+        send(u, 5)
+        arrive(u, 1)
+        send(u, 4)
+        send(u, 6)
+
+    def third(u):
+        arrive(u, 3)
+        send(u, 7)
+        arrive(u, 4)
+        send(u, 8)
+
+    def finish(u):
+        own_copy(u).wait()
+        for kind in (2, 5, 6, 7, 8):
+            arrive(u, kind)
+
+    def all_sent():
+        for u in range(len(pieces)):
+            for kind, (at, part, _, _) in enumerate(routes):
+                if live(u, kind):
+                    target = view(u, at, part)
+                    hop(u, kind, target, target).wait_send()
+
+    return first, second, third, finish, all_sent
+
+
 def line_stream(size, width, bases, parts, landing, sum_ref, sems, spot):
     place, down, up, first, last = spot
     pass_in, pass_out, share_in, share_out, local_done = sems
@@ -311,16 +398,17 @@
 
 def ffn_kernel(
     size, width, bases, schedule, gather,
-    part_ref, token_ref, cot_ref, gate_ref, up_own, down_own, gain_ref,
+    part_ref, token_ref, cot_ref, gate_own, up_own, down_own, gain_ref,
     sum_ref, out_ref, ffn_in_ref, hidden_ref, d_ffn_ref, d_attn_ref, d_middle_ref,
     grad_gate_ref, grad_up_ref, grad_down_ref, full_ref, gain_grad_ref,
     parts, landing, act_a, act_b, stage, cols, rows_w,
     pass_in, pass_out, share_in, share_out, local_done, col_sem, row_sem, io_sem, gather_in, gather_out, own_done,
 ):
     micro, rows, depth = parts.shape
-    units = gate_ref.shape[1]
+    units = gate_own.shape[1]
     stage_t, stage_a, stage_f, stage_c = (stage.at[pl.ds(k * rows, rows)] for k in range(4))
-    up_ref, down_ref = (full_ref.at[0], full_ref.at[1]) if gather else (up_own, down_own)
+    owned = (gate_own, up_own, down_own)
+    gate_ref, up_ref, down_ref = (full_ref.at[k] for k in range(3)) if gather else owned
     spot = place, down, up, first, last = chain_place(size)
     greet_line(down, up, first, last, plane_partners() if gather else ())
 
@@ -336,7 +424,7 @@
         return pltpu.make_async_copy(
             source.at[pl.ds(pl.multiple_of(i * TILE, TILE), TILE)], rows_w.at[kind, slot], row_sem.at[kind, slot])
 
-    def tiles(copy, sources, steps, body, clock):
+    def tiles(copy, sources, steps, body, clock, beside=()):
         @pl.loop(0, steps)
         def _(i):
             slot = lax.rem(i, 2)
@@ -349,6 +437,8 @@
             for kind, source in enumerate(sources):
                 copy(kind, source, i, slot).wait()
             body(i, slot)
+            for at, work in beside:
+                pl.when(i == at)(work)
 
             @pl.when((lax.rem(i, PACE) == PACE - 1) | (i + 1 == steps))
             def _():
@@ -400,7 +490,18 @@
             stage_c[:, at] = (active * up_val).astype(jnp.bfloat16)
             act_a[own_rows(m), at] = active.astype(jnp.bfloat16)
             act_b[own_rows(m), at] = (up_val * slope).astype(jnp.bfloat16)
-        tiles(col_copy, (gate_ref, up_ref), units // TILE, body, clock)
+        def down_one():
+            moved(1, 4)
+
+        def down_two():
+            moved(2, 4)
+            moved(1, 5)
+
+        def down_three():
+            moved(2, 5)
+
+        beside = ((2, down_one), (5, down_two), (8, down_three)) if gather and m == 0 else ()
+        tiles(col_copy, (gate_ref, up_ref), units // TILE, body, clock, beside)
 
     def down_proj(m, clock):
         def body(i, slot):
@@ -504,85 +605,20 @@
                 put(kind, target, i, i % 2).wait()
 
     if gather:
-        share = up_own.shape[0]
-        piece = share // 2
-        dp, seq, _ = (lax.axis_index(name) for name in ("dp", "seq", "tensor"))
-        x, core = dp // 2, lax.rem(dp, 2)
-        over_x, over_y, over_core = plane_partners()
-
-        def block(dx, dy, dc, u):
-            nx, ny, nc = (jnp.abs(now - flip) for now, flip in ((x, dx), (seq, dy), (core, dc)))
-            row = ((nx * 2 + nc) * 2 + ny) * share + (u % 2) * piece
-            return pl.ds(pl.multiple_of(row, 16), piece)
-
-        left_half, right_half = pl.ds(0, units // 2), pl.ds(units // 2, units // 2)
-        everything = pl.ds(0, units)
-
-        def view(u, dx, dy, dc, across=everything):
-            return full_ref.at[u // 2, block(dx, dy, dc, u), across]
-
-        def own(u):
-            return (up_own, down_own)[u // 2].at[pl.ds((u % 2) * piece, piece)]
-
-        def hop(u, kind, source, target, device):
-            return pltpu.make_async_remote_copy(
-                source, target, gather_out.at[u, kind], gather_in.at[u, kind],
-                device_id=device, device_id_type=MESH)
-
-        routes = (
-            ((0, 0, 0), everything, over_x, (1, 0, 0)),
-            ((0, 0, 0), everything, over_y, (0, 1, 0)),
-            ((0, 0, 0), everything, over_core, (0, 0, 1)),
-            ((1, 0, 0), left_half, over_y, (1, 1, 0)),
-            ((0, 1, 0), right_half, over_x, (1, 1, 0)),
-            ((1, 0, 0), everything, over_core, (1, 0, 1)),
-            ((0, 1, 0), everything, over_core, (0, 1, 1)),
-            ((1, 1, 0), left_half, over_core, (1, 1, 1)),
-            ((1, 1, 0), right_half, over_core, (1, 1, 1)),
-        )
-
-        def send(u, kind):
-            at, across, device, _ = routes[kind]
-            source = own(u) if kind < 3 else view(u, *at, across)
-            hop(u, kind, source, view(u, *at, across), device).start()
-
-        def arrive(u, kind):
-            _, across, device, at = routes[kind]
-            target = view(u, *at, across)
-            hop(u, kind, target, target, device).wait_recv()
-
-        def own_copy(u):
-            return pltpu.make_async_copy(own(u), view(u, 0, 0, 0), own_done.at[u])
-
-        def gather_first(u):
-            for kind in (0, 1, 2):
-                send(u, kind)
-            own_copy(u).start()
-
-        def gather_second(u):
-            arrive(u, 0)
-            send(u, 3)
-            send(u, 5)
-            arrive(u, 1)
-            send(u, 4)
-            send(u, 6)
-
-        def gather_third(u):
-            arrive(u, 3)
-            send(u, 7)
-            arrive(u, 4)
-            send(u, 8)
-
-        def gather_last(u):
-            own_copy(u).wait()
-            for kind in (2, 5, 6, 7, 8):
-                arrive(u, kind)
-
-        def gather_sent():
-            for u in range(4):
-                for kind, (at, across, device, _) in enumerate(routes):
-                    source = view(u, *at, across)
-                    hop(u, kind, source, source, device).wait_send()
+        piece = gate_own.shape[0] // 2
+        pieces = tuple((h * piece, piece, 0, units, units // 2) for h in range(2))
+        movers = [
+            plane_gather(full_ref.at[k], owned[k], pieces, gather_in.at[k], gather_out.at[k], own_done.at[k])
+            for k in range(3)
+        ]
+
+        def moved(phase, u):
+            movers[u // 2][phase](u % 2)
+
+    else:
+
+        def moved(phase, u):
+            pass
 
     gain_grad_ref[...] = jnp.zeros_like(gain_grad_ref)
 
@@ -606,27 +642,21 @@
     whole = schedule["attn"][0]
     entry = [load(m, part_ref.at[m], parts.at[m]) for m in range(micro)]
     start(entry)
-    if gather:
-        gather_first(0)
-        gather_first(1)
+    moved(0, 0)
+    moved(0, 1)
     wait(entry)
-    if gather:
-        ticks(0, 7)
-        gather_second(0)
-        gather_first(2)
-        ticks(7, 14)
-        gather_second(1)
-        gather_third(0)
-        gather_first(3)
-        ticks(14, 21)
-        gather_second(2)
-        gather_third(1)
-        ticks(21, 28)
-        gather_second(3)
-        gather_third(2)
-        ticks(28, whole)
-    else:
-        ticks(0, whole)
+    clock = 0
+    for s, phases in (
+        (7, ((1, 0), (0, 2))),
+        (14, ((1, 1), (2, 0), (0, 3))),
+        (21, ((1, 2), (2, 1), (0, 4))),
+        (28, ((1, 3), (2, 2), (0, 5))),
+    ):
+        ticks(clock, s)
+        clock = s
+        for phase, u in phases:
+            moved(phase, u)
+    ticks(clock, whole)
     kept = []
     for m in range(micro):
         norm_s, gate_s, down_s, end_s = schedule["forward"][m]
@@ -638,18 +668,17 @@
         norm_before(m, norm_s)
         kept = [load(6, stage_f, ffn_in_ref.at[m]), load(7, stage_c, hidden_ref.at[m])]
         kept[0].start()
-        if gather and m == 0:
-            gather_third(3)
-            gather_last(0)
-            gather_last(1)
         if m == 0:
+            moved(2, 3)
+            for u in range(4):
+                moved(3, u)
             prime(col_copy, (gate_ref, up_ref))
         gate_and_up(m, gate_s)
         kept[1].start()
         sent(m)
-        if gather and m == 0:
-            gather_last(2)
-            gather_last(3)
+        if m == 0:
+            moved(3, 4)
+            moved(3, 5)
         prime(row_copy, (down_ref,))
         prime(col_copy, (gate_ref, up_ref) if m + 1 < micro else (down_ref,))
         down_proj(m, down_s)
@@ -707,7 +736,8 @@
     sent(STAGES - 2)
     sent(STAGES - 1)
     if gather:
-        gather_sent()
+        for mover in movers:
+            mover[4]()
     wait(kept)
 
     shared()
@@ -754,7 +784,7 @@
     stack = jax.ShapeDtypeStruct((micro, rows, depth), bf16)
     wide = jax.ShapeDtypeStruct((micro, rows, units), bf16)
     grad = jax.ShapeDtypeStruct((depth, units), bf16)
-    full = jax.ShapeDtypeStruct((2, depth, units) if gather else (2, 16, 128), bf16)
+    full = jax.ShapeDtypeStruct((3, depth, units) if gather else (3, 16, 128), bf16)
     dma = pltpu.SemaphoreType.DMA
     flops = 2 * micro * rows * depth * units * 9
     found = pl.pallas_call(
@@ -776,7 +806,7 @@
             pltpu.VMEM((2, 2, TILE, units), bf16),
         ]
         + [dma((2, STAGES, chunks))] * 5
-        + [dma((2, 2)), dma((2, 2)), dma((8,)), dma((4, 9)), dma((4, 9)), dma((4,))],
+        + [dma((2, 2)), dma((2, 2)), dma((8,)), dma((3, 2, 9)), dma((3, 2, 9)), dma((3, 2))],
         compiler_params=pltpu.CompilerParams(
             collective_id=cid, has_side_effects=True, vmem_limit_bytes=60 * 2**20),
         cost_estimate=pl.CostEstimate(
@@ -793,11 +823,11 @@
 
 def tail_kernel(
     size, width, bases,
-    part_ref, up_grad_ref, normed_ref, d_attn_ref, d_qkv_ref, context_ref, gain_ref,
-    sum_ref, up_share_ref, side_share_ref, gain_share_ref,
-    parts, landing, up_acc, side_acc, up_first, side_first, up_second, side_second, up_third, side_third,
+    part_ref, gate_grad_ref, up_grad_ref, normed_ref, d_attn_ref, d_qkv_ref, context_ref, gain_ref,
+    sum_ref, gate_share_ref, up_share_ref, side_share_ref, gain_share_ref,
+    parts, landing, mine_in, side_acc, ffn_first, side_first, ffn_second, side_second, ffn_third, side_third,
     cols, d_qkv, context, gain_in,
-    pass_in, pass_out, share_in, share_out, local_done, col_sem, io_sem, hop_in, hop_out, gain_got, gain_sent,
+    pass_in, pass_out, share_in, share_out, local_done, col_sem, io_sem, mine_sem, hop_in, hop_out, gain_got, gain_sent,
 ):
     micro, rows, depth = parts.shape
     spot = place, down, up, first, last = chain_place(size)
@@ -812,13 +842,14 @@
     share = up_share_ref.shape[0]
     piece = share // 2
     widths = (up_share_ref.shape[1], side_share_ref.shape[1])
+    grads = (gate_grad_ref, up_grad_ref)
     qkv_width = d_qkv.shape[1]
 
     def load(index, source, target):
         return pltpu.make_async_copy(source, target, io_sem.at[index])
 
     def halves(p):
-        all_columns = widths[p // 2]
+        all_columns = widths[p // 4]
         low = -(-all_columns // 256) * 128
         return (pl.ds(0, low), pl.ds(low, all_columns - low))
 
@@ -826,18 +857,18 @@
         return pl.ds(pl.multiple_of(((bx * 2 + bc) * 2 + by) * share + (p % 2) * piece, 16), piece)
 
     def acc(p, bx, by, across):
-        if p < 2:
-            return up_acc.at[bx * 2 + by, pl.ds((p % 2) * piece, piece), across]
+        if p < 4:
+            return ffn_first.at[p, bx * 2 + by, :, across]
         return side_acc.at[block_rows(bx, by, core, p), across]
 
     def whole(p):
-        return pl.ds(0, widths[p // 2])
-
-    first_buf, second_buf, third_buf = (up_first, side_first), (up_second, side_second), (up_third, side_third)
+        return pl.ds(0, widths[p // 4])
+
+    first_buf, second_buf, third_buf = (ffn_first, side_first), (ffn_second, side_second), (ffn_third, side_third)
 
     def land(step, p, k, across):
-        buf = (first_buf, second_buf, third_buf)[step][p // 2]
-        return buf.at[p % 2, k, :, across]
+        buf = (first_buf, second_buf, third_buf)[step][p // 4]
+        return buf.at[p % 4, k, :, across]
 
     def hop(p, k, source, target, device):
         return pltpu.make_async_remote_copy(
@@ -848,8 +879,8 @@
         found = []
         for k in range(4):
             bx, by = k // 2, k % 2
-            if p < 2:
-                source = up_grad_ref.at[block_rows(bx, by, 1 - core, p), :]
+            if p < 4:
+                source = grads[p // 2].at[block_rows(bx, by, 1 - core, p), :]
             else:
                 source = side_acc.at[block_rows(bx, by, 1 - core, p), :]
             found.append((source, land(0, p, k, whole(p)), over_core))
@@ -870,6 +901,14 @@
         hop(p, k, target, target, device).wait_recv()
         return target
 
+    def fetch(p, k):
+        return pltpu.make_async_copy(
+            grads[p // 2].at[block_rows(k // 2, k % 2, core, p), :], mine_in.at[k], mine_sem.at[k])
+
+    def start_fetch(p):
+        for k in range(4):
+            fetch(p, k).start()
+
     def add(p, bx, by, across, arrived):
         mine = acc(p, bx, by, across)
 
@@ -886,9 +925,15 @@
 
     def scatter_second(p):
         for k in range(4):
-            add(p, k // 2, k % 2, whole(p), got(p, k))
+            arrived = got(p, k)
+            if p < 4:
+                fetch(p, k).wait()
+                arrived = mine_in.at[k]
+            add(p, k // 2, k % 2, whole(p), arrived)
         for k in (4, 5, 6, 7):
             go(p, k)
+        if p < 3:
+            start_fetch(p + 1)
 
     def scatter_third(p):
         left, right = halves(p)
@@ -906,8 +951,8 @@
         put(p).start()
 
     def put(p):
-        target = (up_share_ref, side_share_ref)[p // 2].at[pl.ds((p % 2) * piece, piece)]
-        return load(12 + p, acc(p, x, seq, whole(p)), target)
+        target = (gate_share_ref, up_share_ref, side_share_ref)[p // 2].at[pl.ds((p % 2) * piece, piece)]
+        return load(5 + p, acc(p, x, seq, whole(p)), target)
 
     def scatter_sent(p):
         for k, (source, target, device) in enumerate(hops(p)):
@@ -940,36 +985,39 @@
             tick(clock + i)
 
     entry = [load(m, part_ref.at[m], parts.at[m]) for m in range(micro)]
-    up_loads = [
-        load(4 + k, up_grad_ref.at[pl.ds(pl.multiple_of(((k // 2 * 2 + core) * 2 + k % 2) * share, 16), share)], up_acc.at[k])
-        for k in range(4)
-    ]
     side_loads = [
         load(2, d_qkv_ref, d_qkv),
         load(3, context_ref, context),
-        load(8, gain_ref, side_acc.at[:, pl.ds(widths[1] - SIDE_PAD, SIDE_PAD)]),
+        load(4, gain_ref, side_acc.at[:, pl.ds(widths[1] - SIDE_PAD, SIDE_PAD)]),
     ]
     for copy in entry:
         copy.start()
     scatter_first(0)
     scatter_first(1)
-    for copy in side_loads + up_loads:
+    for copy in side_loads:
         copy.start()
+    start_fetch(0)
     tile_copy(0, 0, 0).start()
     tile_copy(1, 0, 0).start()
     for copy in entry:
         copy.wait()
     ticks(0, 1)
-    for copy in side_loads + up_loads:
+    for copy in side_loads:
         copy.wait()
-    side_grads(1)
-    clock = 1 + depth // TILE
+    ticks(1, 4)
+    scatter_second(0)
     scatter_first(2)
-    scatter_first(3)
+    side_grads(4)
+    clock = 4 + depth // TILE
+    scatter_second(1)
+    scatter_third(0)
+    for p in (3, 4, 5):
+        scatter_first(p)
     plan = (
-        (0, (scatter_second, 0)), (1, (scatter_second, 1)), (3, (scatter_third, 0)), (3, (scatter_second, 2)),
-        (4, (scatter_last, 0)), (2, (scatter_second, 3)), (3, (scatter_third, 1)), (4, (scatter_last, 1)),
-        (3, (scatter_third, 2)), (4, (scatter_last, 2)), (3, (scatter_third, 3)), (4, (scatter_last, 3)),
+        (2, (scatter_second, 2)), (2, (scatter_third, 1)), (2, (scatter_last, 0)), (2, (scatter_second, 3)),
+        (2, (scatter_third, 2)), (2, (scatter_last, 1)), (2, (scatter_second, 4)), (2, (scatter_third, 3)),
+        (2, (scatter_last, 2)), (1, (scatter_second, 5)), (2, (scatter_third, 4)), (2, (scatter_last, 3)),
+        (2, (scatter_third, 5)), (2, (scatter_last, 4)), (2, (scatter_last, 5)),
     )
     for pause, (step, p) in plan:
         if pause:
@@ -998,7 +1046,7 @@
         settle(q)
         sent(q)
     shared()
-    for p in range(4):
+    for p in range(6):
         scatter_sent(p)
     for k in range(size - 1):
         gain_hop(k).wait_send()
@@ -1012,7 +1060,7 @@
     pl.semaphore_wait(barrier, len(partners))
 
 
-def tail_block(parts, up_grad, normed, d_attn, d_qkv, context, gain_cols, cid, width=128):
+def tail_block(parts, gate_grad, up_grad, normed, d_attn, d_qkv, context, gain_cols, cid, width=128):
     size = lax.axis_size("tensor")
     micro, rows, depth = parts.shape
     units = up_grad.shape[1]
@@ -1031,21 +1079,22 @@
         out_shape=(
             jax.ShapeDtypeStruct((micro, rows, depth), bf16),
             jax.ShapeDtypeStruct((share, units), bf16),
+            jax.ShapeDtypeStruct((share, units), bf16),
             jax.ShapeDtypeStruct((share, side), bf16),
             jax.ShapeDtypeStruct((share, SIDE_PAD), jnp.float32),
         ),
-        in_specs=[any_spec] * 7,
-        out_specs=(any_spec,) * 3 + (vmem_spec,),
+        in_specs=[any_spec] * 8,
+        out_specs=(any_spec,) * 4 + (vmem_spec,),
         scratch_shapes=[
             pltpu.VMEM((micro, rows, depth), bf16),
             pltpu.VMEM((2, 2, chunks, rows // 2, width), bf16),
-            pltpu.VMEM((4, share, units), bf16),
+            pltpu.VMEM((4, piece, units), bf16),
             pltpu.VMEM((depth, side), bf16),
-            pltpu.VMEM((2, 4, piece, units), bf16),
+            pltpu.VMEM((4, 4, piece, units), bf16),
             pltpu.VMEM((2, 4, piece, side), bf16),
-            pltpu.VMEM((2, 2, piece, units), bf16),
+            pltpu.VMEM((4, 2, piece, units), bf16),
             pltpu.VMEM((2, 2, piece, side), bf16),
-            pltpu.VMEM((2, 1, piece, units), bf16),
+            pltpu.VMEM((4, 1, piece, units), bf16),
             pltpu.VMEM((2, 1, piece, side), bf16),
             pltpu.VMEM((2, 2, total, TILE), bf16),
             pltpu.VMEM(d_qkv.shape, bf16),
@@ -1053,12 +1102,476 @@
             pltpu.VMEM((size - 1, share, SIDE_PAD), bf16),
         ]
         + [dma((2, 2, chunks))] * 5
-        + [dma((2, 2)), dma((16,)), dma((4, 10)), dma((4, 10)), dma((size - 1,)), dma((size - 1,))],
+        + [dma((2, 2)), dma((11,)), dma((4,)), dma((6, 10)), dma((6, 10)), dma((size - 1,)), dma((size - 1,))],
         compiler_params=pltpu.CompilerParams(
             collective_id=cid, has_side_effects=True, vmem_limit_bytes=60 * 2**20),
         cost_estimate=pl.CostEstimate(
             flops=2 * total * depth * side, bytes_accessed=400 * 2**20, transcendentals=0),
-    )(parts, up_grad, normed, d_attn, d_qkv, context, gain_cols)
+    )(parts, gate_grad, up_grad, normed, d_attn, d_qkv, context, gain_cols)
+
+CAP_SCALE = HEAD ** -0.5 / SOFTCAP
+
+
+def capped(query, keys):
+    raw = lax.dot_general(query, keys, (((1,), (1,)), ((), ())), preferred_element_type=jnp.float32)
+    curve = jnp.tanh(raw * CAP_SCALE)
+    return curve, jnp.exp(SOFTCAP * curve)
+
+
+def at_or_before(shape, row_at):
+    return lax.broadcasted_iota(jnp.int32, shape, 1) <= lax.broadcasted_iota(jnp.int32, shape, 0) + row_at
+
+
+def pick_rows(ref, rows, prompt, heads):
+    found = []
+    for m in range(2):
+        for h in range(heads):
+            found.append(ref[m * rows + prompt : (m + 1) * rows, h * HEAD : (h + 1) * HEAD])
+    return jnp.concatenate(found, axis=0)
+
+
+def cont_masks(prompt_of, group, cont, heads):
+    count = 2 * heads * cont
+    row = lax.broadcasted_iota(jnp.int32, (count, 1), 0)
+    sees = jnp.where(row < heads * cont, prompt_of[0], prompt_of[1]) == group
+    row = lax.broadcasted_iota(jnp.int32, (count, 2 * cont), 0)
+    key = lax.broadcasted_iota(jnp.int32, (count, 2 * cont), 1)
+    same = (row // (heads * cont)) == (key // cont)
+    return sees, same & (lax.rem(key, cont) <= lax.rem(row, cont))
+
+
+def turn(values, cosine, sine):
+    half = HEAD // 2
+    low, high = values[:, :half], values[:, half:]
+    return jnp.concatenate([low * cosine - high * sine, high * cosine + low * sine], axis=1)
+
+
+ROW_TILE = 256
+
+
+def head_kernel(
+    heads, cont,
+    prompt_of, token_ref, own_ref, angle_ref,
+    part_ref, context_ref, query_ref, kv_ref, other_ref, sum_ref, normed_ref, full_ref, gain_ref,
+    tokens, normed, full, cosine_sine, queries, kv, other, total, sums, context,
+    gather_in, gather_out, own_done, io_sem, swap_in, swap_out,
+):
+    rows_all, depth = tokens.shape
+    rows = rows_all // 2
+    prompt = rows - cont
+    query_width = heads * HEAD
+    qkv_width = query_width + 2 * HEAD
+    over_x, over_y, over_core = plane_partners()
+    seq = lax.axis_index("seq")
+    greet_plane(over_x, over_y, over_core, ())
+    share = own_ref.shape[0]
+    piece = share // 2
+    side = qkv_width + SIDE_PAD
+    pieces = (
+        (0, share, qkv_width, SIDE_PAD, SIDE_PAD),
+        (0, piece, 0, qkv_width, qkv_width // 2),
+        (piece, piece, 0, qkv_width, qkv_width // 2),
+        (0, share, side, query_width, query_width // 2),
+    )
+    first, second, third, finish, all_sent = plane_gather(full, own_ref, pieces, gather_in, gather_out, own_done)
+
+    def io(index, source, target):
+        return pltpu.make_async_copy(source, target, io_sem.at[index])
+
+    loads = [io(0, token_ref, tokens), io(1, angle_ref, cosine_sine)]
+    for u in (0, 1, 2):
+        first(u)
+    for copy in loads:
+        copy.start()
+    second(0)
+    third(0)
+    first(3)
+    for copy in loads:
+        copy.wait()
+    finish(0)
+    gain_ref[...] = jnp.transpose(full[:, qkv_width:side].astype(jnp.float32))[:8, :]
+
+    def normalize_rows(low, high):
+        @pl.loop(low, high)
+        def _(b):
+            span = pl.ds(pl.multiple_of(b * BLOCK, BLOCK), BLOCK)
+            values = tokens[span, :].astype(jnp.float32)
+            inv = lax.rsqrt(jnp.mean(values * values, axis=-1, keepdims=True) + EPS)
+            normed[span, :] = (values * inv * gain_ref[0:1, :]).astype(jnp.bfloat16)
+
+    blocks = rows_all // BLOCK
+    normalize_rows(0, blocks // 2)
+    second(1)
+    normalize_rows(blocks // 2, blocks)
+    second(2)
+    third(1)
+    second(3)
+    third(2)
+    for u in (1, 2):
+        finish(u)
+
+    stores = [io(2, normed, normed_ref)]
+    stores[0].start()
+    half = HEAD // 2
+
+    def project(m, low, count):
+        return jnp.dot(normed[pl.ds(m * rows, rows), :], full[:, low : low + count], preferred_element_type=jnp.float32)
+
+    def angles(m):
+        span = pl.ds(m * rows, rows)
+        return cosine_sine[span, :half], cosine_sine[span, half:]
+
+    def swap(m):
+        return pltpu.make_async_remote_copy(
+            kv.at[m, pl.ds(0, prompt)], other.at[m], swap_out.at[m], swap_in.at[m],
+            device_id=over_y, device_id_type=MESH)
+
+    for m in range(2):
+        kv[m, :, :HEAD] = turn(project(m, query_width, HEAD), *angles(m)).astype(jnp.bfloat16)
+        kv[m, :, HEAD:] = project(m, query_width + HEAD, HEAD).astype(jnp.bfloat16)
+        swap(m).start()
+    for m in range(2):
+        for h in range(heads):
+            queries[pl.ds(m * rows, rows), h * HEAD : (h + 1) * HEAD] = turn(
+                project(m, h * HEAD, HEAD), *angles(m)).astype(jnp.bfloat16)
+    third(3)
+    stores += [io(3, queries, query_ref), io(4, kv, kv_ref)]
+    stores[1].start()
+    stores[2].start()
+    lanes = sums.shape[-1]
+
+    def spots(i, low, count):
+        m, h = i // heads, lax.rem(i, heads)
+        return m, h, pl.ds(pl.multiple_of(m * rows + low, 16), count), pl.ds(pl.multiple_of(h * HEAD, HEAD), HEAD)
+
+    def attend(weights, values):
+        return jnp.dot(weights.astype(jnp.bfloat16), values, preferred_element_type=jnp.float32)
+
+    tiles = [(low, min(ROW_TILE, prompt - low)) for low in range(0, prompt, ROW_TILE)]
+
+    @pl.loop(0, 2 * heads)
+    def _(i):
+        for low, count in tiles:
+            m, h, span, across = spots(i, low, count)
+            reach = low + count
+            keys = kv[m, :reach, :HEAD]
+            values = kv[m, :reach, HEAD:]
+            _, weights = capped(queries[span, across], keys)
+            weights = jnp.where(at_or_before((count, reach), low), weights, 0.0)
+            sums[h, span, :] = jnp.broadcast_to(jnp.sum(weights, axis=1, keepdims=True), (count, lanes))
+            total[span, across] = attend(weights, values)
+
+    for m in range(2):
+        swap(m).wait_recv()
+
+    @pl.when(seq == 1)
+    def _():
+        @pl.loop(0, 2 * heads)
+        def _(i):
+            for low, count in tiles:
+                m, h, span, across = spots(i, low, count)
+                _, weights = capped(queries[span, across], other[m, :, :HEAD])
+                sums[h, span, :] += jnp.broadcast_to(jnp.sum(weights, axis=1, keepdims=True), (count, lanes))
+                total[span, across] += attend(weights, other[m, :, HEAD:])
+
+    picked = pick_rows(queries, rows, prompt, heads)
+    weight_sum = jnp.zeros((picked.shape[0], 1), jnp.float32)
+    weighted = jnp.zeros((picked.shape[0], HEAD), jnp.float32)
+    for g in range(2):
+        sees, near = cont_masks(prompt_of, g, cont, heads)
+        for pair in (kv[g, :prompt, :], other[g]):
+            _, weights = capped(picked, pair[:, :HEAD])
+            weights = jnp.where(sees, weights, 0.0)
+            weight_sum += jnp.sum(weights, axis=1, keepdims=True)
+            weighted += attend(weights, pair[:, HEAD:])
+    tail = jnp.concatenate([kv[m, prompt:, :] for m in range(2)], axis=0)
+    _, weights = capped(picked, tail[:, :HEAD])
+    weights = jnp.where(near, weights, 0.0)
+    weight_sum += jnp.sum(weights, axis=1, keepdims=True)
+    weighted += attend(weights, tail[:, HEAD:])
+    for m in range(2):
+        for h in range(heads):
+            low = (m * heads + h) * cont
+            span = pl.ds(m * rows + prompt, cont)
+            sums[h, span, :] = jnp.broadcast_to(weight_sum[low : low + cont], (cont, lanes))
+            total[span, h * HEAD : (h + 1) * HEAD] = weighted[low : low + cont]
+
+    for h in range(heads):
+        across = slice(h * HEAD, (h + 1) * HEAD)
+        inverse = 1.0 / sums[h, :, :1]
+        context[:, across] = (total[:, across] * inverse).astype(jnp.bfloat16)
+        sums[h, :, :] = jnp.broadcast_to(inverse, (rows_all, lanes))
+    finish(3)
+    stores += [io(5, context, context_ref), io(6, sums, sum_ref), io(7, other, other_ref), io(8, full, full_ref)]
+    for copy in stores[3:]:
+        copy.start()
+
+    @pl.loop(0, depth // TILE)
+    def _(i):
+        at = pl.ds(pl.multiple_of(i * TILE, TILE), TILE)
+        tokens[:, at] = lax.dot_general(
+            context[...], full[at, side : side + query_width], (((1,), (1,)), ((), ())),
+            preferred_element_type=jnp.float32).astype(jnp.bfloat16)
+
+    stores.append(io(9, tokens, part_ref))
+    stores[-1].start()
+    for m in range(2):
+        swap(m).wait_send()
+    all_sent()
+    for copy in stores:
+        copy.wait()
+
+
+def head_block(tokens, own, angles, prompt_of, heads, cont, cid):
+    rows, depth = tokens.shape
+    half_rows = rows // 2
+    prompt = half_rows - cont
+    width = heads * HEAD
+    group = lax.axis_size("dp") * lax.axis_size("seq")
+    bf16, f32 = jnp.bfloat16, jnp.float32
+    any_spec = pl.BlockSpec(memory_space=pl.ANY)
+    vmem_spec = pl.BlockSpec(memory_space=pltpu.VMEM)
+    dma = pltpu.SemaphoreType.DMA
+    full = (own.shape[0] * group, own.shape[1])
+    shape = jax.ShapeDtypeStruct
+    return pl.pallas_call(
+        functools.partial(head_kernel, heads, cont),
+        out_shape=(
+            shape((rows, depth), bf16),
+            shape((rows, width), bf16),
+            shape((rows, width), bf16),
+            shape((2, half_rows, 2 * HEAD), bf16),
+            shape((2, prompt, 2 * HEAD), bf16),
+            shape((heads, rows, 128), f32),
+            shape((rows, depth), bf16),
+            shape(full, bf16),
+            shape((8, depth), f32),
+        ),
+        in_specs=[pl.BlockSpec(memory_space=pltpu.SMEM)] + [any_spec] * 3,
+        out_specs=(any_spec,) * 8 + (vmem_spec,),
+        scratch_shapes=[
+            pltpu.VMEM((rows, depth), bf16),
+            pltpu.VMEM((rows, depth), bf16),
+            pltpu.VMEM(full, bf16),
+            pltpu.VMEM((rows, HEAD), f32),
+            pltpu.VMEM((rows, width), bf16),
+            pltpu.VMEM((2, half_rows, 2 * HEAD), bf16),
+            pltpu.VMEM((2, prompt, 2 * HEAD), bf16),
+            pltpu.VMEM((rows, width), f32),
+            pltpu.VMEM((heads, rows, 128), f32),
+            pltpu.VMEM((rows, width), bf16),
+            dma((4, 9)), dma((4, 9)), dma((4,)), dma((10,)), dma((2,)), dma((2,)),
+        ],
+        compiler_params=pltpu.CompilerParams(
+            collective_id=cid, has_side_effects=True, vmem_limit_bytes=56 * 2**20),
+        cost_estimate=pl.CostEstimate(
+            flops=2 * rows * depth * (full[1] + width), bytes_accessed=200 * 2**20, transcendentals=rows * 2048),
+    )(prompt_of, tokens, own, angles)
+def back_kernel(
+    heads, cont,
+    prompt_of, d_attn_ref, full_ref, query_ref, kv_ref, other_ref, context_ref, sum_ref, angle_ref, token_ref,
+    d_qkv_ref, part_ref, gain_ref,
+    d_attn, full, tokens, queries, kv, other, context, sums, cosine_sine,
+    d_context, d_query, d_kv, d_other, sent_kv, got_kv, d_qkv, inverses, d_picked,
+    io_sem, swap_in, swap_out,
+):
+    rows_all, depth = tokens.shape
+    rows = rows_all // 2
+    prompt = rows - cont
+    query_width = heads * HEAD
+    qkv_width = query_width + 2 * HEAD
+    side = qkv_width + SIDE_PAD
+    _, over_y, _ = plane_partners()
+    seq = lax.axis_index("seq")
+    barrier = pltpu.get_barrier_semaphore()
+    pl.semaphore_signal(barrier, inc=1, device_id=over_y, device_id_type=MESH)
+    pl.semaphore_wait(barrier, 1)
+
+    def io(index, source, target):
+        return pltpu.make_async_copy(source, target, io_sem.at[index])
+
+    def swap(m):
+        return pltpu.make_async_remote_copy(
+            sent_kv.at[m], got_kv.at[m], swap_out.at[m], swap_in.at[m], device_id=over_y, device_id_type=MESH)
+
+    pairs = (
+        (d_attn_ref, d_attn), (full_ref, full), (query_ref, queries), (kv_ref, kv), (other_ref, other),
+        (context_ref, context), (sum_ref, sums), (angle_ref, cosine_sine), (token_ref, tokens),
+    )
+    loads = [io(k, *pair) for k, pair in enumerate(pairs)]
+    for copy in loads:
+        copy.start()
+    for copy in loads[:2]:
+        copy.wait()
+    for m in range(2):
+        span = pl.ds(m * rows, rows)
+        d_context[span, :] = jnp.dot(
+            d_attn[span, :], full[:, side : side + query_width], preferred_element_type=jnp.float32
+        ).astype(jnp.bfloat16)
+    for copy in loads[2:]:
+        copy.wait()
+
+    def nt(left, right):
+        return lax.dot_general(left, right, (((1,), (1,)), ((), ())), preferred_element_type=jnp.float32)
+
+    def tn(left, right):
+        return lax.dot_general(left, right, (((0,), (0,)), ((), ())), preferred_element_type=jnp.float32)
+
+    def score_grads(query, above, found, inverse, pair, seen):
+        keys, values = pair[:, :HEAD], pair[:, HEAD:]
+        curve, weights = capped(query, keys)
+        weights = weights * inverse
+        if seen is not None:
+            weights = jnp.where(seen, weights, 0.0)
+        d_weights = nt(above, values)
+        inner = jnp.sum(found.astype(jnp.float32) * above.astype(jnp.float32), axis=1, keepdims=True)
+        d_scores = (weights * (d_weights - inner) * ((1.0 - curve * curve) * HEAD ** -0.5)).astype(jnp.bfloat16)
+        d_pair = jnp.concatenate([tn(d_scores, query), tn(weights.astype(jnp.bfloat16), above)], axis=1)
+        return jnp.dot(d_scores, keys, preferred_element_type=jnp.float32), d_pair
+
+    picked = [pick_rows(ref, rows, prompt, heads) for ref in (queries, d_context, context)]
+    picked_inverse = jnp.concatenate(
+        [sums[h, m * rows + prompt : (m + 1) * rows, :1] for m in range(2) for h in range(heads)], axis=0)
+    d_picked[...] = jnp.zeros_like(d_picked)
+    for g in range(2):
+        sees, near = cont_masks(prompt_of, g, cont, heads)
+        d_rows, d_pair = score_grads(*picked, picked_inverse, other[g], sees)
+        d_picked[...] += d_rows
+        d_other[g] = d_pair
+        d_rows, d_pair = score_grads(*picked, picked_inverse, kv[g, :prompt, :], sees)
+        d_picked[...] += d_rows
+        d_kv[g, :prompt, :] = d_pair
+    tail = jnp.concatenate([kv[m, prompt:, :] for m in range(2)], axis=0)
+    d_rows, d_pair = score_grads(*picked, picked_inverse, tail, near)
+    d_picked[...] += d_rows
+    for m in range(2):
+        d_kv[m, prompt:, :] = d_pair[m * cont : (m + 1) * cont]
+
+    def spots(i, low, count):
+        m, h = i // heads, lax.rem(i, heads)
+        return m, h, pl.ds(pl.multiple_of(m * rows + low, 16), count), pl.ds(pl.multiple_of(h * HEAD, HEAD), HEAD)
+
+    tiles = [(low, min(ROW_TILE, prompt - low)) for low in range(0, prompt, ROW_TILE)]
+
+    @pl.when(seq == 0)
+    def _():
+        d_query[...] = jnp.zeros_like(d_query)
+
+    @pl.when(seq == 1)
+    def _():
+        @pl.loop(0, 2 * heads)
+        def _(i):
+            for low, count in tiles:
+                m, h, span, across = spots(i, low, count)
+                d_rows, d_pair = score_grads(
+                    queries[span, across], d_context[span, across], context[span, across], sums[h, span, :1], other[m], None)
+                d_query[span, across] = d_rows
+                d_other[m] += d_pair
+
+    for m in range(2):
+        sent_kv[m] = d_other[m].astype(jnp.bfloat16)
+        swap(m).start()
+    for m in range(2):
+        for h in range(heads):
+            low = (m * heads + h) * cont
+            d_query[m * rows + prompt : (m + 1) * rows, h * HEAD : (h + 1) * HEAD] = d_picked[low : low + cont]
+
+    @pl.loop(0, 2 * heads)
+    def _(i):
+        for low, count in tiles:
+            m, h, span, across = spots(i, low, count)
+            reach = low + count
+            d_rows, d_pair = score_grads(
+                queries[span, across], d_context[span, across], context[span, across], sums[h, span, :1],
+                kv[m, :reach, :], at_or_before((count, reach), low))
+            d_query[span, across] += d_rows
+            d_kv[m, :reach, :] += d_pair
+
+    half = HEAD // 2
+
+    def turn_back_rows(values, span):
+        cosine, sine = cosine_sine[span, :half], cosine_sine[span, half:]
+        return turn(values, cosine, -sine).astype(jnp.bfloat16)
+
+    for m in range(2):
+        span = pl.ds(m * rows, rows)
+        for h in range(heads):
+            across = slice(h * HEAD, (h + 1) * HEAD)
+            d_qkv[span, across] = turn_back_rows(d_query[span, across], span)
+
+    @pl.loop(0, rows_all // BLOCK)
+    def _(b):
+        span = pl.ds(pl.multiple_of(b * BLOCK, BLOCK), BLOCK)
+        values = tokens[span, :].astype(jnp.float32)
+        inverse = lax.rsqrt(jnp.mean(values * values, axis=-1, keepdims=True) + EPS)
+        inverses[span, :] = jnp.broadcast_to(inverse, (BLOCK, inverses.shape[1]))
+
+    for m in range(2):
+        swap(m).wait_recv()
+        span = pl.ds(m * rows, rows)
+        d_kv[m, :prompt, :] += got_kv[m].astype(jnp.float32)
+        d_qkv[span, query_width : query_width + HEAD] = turn_back_rows(d_kv[m, :, :HEAD], span)
+        d_qkv[span, query_width + HEAD :] = d_kv[m, :, HEAD:].astype(jnp.bfloat16)
+    stores = [io(9, d_qkv, d_qkv_ref)]
+    stores[0].start()
+
+    @pl.loop(0, depth // TILE)
+    def _(i):
+        at = pl.ds(pl.multiple_of(i * TILE, TILE), TILE)
+        part = nt(d_qkv[...], full[at, :qkv_width])
+        normed = tokens[:, at].astype(jnp.float32) * inverses[:, :1]
+        gain_ref[0:1, at] = jnp.sum(part * normed, axis=0, keepdims=True)
+        d_attn[:, at] = part.astype(jnp.bfloat16)
+
+    stores.append(io(10, d_attn, part_ref))
+    stores[1].start()
+    for m in range(2):
+        swap(m).wait_send()
+    for copy in stores:
+        copy.wait()
+
+
+def back_block(prompt_of, d_attn, full, queries, kv, other, context, sums, angles, tokens, cont, cid):
+    rows, depth = tokens.shape
+    width = queries.shape[1]
+    heads = width // HEAD
+    qkv_width = width + 2 * HEAD
+    bf16, f32 = jnp.bfloat16, jnp.float32
+    any_spec = pl.BlockSpec(memory_space=pl.ANY)
+    vmem_spec = pl.BlockSpec(memory_space=pltpu.VMEM)
+    dma = pltpu.SemaphoreType.DMA
+    shape = jax.ShapeDtypeStruct
+    return pl.pallas_call(
+        functools.partial(back_kernel, heads, cont),
+        out_shape=(shape((rows, qkv_width), bf16), shape((rows, depth), bf16), shape((8, depth), f32)),
+        in_specs=[pl.BlockSpec(memory_space=pltpu.SMEM)] + [any_spec] * 9,
+        out_specs=(any_spec, any_spec, vmem_spec),
+        scratch_shapes=[
+            pltpu.VMEM(d_attn.shape, bf16),
+            pltpu.VMEM(full.shape, bf16),
+            pltpu.VMEM(tokens.shape, bf16),
+            pltpu.VMEM(queries.shape, bf16),
+            pltpu.VMEM(kv.shape, bf16),
+            pltpu.VMEM(other.shape, bf16),
+            pltpu.VMEM(context.shape, bf16),
+            pltpu.VMEM(sums.shape, f32),
+            pltpu.VMEM(angles.shape, f32),
+            pltpu.VMEM(queries.shape, bf16),
+            pltpu.VMEM(queries.shape, f32),
+            pltpu.VMEM(kv.shape, f32),
+            pltpu.VMEM(other.shape, f32),
+            pltpu.VMEM(other.shape, bf16),
+            pltpu.VMEM(other.shape, bf16),
+            pltpu.VMEM((rows, qkv_width), bf16),
+            pltpu.VMEM((rows, 128), f32),
+            pltpu.VMEM((2 * heads * cont, HEAD), f32),
+            dma((11,)), dma((2,)), dma((2,)),
+        ],
+        compiler_params=pltpu.CompilerParams(
+            collective_id=cid, has_side_effects=True, vmem_limit_bytes=56 * 2**20),
+        cost_estimate=pl.CostEstimate(
+            flops=2 * rows * depth * (qkv_width + width), bytes_accessed=150 * 2**20, transcendentals=rows * 2048),
+    )(prompt_of, d_attn, full, queries, kv, other, context, sums, angles, tokens)
 
 
 def normalize(values):
@@ -1123,7 +1636,7 @@
     return (curved, jnp.where(visible, SOFTCAP * curved, -1e30))
 
 
-def per_device(
+def per_device_general(
     tokens,
     cotangent,
     prompt_of,
@@ -1146,7 +1659,6 @@
     total_rows = micro_count * row_count
     score_scale = HEAD ** (-0.5)
     axes = ("dp", "seq")
-    planar = lax.axis_size("dp") == 4 and seq_count == 2
     query_width = query_weight.shape[1]
     qkv_width = query_width + 2 * HEAD
     f32, bf16 = jnp.float32, jnp.bfloat16
@@ -1168,11 +1680,8 @@
     full_out = lax.all_gather(out_weight, axes, axis=1, tiled=True)
     full_gate = lax.all_gather(gate_weight, axes, axis=0, tiled=True)
     down_turned = down_weight.T
-    if planar:
-        full_up, full_down = up_weight, down_turned
-    else:
-        full_up = lax.all_gather(up_weight, axes, axis=0, tiled=True)
-        full_down = lax.all_gather(down_turned, axes, axis=0, tiled=True)
+    full_up = lax.all_gather(up_weight, axes, axis=0, tiled=True)
+    full_down = lax.all_gather(down_turned, axes, axis=0, tiled=True)
     inputs = tokens.reshape(total_rows, model_width).astype(f32)
     normed_in = (normalize(inputs) * gain_float[0]).astype(bf16)
     key_value = jnp.dot(normed_in, full_qkv[:, query_width:], preferred_element_type=f32)
@@ -1182,14 +1691,7 @@
     key_grid = key_local.reshape(micro_count, row_count, HEAD)
     value_grid = value_local.reshape(micro_count, row_count, HEAD)
     own_pair = jnp.concatenate([key_grid[:, :prompt_dev], value_grid[:, :prompt_dev]], axis=2)
-    if seq_count == 2:
-        other_pair = lax.ppermute(own_pair, "seq", [(0, 1), (1, 0)])
-        early = seq_pos == 0
-        prompt_pair = jnp.concatenate(
-            [jnp.where(early, own_pair, other_pair), jnp.where(early, other_pair, own_pair)], axis=1
-        )
-    else:
-        prompt_pair = lax.all_gather(own_pair, "seq", axis=1, tiled=True)
+    prompt_pair = lax.all_gather(own_pair, "seq", axis=1, tiled=True)
     query_heads = jnp.dot(
         normed_in, full_qkv[:, :query_width], preferred_element_type=f32
     ).reshape(total_rows, -1, HEAD)
@@ -1277,16 +1779,9 @@
         ],
         axis=2,
     )
-    if seq_count == 2:
-        low_part, high_part = pair_grad[:, :prompt_dev], pair_grad[:, prompt_dev:]
-        early = seq_pos == 0
-        sent = jnp.where(early, high_part, low_part).astype(bf16)
-        kept = jnp.where(early, low_part, high_part)
-        pair_grad = kept + lax.ppermute(sent, "seq", [(0, 1), (1, 0)]).astype(f32)
-    else:
-        pair_grad = lax.psum_scatter(
-            pair_grad.astype(bf16), "seq", scatter_dimension=1, tiled=True
-        ).astype(f32)
+    pair_grad = lax.psum_scatter(
+        pair_grad.astype(bf16), "seq", scatter_dimension=1, tiled=True
+    ).astype(f32)
     prompt_key_grad, prompt_value_grad = pair_grad[..., :HEAD], pair_grad[..., HEAD:]
     own_keys = jnp.concatenate(
         [prompt_key_grad, key_grad[split_at:].reshape(micro_count, CONT, HEAD)], axis=1
@@ -1304,33 +1799,14 @@
     )
     gain_cols = jnp.pad(grad_gains.T, ((0, 0), (0, SIDE_PAD - grad_gains.shape[0])))
     attn_part = attn_part.astype(bf16)
-    if planar:
-        d_normed, share_up, share_side, share_gains = tail_block(
-            attn_part.reshape(micro_count, row_count, model_width),
-            block["grad_up"],
-            normed_in,
-            d_attn,
-            d_qkv,
-            context,
-            gain_cols.astype(bf16),
-            1,
-        )
-        d_normed, share_gate, share_down = lax.optimization_barrier(
-            (d_normed, share_gate, share_down)
-        )
-        d_normed = d_normed.reshape(total_rows, model_width)
-        share_up, share_side = share_up.astype(f32), share_side.astype(f32)
-        share_out = share_side[:, qkv_width : qkv_width + query_width].T
-        share_gains = share_gains[:, :4].T
-    else:
-        share_up = scatter(block["grad_up"], 0)
-        share_out = scatter(
-            jnp.einsum("rc,rd->cd", context, d_attn, preferred_element_type=f32), 1
-        )
-        side_grad = jnp.einsum("rd,rc->dc", normed_in, d_qkv, preferred_element_type=f32)
-        d_normed = chain_sum(attn_part, 1)
-        share_side = scatter(jnp.concatenate([side_grad, gain_cols], axis=1), 0)
-        share_gains = lax.psum(share_side[:, qkv_width : qkv_width + 4].T, "tensor")
+    share_up = scatter(block["grad_up"], 0)
+    share_out = scatter(
+        jnp.einsum("rc,rd->cd", context, d_attn, preferred_element_type=f32), 1
+    )
+    side_grad = jnp.einsum("rd,rc->dc", normed_in, d_qkv, preferred_element_type=f32)
+    d_normed = chain_sum(attn_part, 1)
+    share_side = scatter(jnp.concatenate([side_grad, gain_cols], axis=1), 0)
+    share_gains = lax.psum(share_side[:, qkv_width : qkv_width + 4].T, "tensor")
     d_in_norm = norm_back(inputs, gain_float[0], d_normed.astype(f32))
     input_grad = d_middle + d_in_norm
     return (
@@ -1345,6 +1821,119 @@
         share_down,
         share_gains,
     )
+
+
+def per_device_planar(
+    tokens,
+    cotangent,
+    prompt_of,
+    query_weight,
+    key_weight,
+    value_weight,
+    out_weight,
+    gate_weight,
+    up_weight,
+    down_weight,
+    norm_gains,
+):
+    micro_count, _, row_count, model_width = tokens.shape
+    seq_pos = lax.axis_index("seq")
+    total_rows = micro_count * row_count
+    axes = ("dp", "seq")
+    query_width = query_weight.shape[1]
+    qkv_width = query_width + 2 * HEAD
+    heads = query_width // HEAD
+    f32, bf16 = jnp.float32, jnp.bfloat16
+    owners = prompt_of[:, 0]
+    angles = turn_angles(row_count, seq_pos, micro_count)
+    flat = tokens.reshape(total_rows, model_width)
+    own_side = jnp.concatenate(
+        [
+            query_weight,
+            key_weight,
+            value_weight,
+            jnp.pad(norm_gains.T, ((0, 0), (0, SIDE_PAD - norm_gains.shape[0]))),
+            out_weight.T,
+        ],
+        axis=1,
+    )
+    attn_part, context, queries, own_kv, other_kv, sums, normed_in, full_side, gains = head_block(
+        flat, own_side, angles, owners, heads, CONT, 0
+    )
+    stacked = (micro_count, row_count, model_width)
+    block = ffn_block(
+        attn_part.reshape(stacked),
+        tokens[:, 0],
+        cotangent[:, 0],
+        gate_weight,
+        up_weight,
+        down_weight.T,
+        gains,
+        1,
+    )
+    gain_sums = jnp.sum(block["gain_grad"].reshape(3, 8, model_width), axis=1)
+    d_attn = block["d_attn"].reshape(total_rows, model_width)
+
+    def scatter(grad):
+        return lax.psum_scatter(grad, axes, scatter_dimension=0, tiled=True).astype(f32)
+
+    share_down = scatter(block["grad_down"]).T
+    d_qkv, attn_part, gain_first = back_block(
+        owners, d_attn, full_side, queries, own_kv, other_kv, context, sums, angles, flat, CONT, 2
+    )
+    grad_gains = jnp.concatenate(
+        [gain_first[:1], jnp.where(lax.axis_index("tensor") == 0, gain_sums, 0.0)], axis=0
+    )
+    gain_cols = jnp.pad(grad_gains.T, ((0, 0), (0, SIDE_PAD - grad_gains.shape[0])))
+    d_normed, share_gate, share_up, share_side, share_gains = tail_block(
+        attn_part.reshape(stacked),
+        block["grad_gate"],
+        block["grad_up"],
+        normed_in,
+        d_attn,
+        d_qkv,
+        context,
+        gain_cols.astype(bf16),
+        3,
+    )
+    d_normed, share_down = lax.optimization_barrier((d_normed, share_down))
+    share_side = share_side.astype(f32)
+    d_in_norm = norm_back(
+        flat.astype(f32), gains[0], d_normed.reshape(total_rows, model_width).astype(f32)
+    )
+    d_middle = block["d_middle"].reshape(total_rows, model_width).astype(f32)
+    return (
+        block["out"].reshape(tokens.shape),
+        (d_middle + d_in_norm).reshape(tokens.shape),
+        share_side[:, :query_width],
+        share_side[:, query_width : query_width + HEAD],
+        share_side[:, query_width + HEAD : qkv_width],
+        share_side[:, qkv_width : qkv_width + query_width].T,
+        share_gate.astype(f32),
+        share_up.astype(f32),
+        share_down,
+        share_gains[:, :4].T,
+    )
+
+
+def turn_angles(row_count, seq_pos, micro_count):
+    half_width = HEAD // 2
+    rows = jnp.arange(row_count)
+    prompt_dev = row_count - CONT
+    prompt_all = prompt_dev * lax.axis_size("seq")
+    places = jnp.where(
+        rows < prompt_dev, seq_pos * prompt_dev + rows, prompt_all + rows - prompt_dev
+    )
+    spectrum = THETA ** (-2.0 * jnp.arange(half_width, dtype=jnp.float32) / HEAD)
+    angles = places.astype(jnp.float32)[:, None] * spectrum
+    both = jnp.concatenate([jnp.cos(angles), jnp.sin(angles)], axis=1)
+    return jnp.tile(both, (micro_count, 1))
+
+
+def per_device(*arrays):
+    if lax.axis_size("dp") == 4 and lax.axis_size("seq") == 2:
+        return per_device_planar(*arrays)
+    return per_device_general(*arrays)
 
 
 def solution(mesh):

time: 917 us -> 813 us (0.89)
  Pallas kernels: 595 us -> 744 us
  waiting for transfers between devices: 103 us -> 0.02 us
  matrix products: 94.9 us -> 0 us
  other arithmetic: 73.8 us -> 30.5 us
  local copies, waits for them, and re-layouts: 27.4 us -> 15.7 us
    pallas_call x0 -> x2, Pallas kernels: none -> 132 us  [the longest x1 71.3 us: head_block(): pl.pallas_call(functools.partial(head_kernel, heads, cont), out_shape=(sh...]
    dot_general x17 -> x0, matrix products: 94.9 us -> none  [the longest x2 23 us: per_device(): jnp.einsum('rd,kd->rk', d_context[:, head_pos], value_rows, preferred_ele...]
    all_gather x3 -> x0, waiting for transfers between devices: 56.2 us -> none  [the longest x1 38.4 us: per_device(): full_side = lax.all_gather(side_weights, axes, axis=0, tiled=True)]
    ppermute x2 -> x0, waiting for transfers between devices: 44.9 us -> none  [the longest x1 24.5 us: per_device(): other_pair = lax.ppermute(own_pair, 'seq', [(0, 1), (1, 0)])]
    convert_element_type x11 -> x4, other arithmetic: 35.6 us -> 6.1 us  [the longest x1 2.99 us: per_device_planar(): share_gate.astype(f32)]
    pallas_call x1, Pallas kernels: 432 us -> 450 us  [ffn_block(): pl.pallas_call(functools.partial(ffn_kernel, size, width, bases, schedule...]
  transfers between devices with their start and end apart: 7 -> 1, of which waited for: 4 -> 0; matrix products, arithmetic and copies ran while one was open for 18% -> 2% of each run, Pallas kernels for 18% -> 28%
where the time goes in v6:
time: 813 us; the launch traced here: 804 us
  Pallas kernels  744 us (92%)
  other arithmetic  30.5 us (4%)
  local copies, waits for them, and re-layouts  15.7 us (2%)
  between operations  14.4 us (2%)
    pallas_call x1, Pallas kernels, ffn_block(): pl.pallas_call(functools.partial(ffn_kernel, size, width, bases, schedule...  450 us
    pallas_call x1, Pallas kernels, tail_block(): pl.pallas_call(functools.partial(tail_kernel, size, width, bases), out_sh...  162 us
    pallas_call x1, Pallas kernels, head_block(): pl.pallas_call(functools.partial(head_kernel, heads, cont), out_shape=(sh...  71.3 us
    pallas_call x1, Pallas kernels, back_block(): pl.pallas_call(functools.partial(back_kernel, heads, cont), out_shape=(sh...  60.7 us
  transfers between devices with their start and end apart: 1, of which 0 were waited for; matrix products, arithmetic and copies ran while one was open for 2% of the time, Pallas kernels for 28%

profile of v6, /device:TPU:0, one launch (start us, length us, event | category | flops | bytes accessed | tf_op | source)
XLA Modules:
  0.0 804.2 jit_solution(17611958972162814406)
XLA Ops:
  7.2 0.0 reduce-scatter.2.cloned.1.call-start
  7.3 1.0 constant_dynamic-update-slice_fusion.2
  8.2 0.8 copy.27
  9.1 1.0 multiply_cosine_fusion
  10.2 0.9 constant_dynamic-update-slice_fusion.1
  11.1 0.9 constant_dynamic-update-slice_fusion
  12.1 1.0 bitcast_dynamic-update-slice_fusion.own_ref
  13.0 0.0 copy-start.4
  13.1 1.2 tile.4
  14.2 0.1 copy-done.4
  14.3 71.3 %shard_map.186 = (bf16[1088,2304]{1,0:T(8,128)(2,1)}, bf16[1088,512]{1,0:T(8,128)(2,1)}, bf16[1088,512]{1,0:T(8,128)(2,1)}, bf16[2,544,512]{2,1,0:T(8,128)(2,1)}...) custom-call(s32[2]{0:T(128)} %bitcast.52, ...), custom_call_target="tpu_custom_call" | custom-call | flops 10909384704 | bytes 209715200 | tf_op jit(solution)/shard_map/pallas_call | solution.py:1337
  85.6 449.8 %shard_map.187 = (bf16[6,544,2304]{2,1,0:T(8,128)(2,1)}, bf16[2,544,2304]{2,1,0:T(8,128)(2,1)}, bf16[2,544,2304]{2,1,0:T(8,128)(2,1)}, bf16[2,544,2304]{2,1,0:T(...) custom-call(bf16[2,544,2304]{2,1,0:T(8,128)(2,1)} %bitcast.54, ...), custom_call_target="tpu_custom_call" | custom-call | flops 103960018944 | bytes 1073741824 | tf_op jit(solution)/shard_map/pallas_call | solution.py:790
  535.5 0.0 reduce-scatter.2.cloned.1.call-update
  535.5 0.0 copy-start.2
  535.5 60.7 %shard_map.188 = (bf16[1088,1024]{1,0:T(8,128)(2,1)}, bf16[1088,2304]{1,0:T(8,128)(2,1)}, f32[8,2304]{1,0:T(8,128)}) custom-call(s32[2]{0:T(128)} %bitcast.53, bf16[1088,2304]{1,0:T(8,128)(2,1)} %bitcast.43, bf16[2304,1664]{1,0:T(8,128)(2,1)} %get-tuple-element.41.full_ref, bf16[1088,512]{1,0:T(8,128)(2,1)} %get-tuple-element.42.query_ref, ...), custom_call_target="tpu_custom_call" | custom-call | flops 7700742144 | bytes 157286400 | tf_op jit(solution)/shard_map/pallas_call | solution.py:1544
  596.2 0.9 slice.38
  597.1 0.0 copy-done.2
  597.1 0.1 bitcast_reduce_fusion
  597.2 0.3 copy.29
  597.6 0.9 pad.10.gain_ref
  598.5 161.7 %shard_map.189 = (bf16[2,544,2304]{2,1,0:T(8,128)(2,1)}, bf16[288,2304]{1,0:T(8,128)(2,1)}, bf16[288,2304]{1,0:T(8,128)(2,1)}, bf16[288,1664]{1,0:T(8,128)(2,1)}, f32[288,128]{1,0:T(8,128)}) custom-call(bf16[2,544,2304]{2,1,0:T(8,128)(2,1)} %bitcast.45, bf16[2304,2304]{1,0:T(8,128)(2,1)} %get-tuple-element.48.gate_grad_ref, ...), custom_call_target="tpu_custom_call" | custom-call | flops 8342470656 | bytes 419430400 | tf_op jit(solution)/shard_map/pallas_call | solution.py:1077
  760.2 0.0 copy-start.1
  760.3 1.4 convert_element_type.49
  761.7 0.0 copy-start.3
  761.7 1.9 slice.30
  763.6 3.0 convert_element_type.50
  766.6 0.0 copy-start
  766.6 0.0 copy-done.1
  766.6 1.7 convert_element_type.51
  768.2 0.0 copy-done.3
  768.3 0.7 copy.32
  769.0 0.9 slice_reduce_fusion
  769.9 3.5 fusion
  773.4 0.0 copy-done
  773.4 0.9 fusion.6
  774.2 0.0 slice-start
  774.2 0.9 slice_bitcast_fusion
  775.1 0.0 reduce-scatter.2.cloned.1.call-done
  775.1 3.0 convert_bitcast_fusion
  778.1 0.0 slice-start.1
  778.1 0.0 slice-start.2
  778.1 6.2 multiply_reduce_fusion
  784.3 0.0 slice-done
  784.3 0.0 slice-done.1
  784.3 0.0 slice-start.3
  784.4 10.5 %fusion.5 = f32[2,1,544,2304]{3,2,1,0:T(8,128)} fusion(bf16[2,544,2304]{2,1,0:T(8,128)(2,1)} %get-tuple-element.56, bf16[2,544,2304]{2,1,0:T(8,128)(2,1)} %get-tuple-element.39, bf16[2,1,544,2304]{3,2,1,0:T(8,128)(2,1)S(1)} %bitcast.39, f32[2,544]{1,0:T(2,128)S(1)} %broadcast_multiply_fusion, f32[2304]{0:T(1024)S(1)} %slice_reduce_fusion, ...), kind=kLoop, calls=%fused_computation.7 | loop fusion | flops 22560768 | bytes 25085440
  794.9 0.0 slice-done.2
  794.9 0.0 slice-done.3
  794.9 2.3 copy.38
  (11 shorter events, 0.2 us)
Async XLA Ops:
  7.2 767.9 %reduce-scatter.2.cloned.1.call-start = ((), (), s32[]{:S(2)}) async-start(), calls=%async_computation.1 | async-start | bytes 11943936 | tf_op jit(solution)/shard_map/reduce_scatter | solution.py:1878
  13.0 1.3 copy-start.4
  535.5 61.6 %copy-start.2 = (f32[24,2304]{1,0:T(8,128)S(1)}, f32[24,2304]{1,0:T(8,128)}, u32[]{:S(2)}) copy-start(f32[24,2304]{1,0:T(8,128)} %get-tuple-element.53) | copy-start | bytes 663556
  760.2 6.3 copy-start.1
  761.7 6.6 copy-start.3
  766.6 6.8 copy-start
  774.2 10.1 %slice-start = ((s8[5013504]{0:T(1024)(128)(4,1)}), s8[819200]{0:T(1024)(128)(4,1)S(1)}, s32[]{:S(2)}) async-start(s8[5013504]{0:T(1024)(128)(4,1)} %bitcast.38), calls=%async_computation.2 | async-start | bytes 1638400
  778.1 6.2 slice-start.1
  778.1 16.7 %slice-start.2 = ((s8[5013504]{0:T(1024)(128)(4,1)}), s8[819200]{0:T(1024)(128)(4,1)S(1)}, s32[]{:S(2)}) async-start(s8[5013504]{0:T(1024)(128)(4,1)} %bitcast.40), calls=%async_computation.4 | async-start | bytes 1638400
  784.3 10.5 %slice-start.3 = ((s8[5013504]{0:T(1024)(128)(4,1)}), s8[4194304]{0:T(1024)(128)(4,1)S(1)}, s32[]{:S(2)}) async-start(s8[5013504]{0:T(1024)(128)(4,1)} %bitcast.40), calls=%async_computation.5 | async-start | bytes 8388608
Sparse Core Ops, SparseCore 0:
  535.6 102.2 reduce-scatter.1

commit v7 on v6

--- a/solution.py
+++ b/solution.py
@@ -138,6 +138,8 @@
 
 TILE = 256
 STAGES = 6
+NORM_ROWS = 32
+NORM_TICKS = 3
 LAG = 2
 PACE = 1
 
@@ -455,12 +457,13 @@
         return pltpu.make_async_copy(source, target, io_sem.at[index])
 
     def row_blocks(body, clock):
-        count = rows // BLOCK
-        for low, high, s in ((0, count // 2, clock), (count // 2, count, clock + 1)):
+        count = rows // NORM_ROWS
+        marks = [count * k // NORM_TICKS for k in range(NORM_TICKS + 1)]
+        for k, (low, high) in enumerate(zip(marks, marks[1:])):
             @pl.loop(low, high)
             def _(b):
-                body(pl.ds(pl.multiple_of(b * BLOCK, BLOCK), BLOCK))
-            tick(s)
+                body(pl.ds(pl.multiple_of(b * NORM_ROWS, NORM_ROWS), NORM_ROWS))
+            tick(clock + k)
 
     def own_rows(m):
         return pl.ds(m * rows, rows)
@@ -522,7 +525,7 @@
             d_ffn = inv * (scaled - normed * jnp.mean(scaled * normed, axis=-1, keepdims=True))
             stage_c[span, :] = d_ffn.astype(jnp.bfloat16)
             term = above * normed
-            gain_grad_ref[16:24, :] += term[:8] + term[8:]
+            gain_grad_ref[16:24, :] += jnp.sum(term.reshape(NORM_ROWS // 8, 8, depth), axis=0)
         row_blocks(body, clock)
 
     def d_hidden(m, clock):
@@ -556,13 +559,13 @@
             d_middle = stage_c[span, :].astype(jnp.float32) + inv * (
                 scaled - normed * jnp.mean(scaled * normed, axis=-1, keepdims=True))
             term = below * normed
-            gain_grad_ref[8:16, :] += term[:8] + term[8:]
+            gain_grad_ref[8:16, :] += jnp.sum(term.reshape(NORM_ROWS // 8, 8, depth), axis=0)
             stage_c[span, :] = d_middle.astype(jnp.bfloat16)
             scaled = d_middle * gain(1)
             d_attn = attn_inv * (scaled - attn_normed * jnp.mean(scaled * attn_normed, axis=-1, keepdims=True))
             stage_f[span, :] = d_attn.astype(jnp.bfloat16)
             term = d_middle * attn_normed
-            gain_grad_ref[0:8, :] += term[:8] + term[8:]
+            gain_grad_ref[0:8, :] += jnp.sum(term.reshape(NORM_ROWS // 8, 8, depth), axis=0)
         row_blocks(body, clock)
 
     def tall_copy(source, i, slot, m):
@@ -625,11 +628,8 @@
     def load(index, source, target):
         return pltpu.make_async_copy(source, target, io_sem.at[index])
 
-    def bring(m, third=None, fourth=None):
-        found = [load(2, token_ref.at[m], stage_t), load(3, sum_ref.at[m], stage_a)]
-        if third is not None:
-            found += [load(4, third, stage_f), load(5, fourth, stage_c)]
-        return found
+    def bring(m):
+        return [load(2, token_ref.at[m], stage_t), load(3, sum_ref.at[m], stage_a)]
 
     def start(copies):
         for copy in copies:
@@ -658,16 +658,23 @@
             moved(phase, u)
     ticks(clock, whole)
     kept = []
+    loads = [load(2, token_ref.at[0], stage_t)]
+    start(loads)
     for m in range(micro):
         norm_s, gate_s, down_s, end_s = schedule["forward"][m]
         settle(m)
+        loads.append(load(3, sum_ref.at[m], stage_a))
+        loads[-1].start()
         wait(kept)
-        loads = bring(m)
-        start(loads)
         wait(loads)
         norm_before(m, norm_s)
         kept = [load(6, stage_f, ffn_in_ref.at[m]), load(7, stage_c, hidden_ref.at[m])]
         kept[0].start()
+        if m + 1 < micro:
+            loads = [load(2, token_ref.at[m + 1], stage_t)]
+        else:
+            loads = bring(0)
+        start(loads)
         if m == 0:
             moved(2, 3)
             for u in range(4):
@@ -682,31 +689,40 @@
         prime(row_copy, (down_ref,))
         prime(col_copy, (gate_ref, up_ref) if m + 1 < micro else (down_ref,))
         down_proj(m, down_s)
+        if m + 1 == micro:
+            wait(kept)
+            loads.append(load(5, cot_ref.at[0], stage_c))
+            loads[-1].start()
         ticks(down_s + -(-depth // (TILE * PACE)), end_s)
-    wait(kept)
+    kept = []
     for m in range(micro):
         norm_s, dh_s, di_s, end_s = schedule["backward"][m]
         settle(micro + m)
-        if m:
-            wait(kept)
-        loads = bring(m, sum_ref.at[micro + m], cot_ref.at[m])
-        start(loads)
+        wait(kept[:1])
+        loads.append(load(4, sum_ref.at[micro + m], stage_f))
+        loads[-1].start()
         wait(loads)
         norm_after(m, norm_s)
         kept = [load(6, stage_f, out_ref.at[m]), load(7, stage_c, d_ffn_ref.at[m])]
         start(kept)
+        after = (m + 1) % micro
+        loads = bring(after)
+        start(loads)
         prime(row_copy, (gate_ref, up_ref))
         d_hidden(m, dh_s)
         sent(micro + m)
         if m + 1 < micro:
             prime(col_copy, (down_ref,))
+        kept[1].wait()
+        loads.append(load(5, cot_ref.at[after], stage_c))
+        loads[-1].start()
         d_input(m, di_s)
         ticks(di_s + -(-depth // (TILE * PACE)), end_s)
-    wait(kept)
     norm_s, grads_s, down_s, end_s = schedule["grads"]
     settle(2 * micro)
-    loads = bring(0, sum_ref.at[2 * micro], cot_ref.at[0])
-    start(loads)
+    wait(kept[:1])
+    loads.append(load(4, sum_ref.at[2 * micro], stage_f))
+    loads[-1].start()
     for m in range(micro):
         tall_copy(ffn_in_ref, 0, 0, m).start()
     wait(loads)
@@ -722,7 +738,7 @@
     wait(hidden_loads)
     weight_grads(d_ffn_ref, ((stage, grad_down_ref),), steps, down_s)
     wait(kept)
-    tail = bring(1, None)
+    tail = bring(1)
     tail.append(load(5, cot_ref.at[1], stage_c))
     start(tail)
     ticks(down_s + steps, end_s)
@@ -751,7 +767,7 @@
     forward = []
     for m in range(2):
         norm_s = at
-        gate_s = norm_s + 2
+        gate_s = norm_s + NORM_TICKS
         down_s = gate_s + tiles
         bases.append(max(down_s, bases[-1] + chunks))
         at = max(down_s + tiles, bases[m + 1] + whole)
@@ -759,12 +775,12 @@
     backward = []
     for m in range(2):
         norm_s = at
-        dh_s = norm_s + 2
+        dh_s = norm_s + NORM_TICKS
         di_s = dh_s + tiles
         bases.append(max(di_s, bases[-1] + chunks))
         at = max(di_s + tiles, bases[m + 3] + whole)
         backward.append((norm_s, dh_s, di_s, at))
-    grads_s = at + 2
+    grads_s = at + NORM_TICKS
     grads = (at, grads_s, grads_s + tiles, max(grads_s + 2 * tiles, bases[-1] + whole))
     return tuple(bases), {
         "attn": attn, "forward": tuple(forward), "backward": tuple(backward), "grads": grads
@@ -1574,6 +1590,56 @@
     )(prompt_of, d_attn, full, queries, kv, other, context, sums, angles, tokens)
 
 
+FINAL_ROWS = 64
+
+
+def final_kernel(
+    sums_ref, token_ref, middle_ref, layer_ref, gain_ref, gate_ref, up_ref, down_ref, side_ref,
+    layer_out, grad_ref, gate_out, up_out, down_out, query_out, key_out, value_out, out_out,
+):
+    values = token_ref[...].astype(jnp.float32)
+    inverse = lax.rsqrt(jnp.mean(values * values, axis=-1, keepdims=True) + EPS)
+    normed = values * inverse
+    scaled = sums_ref[...].astype(jnp.float32) * gain_ref[0:1, :]
+    backed = inverse * (scaled - normed * jnp.mean(scaled * normed, axis=-1, keepdims=True))
+    grad_ref[...] = middle_ref[...].astype(jnp.float32) + backed
+    layer_out[...] = layer_ref[...]
+    for source, target in ((gate_ref, gate_out), (up_ref, up_out), (down_ref, down_out)):
+        target[...] = source[...].astype(jnp.float32)
+    low = 0
+    for target in (query_out, key_out, value_out, out_out):
+        target[...] = side_ref[:, low : low + target.shape[1]].astype(jnp.float32)
+        low += target.shape[1]
+
+
+def final_block(sums, tokens, middle, layer, gains, gate, up, down, side, query_width):
+    rows, depth = tokens.shape
+    share, units = gate.shape
+    steps = share // BLOCK
+    blocks = -(-rows // FINAL_ROWS)
+    f32 = jnp.float32
+
+    def wide(width):
+        return pl.BlockSpec((FINAL_ROWS, width), lambda i: (jnp.minimum(i, blocks - 1), 0))
+
+    def thin(width):
+        return pl.BlockSpec((BLOCK, width), lambda i: (i, 0))
+
+    widths = (units, units, units, query_width, HEAD, HEAD, query_width)
+    return pl.pallas_call(
+        final_kernel,
+        grid=(steps,),
+        out_shape=(jax.ShapeDtypeStruct((rows, depth), layer.dtype), jax.ShapeDtypeStruct((rows, depth), f32))
+        + tuple(jax.ShapeDtypeStruct((share, width), f32) for width in widths),
+        in_specs=[wide(depth)] * 4
+        + [pl.BlockSpec(gains.shape, lambda i: (0, 0))]
+        + [thin(units)] * 3
+        + [thin(side.shape[1])],
+        out_specs=(wide(depth),) * 2 + tuple(thin(width) for width in widths),
+        compiler_params=pltpu.CompilerParams(vmem_limit_bytes=60 * 2**20),
+    )(sums, tokens, middle, layer, gains, gate, up, down, side)
+
+
 def normalize(values):
     return values * lax.rsqrt(jnp.mean(values * values, axis=-1, keepdims=True) + EPS)
 
@@ -1843,7 +1909,7 @@
     query_width = query_weight.shape[1]
     qkv_width = query_width + 2 * HEAD
     heads = query_width // HEAD
-    f32, bf16 = jnp.float32, jnp.bfloat16
+    bf16 = jnp.bfloat16
     owners = prompt_of[:, 0]
     angles = turn_angles(row_count, seq_pos, micro_count)
     flat = tokens.reshape(total_rows, model_width)
@@ -1875,9 +1941,9 @@
     d_attn = block["d_attn"].reshape(total_rows, model_width)
 
     def scatter(grad):
-        return lax.psum_scatter(grad, axes, scatter_dimension=0, tiled=True).astype(f32)
-
-    share_down = scatter(block["grad_down"]).T
+        return lax.psum_scatter(grad, axes, scatter_dimension=0, tiled=True)
+
+    share_down = scatter(block["grad_down"])
     d_qkv, attn_part, gain_first = back_block(
         owners, d_attn, full_side, queries, own_kv, other_kv, context, sums, angles, flat, CONT, 2
     )
@@ -1897,21 +1963,29 @@
         3,
     )
     d_normed, share_down = lax.optimization_barrier((d_normed, share_down))
-    share_side = share_side.astype(f32)
-    d_in_norm = norm_back(
-        flat.astype(f32), gains[0], d_normed.reshape(total_rows, model_width).astype(f32)
-    )
-    d_middle = block["d_middle"].reshape(total_rows, model_width).astype(f32)
+    layer, input_grad, *grads = final_block(
+        d_normed.reshape(total_rows, model_width),
+        flat,
+        block["d_middle"].reshape(total_rows, model_width),
+        block["out"].reshape(total_rows, model_width),
+        gains,
+        share_gate,
+        share_up,
+        share_down,
+        share_side,
+        query_width,
+    )
+    grad_gate, grad_up, grad_down, grad_query, grad_key, grad_value, grad_out = grads
     return (
-        block["out"].reshape(tokens.shape),
-        (d_middle + d_in_norm).reshape(tokens.shape),
-        share_side[:, :query_width],
-        share_side[:, query_width : query_width + HEAD],
-        share_side[:, query_width + HEAD : qkv_width],
-        share_side[:, qkv_width : qkv_width + query_width].T,
-        share_gate.astype(f32),
-        share_up.astype(f32),
-        share_down,
+        layer.reshape(tokens.shape),
+        input_grad.reshape(tokens.shape),
+        grad_query,
+        grad_key,
+        grad_value,
+        grad_out.T,
+        grad_gate,
+        grad_up,
+        grad_down.T,
         share_gains[:, :4].T,
     )
 

time: 813 us -> 770 us (0.947)
  other arithmetic: 30.5 us -> 1.2 us
    pallas_call x1, Pallas kernels: 450 us -> 421 us  [ffn_block(): pl.pallas_call(functools.partial(ffn_kernel, size, width, bases, schedule...]
    pallas_call x0 -> x1, Pallas kernels: none -> 24.3 us  [final_block(): pl.pallas_call(final_kernel, grid=(steps,), out_shape=(jax.ShapeDtypeStru...]
    unnamed x3 -> x0, other arithmetic: 10.5 us -> none
    reduce_sum x2 -> x0, other arithmetic: 9.66 us -> none  [the longest x1 6.18 us: norm_back(): jnp.mean(scaled * normed, axis=-1, keepdims=True)]
  transfers between devices with their start and end apart: 1 -> 1, of which waited for: 0 -> 0; matrix products, arithmetic and copies ran while one was open for 2% -> 1% of each run, Pallas kernels for 28% -> 29%
where the time goes in v7:
time: 770 us; the launch traced here: 762 us
  Pallas kernels  736 us (96%)
  between operations  14.6 us (2%)
  local copies, waits for them, and re-layouts  9.77 us (1%)
    pallas_call x1, Pallas kernels, ffn_block(): pl.pallas_call(functools.partial(ffn_kernel, size, width, bases, schedule...  421 us
    pallas_call x1, Pallas kernels, tail_block(): pl.pallas_call(functools.partial(tail_kernel, size, width, bases), out_sh...  163 us
    pallas_call x1, Pallas kernels, head_block(): pl.pallas_call(functools.partial(head_kernel, heads, cont), out_shape=(sh...  71.3 us
    pallas_call x1, Pallas kernels, back_block(): pl.pallas_call(functools.partial(back_kernel, heads, cont), out_shape=(sh...  56.6 us
    pallas_call x1, Pallas kernels, final_block(): pl.pallas_call(final_kernel, grid=(steps,), out_shape=(jax.ShapeDtypeStru...  24.3 us
  transfers between devices with their start and end apart: 1, of which 0 were waited for; matrix products, arithmetic and copies ran while one was open for 1% of the time, Pallas kernels for 29%

profile of v7, /device:TPU:0, one launch (start us, length us, event | category | flops | bytes accessed | tf_op | source)
XLA Modules:
  0.0 762.1 jit_solution(13824399697533627936)
XLA Ops:
  7.2 0.0 reduce-scatter.2.cloned.1.call-start
  7.3 0.8 copy.26
  8.1 1.0 constant_dynamic-update-slice_fusion.2
  9.1 1.0 multiply_cosine_fusion
  10.2 0.9 constant_dynamic-update-slice_fusion.1
  11.1 0.9 constant_dynamic-update-slice_fusion
  12.1 1.0 bitcast_dynamic-update-slice_fusion.own_ref
  13.0 0.0 copy-start.1
  13.1 1.2 tile.4
  14.2 0.1 copy-done.1
  14.3 71.3 %shard_map.186 = (bf16[1088,2304]{1,0:T(8,128)(2,1)}, bf16[1088,512]{1,0:T(8,128)(2,1)}, bf16[1088,512]{1,0:T(8,128)(2,1)}, bf16[2,544,512]{2,1,0:T(8,128)(2,1)}...) custom-call(s32[2]{0:T(128)} %bitcast.48, ...), custom_call_target="tpu_custom_call" | custom-call | flops 10909384704 | bytes 209715200 | tf_op jit(solution)/shard_map/pallas_call | solution.py:1353
  85.6 421.3 %shard_map.187 = (bf16[6,544,2304]{2,1,0:T(8,128)(2,1)}, bf16[2,544,2304]{2,1,0:T(8,128)(2,1)}, bf16[2,544,2304]{2,1,0:T(8,128)(2,1)}, bf16[2,544,2304]{2,1,0:T(...) custom-call(bf16[2,544,2304]{2,1,0:T(8,128)(2,1)} %bitcast.50, ...), custom_call_target="tpu_custom_call" | custom-call | flops 103960018944 | bytes 1073741824 | tf_op jit(solution)/shard_map/pallas_call | solution.py:806
  506.9 0.0 reduce-scatter.2.cloned.1.call-update
  506.9 0.0 copy-start
  506.9 56.6 %shard_map.188 = (bf16[1088,1024]{1,0:T(8,128)(2,1)}, bf16[1088,2304]{1,0:T(8,128)(2,1)}, f32[8,2304]{1,0:T(8,128)}) custom-call(s32[2]{0:T(128)} %bitcast.49, bf16[1088,2304]{1,0:T(8,128)(2,1)} %bitcast.34, bf16[2304,1664]{1,0:T(8,128)(2,1)} %get-tuple-element.48.full_ref, bf16[1088,512]{1,0:T(8,128)(2,1)} %get-tuple-element.49.query_ref, ...), custom_call_target="tpu_custom_call" | custom-call | flops 7700742144 | bytes 157286400 | tf_op jit(solution)/shard_map/pallas_call | solution.py:1560
  563.5 0.9 slice.12
  564.4 0.0 copy-done
  564.4 0.1 bitcast_reduce_fusion
  564.5 0.3 copy.27
  564.9 0.9 pad.10.gain_ref
  565.8 163.1 %shard_map.189 = (bf16[2,544,2304]{2,1,0:T(8,128)(2,1)}, bf16[288,2304]{1,0:T(8,128)(2,1)}, bf16[288,2304]{1,0:T(8,128)(2,1)}, bf16[288,1664]{1,0:T(8,128)(2,1)}, f32[288,128]{1,0:T(8,128)}) custom-call(bf16[2,544,2304]{2,1,0:T(8,128)(2,1)} %bitcast.36, bf16[2304,2304]{1,0:T(8,128)(2,1)} %get-tuple-element.55.gate_grad_ref, ...), custom_call_target="tpu_custom_call" | custom-call | flops 8342470656 | bytes 419430400 | tf_op jit(solution)/shard_map/pallas_call | solution.py:1093
  728.9 0.9 slice_bitcast_fusion
  729.8 0.7 copy.30
  730.5 0.0 reduce-scatter.2.cloned.1.call-done.down_ref
  730.5 24.3 %shard_map.190 = (bf16[1088,2304]{1,0:T(8,128)(2,1)}, f32[1088,2304]{1,0:T(8,128)}, f32[288,2304]{1,0:T(8,128)}, f32[288,2304]{1,0:T(8,128)}, f32[288,2304]{1,0:...) custom-call(bf16[1088,2304]{1,0:T(8,128)(2,1)} %bitcast.37, ...), custom_call_target="tpu_custom_call" | custom-call | tf_op jit(solution)/shard_map/pallas_call | solution.py:1629
  (6 shorter events, 0.1 us)
Async XLA Ops:
  7.2 723.3 %reduce-scatter.2.cloned.1.call-start = ((), (), s32[]{:S(2)}) async-start(), calls=%async_computation.1 | async-start | bytes 11943936 | tf_op jit(solution)/shard_map/reduce_scatter | solution.py:1944
  13.0 1.3 copy-start.1
  506.9 57.5 %copy-start = (f32[24,2304]{1,0:T(8,128)S(1)}, f32[24,2304]{1,0:T(8,128)}, u32[]{:S(2)}) copy-start(f32[24,2304]{1,0:T(8,128)} %get-tuple-element.60) | copy-start | bytes 663556
Sparse Core Ops, SparseCore 0:
  507.1 99.9 reduce-scatter.1

commit v8 on v7

--- a/solution.py
+++ b/solution.py
@@ -1170,7 +1170,7 @@
     prompt_of, token_ref, own_ref, angle_ref,
     part_ref, context_ref, query_ref, kv_ref, other_ref, sum_ref, normed_ref, full_ref, gain_ref,
     tokens, normed, full, cosine_sine, queries, kv, other, total, sums, context,
-    gather_in, gather_out, own_done, io_sem, swap_in, swap_out,
+    gather_in, gather_out, own_done, io_sem, part_sem, swap_in, swap_out,
 ):
     rows_all, depth = tokens.shape
     rows = rows_all // 2
@@ -1233,9 +1233,8 @@
     def project(m, low, count):
         return jnp.dot(normed[pl.ds(m * rows, rows), :], full[:, low : low + count], preferred_element_type=jnp.float32)
 
-    def angles(m):
-        span = pl.ds(m * rows, rows)
-        return cosine_sine[span, :half], cosine_sine[span, half:]
+    def angles():
+        return cosine_sine[:, :half], cosine_sine[:, half:]
 
     def swap(m):
         return pltpu.make_async_remote_copy(
@@ -1243,13 +1242,13 @@
             device_id=over_y, device_id_type=MESH)
 
     for m in range(2):
-        kv[m, :, :HEAD] = turn(project(m, query_width, HEAD), *angles(m)).astype(jnp.bfloat16)
+        kv[m, :, :HEAD] = turn(project(m, query_width, HEAD), *angles()).astype(jnp.bfloat16)
         kv[m, :, HEAD:] = project(m, query_width + HEAD, HEAD).astype(jnp.bfloat16)
         swap(m).start()
     for m in range(2):
         for h in range(heads):
             queries[pl.ds(m * rows, rows), h * HEAD : (h + 1) * HEAD] = turn(
-                project(m, h * HEAD, HEAD), *angles(m)).astype(jnp.bfloat16)
+                project(m, h * HEAD, HEAD), *angles()).astype(jnp.bfloat16)
     third(3)
     stores += [io(3, queries, query_ref), io(4, kv, kv_ref)]
     stores[1].start()
@@ -1322,20 +1321,27 @@
     for copy in stores[3:]:
         copy.start()
 
+    def part_copy(i):
+        at = pl.ds(pl.multiple_of(i * TILE, TILE), TILE)
+        return pltpu.make_async_copy(tokens.at[:, at], part_ref.at[:, at], part_sem.at[i])
+
     @pl.loop(0, depth // TILE)
     def _(i):
         at = pl.ds(pl.multiple_of(i * TILE, TILE), TILE)
         tokens[:, at] = lax.dot_general(
             context[...], full[at, side : side + query_width], (((1,), (1,)), ((), ())),
             preferred_element_type=jnp.float32).astype(jnp.bfloat16)
-
-    stores.append(io(9, tokens, part_ref))
-    stores[-1].start()
+        part_copy(i).start()
+
     for m in range(2):
         swap(m).wait_send()
     all_sent()
     for copy in stores:
         copy.wait()
+
+    @pl.loop(0, depth // TILE)
+    def _(i):
+        part_copy(i).wait()
 
 
 def head_block(tokens, own, angles, prompt_of, heads, cont, cid):
@@ -1369,14 +1375,14 @@
             pltpu.VMEM((rows, depth), bf16),
             pltpu.VMEM((rows, depth), bf16),
             pltpu.VMEM(full, bf16),
-            pltpu.VMEM((rows, HEAD), f32),
+            pltpu.VMEM((half_rows, HEAD), f32),
             pltpu.VMEM((rows, width), bf16),
             pltpu.VMEM((2, half_rows, 2 * HEAD), bf16),
             pltpu.VMEM((2, prompt, 2 * HEAD), bf16),
             pltpu.VMEM((rows, width), f32),
             pltpu.VMEM((heads, rows, 128), f32),
             pltpu.VMEM((rows, width), bf16),
-            dma((4, 9)), dma((4, 9)), dma((4,)), dma((10,)), dma((2,)), dma((2,)),
+            dma((4, 9)), dma((4, 9)), dma((4,)), dma((9,)), dma((depth // TILE,)), dma((2,)), dma((2,)),
         ],
         compiler_params=pltpu.CompilerParams(
             collective_id=cid, has_side_effects=True, vmem_limit_bytes=56 * 2**20),
@@ -1389,7 +1395,7 @@
     d_qkv_ref, part_ref, gain_ref,
     d_attn, full, tokens, queries, kv, other, context, sums, cosine_sine,
     d_context, d_query, d_kv, d_other, sent_kv, got_kv, d_qkv, inverses, d_picked,
-    io_sem, swap_in, swap_out,
+    io_sem, part_sem, swap_in, swap_out,
 ):
     rows_all, depth = tokens.shape
     rows = rows_all // 2
@@ -1411,8 +1417,10 @@
             sent_kv.at[m], got_kv.at[m], swap_out.at[m], swap_in.at[m], device_id=over_y, device_id_type=MESH)
 
     pairs = (
-        (d_attn_ref, d_attn), (full_ref, full), (query_ref, queries), (kv_ref, kv), (other_ref, other),
+        (d_attn_ref, d_attn), (full_ref.at[:, pl.ds(side, query_width)], full.at[:, pl.ds(side, query_width)]),
+        (query_ref, queries), (kv_ref, kv), (other_ref, other),
         (context_ref, context), (sum_ref, sums), (angle_ref, cosine_sine), (token_ref, tokens),
+        (full_ref.at[:, pl.ds(0, side)], full.at[:, pl.ds(0, side)]),
     )
     loads = [io(k, *pair) for k, pair in enumerate(pairs)]
     for copy in loads:
@@ -1505,15 +1513,14 @@
 
     half = HEAD // 2
 
-    def turn_back_rows(values, span):
-        cosine, sine = cosine_sine[span, :half], cosine_sine[span, half:]
-        return turn(values, cosine, -sine).astype(jnp.bfloat16)
+    def turn_back_rows(values):
+        return turn(values, cosine_sine[:, :half], -cosine_sine[:, half:]).astype(jnp.bfloat16)
 
     for m in range(2):
         span = pl.ds(m * rows, rows)
         for h in range(heads):
             across = slice(h * HEAD, (h + 1) * HEAD)
-            d_qkv[span, across] = turn_back_rows(d_query[span, across], span)
+            d_qkv[span, across] = turn_back_rows(d_query[span, across])
 
     @pl.loop(0, rows_all // BLOCK)
     def _(b):
@@ -1526,10 +1533,14 @@
         swap(m).wait_recv()
         span = pl.ds(m * rows, rows)
         d_kv[m, :prompt, :] += got_kv[m].astype(jnp.float32)
-        d_qkv[span, query_width : query_width + HEAD] = turn_back_rows(d_kv[m, :, :HEAD], span)
+        d_qkv[span, query_width : query_width + HEAD] = turn_back_rows(d_kv[m, :, :HEAD])
         d_qkv[span, query_width + HEAD :] = d_kv[m, :, HEAD:].astype(jnp.bfloat16)
-    stores = [io(9, d_qkv, d_qkv_ref)]
+    stores = [io(10, d_qkv, d_qkv_ref)]
     stores[0].start()
+
+    def part_copy(i):
+        at = pl.ds(pl.multiple_of(i * TILE, TILE), TILE)
+        return pltpu.make_async_copy(d_attn.at[:, at], part_ref.at[:, at], part_sem.at[i])
 
     @pl.loop(0, depth // TILE)
     def _(i):
@@ -1538,13 +1549,16 @@
         normed = tokens[:, at].astype(jnp.float32) * inverses[:, :1]
         gain_ref[0:1, at] = jnp.sum(part * normed, axis=0, keepdims=True)
         d_attn[:, at] = part.astype(jnp.bfloat16)
-
-    stores.append(io(10, d_attn, part_ref))
-    stores[1].start()
+        part_copy(i).start()
+
     for m in range(2):
         swap(m).wait_send()
     for copy in stores:
         copy.wait()
+
+    @pl.loop(0, depth // TILE)
+    def _(i):
+        part_copy(i).wait()
 
 
 def back_block(prompt_of, d_attn, full, queries, kv, other, context, sums, angles, tokens, cont, cid):
@@ -1581,7 +1595,7 @@
             pltpu.VMEM((rows, qkv_width), bf16),
             pltpu.VMEM((rows, 128), f32),
             pltpu.VMEM((2 * heads * cont, HEAD), f32),
-            dma((11,)), dma((2,)), dma((2,)),
+            dma((11,)), dma((depth // TILE,)), dma((2,)), dma((2,)),
         ],
         compiler_params=pltpu.CompilerParams(
             collective_id=cid, has_side_effects=True, vmem_limit_bytes=56 * 2**20),
@@ -1590,7 +1604,8 @@
     )(prompt_of, d_attn, full, queries, kv, other, context, sums, angles, tokens)
 
 
-FINAL_ROWS = 64
+FINAL_ROWS = 128
+SHARE_ROWS = 32
 
 
 def final_kernel(
@@ -1615,15 +1630,16 @@
 def final_block(sums, tokens, middle, layer, gains, gate, up, down, side, query_width):
     rows, depth = tokens.shape
     share, units = gate.shape
-    steps = share // BLOCK
+    steps = share // SHARE_ROWS
     blocks = -(-rows // FINAL_ROWS)
+    assert blocks <= steps
     f32 = jnp.float32
 
     def wide(width):
         return pl.BlockSpec((FINAL_ROWS, width), lambda i: (jnp.minimum(i, blocks - 1), 0))
 
     def thin(width):
-        return pl.BlockSpec((BLOCK, width), lambda i: (i, 0))
+        return pl.BlockSpec((SHARE_ROWS, width), lambda i: (i, 0))
 
     widths = (units, units, units, query_width, HEAD, HEAD, query_width)
     return pl.pallas_call(
@@ -1911,7 +1927,7 @@
     heads = query_width // HEAD
     bf16 = jnp.bfloat16
     owners = prompt_of[:, 0]
-    angles = turn_angles(row_count, seq_pos, micro_count)
+    angles = turn_angles(row_count, seq_pos)
     flat = tokens.reshape(total_rows, model_width)
     own_side = jnp.concatenate(
         [
@@ -1990,7 +2006,7 @@
     )
 
 
-def turn_angles(row_count, seq_pos, micro_count):
+def turn_angles(row_count, seq_pos):
     half_width = HEAD // 2
     rows = jnp.arange(row_count)
     prompt_dev = row_count - CONT
@@ -2000,8 +2016,7 @@
     )
     spectrum = THETA ** (-2.0 * jnp.arange(half_width, dtype=jnp.float32) / HEAD)
     angles = places.astype(jnp.float32)[:, None] * spectrum
-    both = jnp.concatenate([jnp.cos(angles), jnp.sin(angles)], axis=1)
-    return jnp.tile(both, (micro_count, 1))
+    return jnp.concatenate([jnp.cos(angles), jnp.sin(angles)], axis=1)
 
 
 def per_device(*arrays):

time: 770 us -> 768 us (level)
    pallas_call x1, Pallas kernels: 163 us -> 152 us  [tail_block(): pl.pallas_call(functools.partial(tail_kernel, size, width, bases), out_sh...]
    pallas_call x1, Pallas kernels: 56.6 us -> 66.6 us  [back_block(): pl.pallas_call(functools.partial(back_kernel, heads, cont), out_shape=(sh...]
where the time goes in v8:
time: 768 us; the launch traced here: 759 us
  Pallas kernels  733 us (95%)
  between operations  14.6 us (2%)
  local copies, waits for them, and re-layouts  9.4 us (1%)
    pallas_call x1, Pallas kernels, ffn_block(): pl.pallas_call(functools.partial(ffn_kernel, size, width, bases, schedule...  423 us
    pallas_call x1, Pallas kernels, tail_block(): pl.pallas_call(functools.partial(tail_kernel, size, width, bases), out_sh...  152 us
    pallas_call x1, Pallas kernels, head_block(): pl.pallas_call(functools.partial(head_kernel, heads, cont), out_shape=(sh...  70.4 us
    pallas_call x1, Pallas kernels, back_block(): pl.pallas_call(functools.partial(back_kernel, heads, cont), out_shape=(sh...  66.6 us
    pallas_call x1, Pallas kernels, final_block(): pl.pallas_call(final_kernel, grid=(steps,), out_shape=(jax.ShapeDtypeStru...  21.1 us
  transfers between devices with their start and end apart: 1, of which 0 were waited for; matrix products, arithmetic and copies ran while one was open for 1% of the time, Pallas kernels for 29%

profile of v8, /device:TPU:0, one launch (start us, length us, event | category | flops | bytes accessed | tf_op | source)
XLA Modules:
  0.0 759.4 jit_solution(871266653575392061)
XLA Ops:
  7.2 0.0 reduce-scatter.2.cloned.1.call-start
  7.3 0.8 copy.26
  8.1 1.0 constant_dynamic-update-slice_fusion.2
  9.1 1.0 multiply_cosine_fusion
  10.1 0.8 pad_maximum_fusion.angle_ref
  11.0 0.9 constant_dynamic-update-slice_fusion.1
  11.9 0.9 constant_dynamic-update-slice_fusion
  12.8 1.0 bitcast_dynamic-update-slice_fusion.own_ref
  13.8 0.0 copy-start.1
  13.8 0.9 copy-done.1
  14.8 70.4 %shard_map.186 = (bf16[1088,2304]{1,0:T(8,128)(2,1)}, bf16[1088,512]{1,0:T(8,128)(2,1)}, bf16[1088,512]{1,0:T(8,128)(2,1)}, bf16[2,544,512]{2,1,0:T(8,128)(2,1)}...) custom-call(s32[2]{0:T(128)} %bitcast.45, ...), custom_call_target="tpu_custom_call" | custom-call | flops 10909384704 | bytes 209715200 | tf_op jit(solution)/shard_map/pallas_call | solution.py:1359
  85.2 423.3 %shard_map.187 = (bf16[6,544,2304]{2,1,0:T(8,128)(2,1)}, bf16[2,544,2304]{2,1,0:T(8,128)(2,1)}, bf16[2,544,2304]{2,1,0:T(8,128)(2,1)}, bf16[2,544,2304]{2,1,0:T(...) custom-call(bf16[2,544,2304]{2,1,0:T(8,128)(2,1)} %bitcast.47, ...), custom_call_target="tpu_custom_call" | custom-call | flops 103960018944 | bytes 1073741824 | tf_op jit(solution)/shard_map/pallas_call | solution.py:806
  508.4 0.0 reduce-scatter.2.cloned.1.call-update
  508.5 0.0 copy-start
  508.5 66.6 %shard_map.188 = (bf16[1088,1024]{1,0:T(8,128)(2,1)}, bf16[1088,2304]{1,0:T(8,128)(2,1)}, f32[8,2304]{1,0:T(8,128)}) custom-call(s32[2]{0:T(128)} %bitcast.46, bf16[1088,2304]{1,0:T(8,128)(2,1)} %bitcast.33, bf16[2304,1664]{1,0:T(8,128)(2,1)} %get-tuple-element.48.full_ref, bf16[1088,512]{1,0:T(8,128)(2,1)} %get-tuple-element.49.query_ref, ...), custom_call_target="tpu_custom_call" | custom-call | flops 7700742144 | bytes 157286400 | tf_op jit(solution)/shard_map/pallas_call | solution.py:1574
  575.1 0.9 slice.12
  576.0 0.0 copy-done
  576.0 0.1 bitcast_reduce_fusion
  576.1 0.3 copy.27
  576.5 0.9 pad.10.gain_ref
  577.4 152.0 %shard_map.189 = (bf16[2,544,2304]{2,1,0:T(8,128)(2,1)}, bf16[288,2304]{1,0:T(8,128)(2,1)}, bf16[288,2304]{1,0:T(8,128)(2,1)}, bf16[288,1664]{1,0:T(8,128)(2,1)}, f32[288,128]{1,0:T(8,128)}) custom-call(bf16[2,544,2304]{2,1,0:T(8,128)(2,1)} %bitcast.35, bf16[2304,2304]{1,0:T(8,128)(2,1)} %get-tuple-element.55.gate_grad_ref, ...), custom_call_target="tpu_custom_call" | custom-call | flops 8342470656 | bytes 419430400 | tf_op jit(solution)/shard_map/pallas_call | solution.py:1093
  729.4 0.9 slice_bitcast_fusion
  730.3 0.7 copy.30
  731.0 0.0 reduce-scatter.2.cloned.1.call-done.down_ref
  731.0 21.1 %shard_map.190 = (bf16[1088,2304]{1,0:T(8,128)(2,1)}, f32[1088,2304]{1,0:T(8,128)}, f32[288,2304]{1,0:T(8,128)}, f32[288,2304]{1,0:T(8,128)}, f32[288,2304]{1,0:...) custom-call(bf16[1088,2304]{1,0:T(8,128)(2,1)} %bitcast.36, ...), custom_call_target="tpu_custom_call" | custom-call | tf_op jit(solution)/shard_map/pallas_call | solution.py:1645
  (5 shorter events, 0.1 us)
Async XLA Ops:
  7.2 723.9 %reduce-scatter.2.cloned.1.call-start = ((), (), s32[]{:S(2)}) async-start(), calls=%async_computation.1 | async-start | bytes 11943936 | tf_op jit(solution)/shard_map/reduce_scatter | solution.py:1960
  13.8 0.9 copy-start.1
  508.5 67.5 %copy-start = (f32[24,2304]{1,0:T(8,128)S(1)}, f32[24,2304]{1,0:T(8,128)}, u32[]{:S(2)}) copy-start(f32[24,2304]{1,0:T(8,128)} %get-tuple-element.60) | copy-start | bytes 663556
Sparse Core Ops, SparseCore 0:
  508.6 92.8 reduce-scatter.1
